TPU v7x, 128 devices: a whole 4x4x4 slice. The times are simulated.
128 devices in a mesh: gs: 16 (over z, y), img: 8 (over x, core).
Axes of the slice: x: 4, y: 4, z: 4, core: 2. Of those that a mesh axis runs over, the one named last changes fastest.
Arguments:
- gaussians: float32 [59, 655360], P(None, ('gs', 'img')), may hold values from -6 to 4096, as said below
- send_slots: int32 [128, 10240], P(('gs', 'img')), may hold values from 0 to 5119, as said below
- tile_lists: int32 [64, 256, 512], P('img', 'gs'), may hold values from -1 to 10239, as said below
- truth: float32 [3, 1024, 4096], P(None, 'img', 'gs'), may hold values from 0 to 1
Outputs:
- rendered: float32 [3, 1024, 4096], P(None, 'img', 'gs')
- pixel_loss: float32 [1024, 4096], P('img', 'gs')
Inputs may be any that keep to these rules, and one draw needn't show every extreme that they name: `gaussians`: rows 0 and 1 are pixel positions, row 2 a depth of 10 to 60, rows 3 to 5 log scales, rows 6 to 9 a quaternion whose first component is at least 0.5, row 10 an opacity logit, rows 11 to 58 colour harmonics, 16 for each channel. `send_slots`: row s lists, for each destination device in order, 80 indices of source s's own Gaussians. `tile_lists`: live entries (0 or more) name distinct slots of the owning device's received Gaussians and come first, ordered by increasing depth (row 2) of the Gaussians they name; the rest are -1.
All inputs are finite; a program needn't handle non-finite values.
Results may differ from a plain program's by a relative error of at most 0.0003.
Values sent between devices are 32-bit elements; how exact they have to be, the bound alone decides.
A program may use at most 64 MiB of HBM per device.

v0:
```python
import jax
import jax.numpy as jnp
from jax import lax
from jax.sharding import PartitionSpec as P

TILE = 16


coef_zero = 0.28209479177387814
coef_one = 0.4886025119029199
coef_two = [
    1.0925484305920792,
    -1.0925484305920792,
    0.31539156525252005,
    -1.0925484305920792,
    0.5462742152960396,
]
coef_three = [
    -0.5900435899266435,
    2.890611442640554,
    -0.4570457994644658,
    0.3731763325901154,
    -0.4570457994644658,
    1.445305721320277,
    -0.5900435899266435,
]
camera_z = -3000.0
ssim_share = 0.2
stable_one = 0.0001
stable_two = 0.0009


def extended(value, sides, width):
    for axis, dim in sides:
        size, length = (lax.axis_size(axis), value.shape[dim])
        up = [(i, (i + 1) % size) for i in range(size - 1)]
        down = [(j, i) for i, j in up]
        last = lax.slice_in_dim(value, length - width, length, axis=dim)
        first = lax.slice_in_dim(value, 0, width, axis=dim)
        before = lax.ppermute(last, axis, up)
        after = lax.ppermute(first, axis, down)
        value = jnp.concatenate([before, value, after], axis=dim)
    return value


def project(gauss):
    mean_x, mean_y, mean_z = (gauss[0], gauss[1], gauss[2])
    squared = jnp.exp(2.0 * gauss[3:6])
    rotation = gauss[6:10] / jnp.sqrt(jnp.sum(gauss[6:10] * gauss[6:10], axis=0))
    quat_w, quat_x, quat_y, quat_z = (rotation[0], rotation[1], rotation[2], rotation[3])
    first_a = 1.0 - 2.0 * (quat_y * quat_y + quat_z * quat_z)
    first_b = 2.0 * (quat_x * quat_y - quat_w * quat_z)
    first_c = 2.0 * (quat_x * quat_z + quat_w * quat_y)
    second_a = 2.0 * (quat_x * quat_y + quat_w * quat_z)
    second_b = 1.0 - 2.0 * (quat_x * quat_x + quat_z * quat_z)
    second_c = 2.0 * (quat_y * quat_z - quat_w * quat_x)
    cov_xx = (
        first_a * first_a * squared[0]
        + first_b * first_b * squared[1]
        + first_c * first_c * squared[2]
        + 0.3
    )
    cov_xy = (
        first_a * second_a * squared[0]
        + first_b * second_b * squared[1]
        + first_c * second_c * squared[2]
    )
    cov_yy = (
        second_a * second_a * squared[0]
        + second_b * second_b * squared[1]
        + second_c * second_c * squared[2]
        + 0.3
    )
    determinant = cov_xx * cov_yy - cov_xy * cov_xy
    opacity = jax.nn.sigmoid(gauss[10])
    delta_z = mean_z - camera_z
    length = jnp.sqrt(mean_x * mean_x + mean_y * mean_y + delta_z * delta_z)
    dir_x, dir_y, dir_z = (mean_x / length, mean_y / length, delta_z / length)
    sq_x, sq_y, sq_z = (dir_x * dir_x, dir_y * dir_y, dir_z * dir_z)
    prod_xy, prod_yz, prod_xz = (dir_x * dir_y, dir_y * dir_z, dir_x * dir_z)
    harmonic_basis = jnp.stack(
        [
            coef_zero * jnp.ones_like(dir_x),
            -coef_one * dir_y,
            coef_one * dir_z,
            -coef_one * dir_x,
            coef_two[0] * prod_xy,
            coef_two[1] * prod_yz,
            coef_two[2] * (2.0 * sq_z - sq_x - sq_y),
            coef_two[3] * prod_xz,
            coef_two[4] * (sq_x - sq_y),
            coef_three[0] * dir_y * (3.0 * sq_x - sq_y),
            coef_three[1] * prod_xy * dir_z,
            coef_three[2] * dir_y * (4.0 * sq_z - sq_x - sq_y),
            coef_three[3] * dir_z * (2.0 * sq_z - 3.0 * sq_x - 3.0 * sq_y),
            coef_three[4] * dir_x * (4.0 * sq_z - sq_x - sq_y),
            coef_three[5] * dir_z * (sq_x - sq_y),
            coef_three[6] * dir_x * (sq_x - 3.0 * sq_y),
        ]
    )
    harmonics = gauss[11:59].reshape(3, 16, gauss.shape[1])
    colour = jnp.maximum(jnp.sum(harmonics * harmonic_basis[None], axis=1) + 0.5, 0.0)
    return jnp.stack(
        [
            mean_x,
            mean_y,
            cov_yy / determinant,
            -cov_xy / determinant,
            cov_xx / determinant,
            opacity,
            colour[0],
            colour[1],
            colour[2],
        ]
    )


def splat_alpha(params, live_mask, pix_x, pix_y):
    delta_x = pix_x[:, :, None] - params[0][:, None, :]
    delta_y = pix_y[:, :, None] - params[1][:, None, :]
    power = -0.5 * (
        params[2][:, None, :] * delta_x * delta_x + params[4][:, None, :] * delta_y * delta_y
    )
    power = power - params[3][:, None, :] * delta_x * delta_y
    return jnp.where(live_mask[:, None, :], params[5][:, None, :] * jnp.exp(power), 0.0)


def window():
    offsets = jnp.arange(11, dtype=jnp.float32) - 5.0
    weights = jnp.exp(-offsets * offsets / 4.5)
    return weights / jnp.sum(weights)


def band_matrix(outputs, inputs_len, sign):
    difference = sign * (
        jnp.arange(inputs_len, dtype=jnp.int32)[None, :]
        - jnp.arange(outputs, dtype=jnp.int32)[:, None]
    )
    offsets = jnp.arange(11, dtype=jnp.int32)
    return jnp.sum(
        jnp.where(difference[:, :, None] == offsets[None, None, :], window()[None, None, :], 0.0),
        axis=2,
    )


def loss_from(filtered, rendered, truth):
    mean_r, mean_t = (filtered[0:3], filtered[3:6])
    variance_r = filtered[6:9] - mean_r * mean_r
    variance_t = filtered[9:12] - mean_t * mean_t
    covariance = filtered[12:15] - mean_r * mean_t
    similarity = (
        (2.0 * mean_r * mean_t + stable_one)
        * (2.0 * covariance + stable_two)
        / (
            (mean_r * mean_r + mean_t * mean_t + stable_one)
            * (variance_r + variance_t + stable_two)
        )
    )
    return (1.0 - ssim_share) * jnp.mean(jnp.abs(rendered - truth), axis=0) + ssim_share * (
        1.0 - jnp.mean(similarity, axis=0)
    )


def on_device(gaussians, send_slots, tile_lists, truth):
    local_index = send_slots[0]
    outgoing = gaussians[:, local_index]
    arrived = lax.all_to_all(outgoing, ("gs", "img"), split_axis=1, concat_axis=1, tiled=True)
    splats = project(arrived)
    rows_here, cols_here, list_len = tile_lists.shape
    tile_count = rows_here * cols_here
    group_size = 32
    groups = tile_count // group_size
    flat_lists = tile_lists.reshape(tile_count, list_len)
    tile_number = jnp.arange(tile_count, dtype=jnp.int32)
    tile_row = lax.axis_index("img") * rows_here + tile_number // cols_here
    tile_col = lax.axis_index("gs") * cols_here + tile_number % cols_here
    pixels = jnp.arange(TILE * TILE, dtype=jnp.int32)
    pix_x = (tile_col[:, None] * TILE + pixels[None, :] % TILE).astype(jnp.float32) + 0.5
    pix_y = (tile_row[:, None] * TILE + pixels[None, :] // TILE).astype(jnp.float32) + 0.5
    live_blocks = (jnp.sum((flat_lists >= 0).astype(jnp.int32), axis=1) + 127) // 128
    group_blocks = jnp.max(live_blocks.reshape(groups, group_size), axis=1)
    strict = (jnp.arange(128)[:, None] < jnp.arange(128)[None, :]).astype(jnp.float32)

    def render_group(inputs):
        group_lists, group_x, group_y, block_limit = inputs

        def blend_block(block_index, state_pair):
            log_left, colour = state_pair
            block_lists = lax.dynamic_slice_in_dim(group_lists, block_index * 128, 128, 1)
            block_live = block_lists >= 0
            block_params = splats[:, jnp.maximum(block_lists, 0)]
            alphas = splat_alpha(block_params, block_live, group_x, group_y)
            log_keep = jnp.log1p(-alphas)
            before = jnp.einsum("tpk,kj->tpj", log_keep, strict, precision=lax.Precision.HIGHEST)
            weight = jnp.exp(log_left[:, :, None] + before) * alphas
            colour = colour + jnp.einsum(
                "tpk,ctk->ctp", weight, block_params[6:9], precision=lax.Precision.HIGHEST
            )
            return (log_left + jnp.sum(log_keep, axis=2), colour)

        block_count = list_len // 128
        initial = (
            jnp.zeros((group_size, TILE * TILE), jnp.float32),
            jnp.zeros((3, group_size, TILE * TILE), jnp.float32),
        )
        return lax.fori_loop(0, block_count, blend_block, initial)[1]

    colours = lax.map(
        render_group,
        (
            flat_lists.reshape(groups, group_size, list_len),
            pix_x.reshape(groups, group_size, TILE * TILE),
            pix_y.reshape(groups, group_size, TILE * TILE),
            group_blocks,
        ),
    )
    rendered = (
        colours.transpose(1, 0, 2, 3)
        .reshape(3, rows_here, cols_here, TILE, TILE)
        .transpose(0, 1, 3, 2, 4)
    )
    rendered = rendered.reshape(3, rows_here * TILE, cols_here * TILE)
    stacked = jnp.concatenate([rendered, truth])
    padded = extended(stacked, (("gs", 2), ("img", 1)), 5)
    rim_r, rim_t = (padded[0:3], padded[3:6])
    quantities = jnp.concatenate([rim_r, rim_t, rim_r * rim_r, rim_t * rim_t, rim_r * rim_t])
    img_height, img_width = (rendered.shape[1], rendered.shape[2])
    band_rows = band_matrix(img_height, img_height + 10, 1)
    band_cols = band_matrix(img_width, img_width + 10, 1).T
    filtered = jnp.einsum("ij,cjw->ciw", band_rows, quantities, precision=lax.Precision.HIGHEST)
    filtered = jnp.einsum("ciw,wv->civ", filtered, band_cols, precision=lax.Precision.HIGHEST)
    return (rendered, loss_from(filtered, rendered, truth))


def solution(mesh):
    return jax.shard_map(
        on_device,
        mesh=mesh,
        in_specs=(
            P(None, ("gs", "img")),
            P(("gs", "img"), None),
            P("img", "gs", None),
            P(None, "img", "gs"),
        ),
        out_specs=(P(None, "img", "gs"), P("img", "gs")),
        check_vma=False,
    )
```

profile of v0, /device:TPU:0, one launch (start us, length us, event | category | flops | bytes accessed | tf_op | source)
XLA Modules:
  0.0 747.1 jit_solution(5034656531834304779)
XLA Ops:
  3.4 34.3 %gather_fusion.1 = f32[10240,59]{1,0:T(8,128)} fusion(f32[59,5120]{0,1:T(8,128)S(1)} %copy.69, s32[10240]{0:T(1024)S(1)} %broadcast_clamp_fusion), kind=kCustom, calls=%fused_computation.1 | custom fusion | bytes 4874240 | tf_op jit(solution)/shard_map/gather | solution.py:166
  43.6 11.7 %all-to-all-start = ((f32[59,128,80]{2,0,1:T(8,128)}), f32[59,128,80]{2,0,1:T(8,128)}, u32[]{:S(2)}, u32[]{:S(2)}) async-start(f32[59,128,80]{2,0,1:T(8,128)} %copy.70), calls=%async_computation | async-start | bytes 8388608 | tf_op jit(solution)/shard_map/all_to_all | solution.py:167
  57.8 49.8 %all-to-all-done = f32[59,128,80]{2,0,1:T(8,128)} async-done(((f32[59,128,80]{2,0,1:T(8,128)}), f32[59,128,80]{2,0,1:T(8,128)}, u32[]{:S(2)}, u32[]{:S(2)}) %all-to-all-start) | async-done | bytes 2416672 | tf_op jit(solution)/shard_map/all_to_all | solution.py:167
  144.9 559.9 %while.29 = (s32[]{:T(128)}, f32[4,3,32,256]{3,1,2,0:T(4,128)}, s32[4,32,512]{2,1,0:T(8,128)}, f32[4,32,256]{2,1,0:T(8,128)S(1)}, f32[4,32,256]{2,1,0:T(8,128)S(...) while((s32[]{:T(128)}, f32[4,3,32,256]{3,1,2,0:T(4,128)}, ...), condition=%wide.region_6.7_spmd.clone, body=%wide.region_2.6_spmd.clone.sunk | while | flops 1694601216 | bytes 10863023 | solution.py:208
  145.7 138.4 %while.30 = (s32[]{:T(128)}, f32[32,256]{1,0:T(8,128)S(1)}, f32[3,32,256]{2,0,1:T(4,128)S(1)}, s32[32,512]{1,0:T(8,128)S(1)}, f32[9,10240]{0,1:T(8,128)}, /*inde...) while((s32[]{:T(128)}, f32[32,256]{1,0:T(8,128)S(1)}, ...), condition=%wide.region_5.5_spmd.clone, body=%wide.region_3.4_spmd.clone.sunk | while | flops 1694568448 | bytes 10305726 | solution.py:206
  145.8 13.2 %gather_fusion = f32[4096,9]{1,0:T(8,128)S(1)} fusion(f32[9,10240]{0,1:T(8,128)} %get-tuple-element.492, s32[4096]{0:T(1024)S(1)} %bitcast_clamp_fusion.2), kind=kCustom, calls=%fused_computation.clone.clone.1 | custom fusion | bytes 311296 | tf_op jit(solution)/shard_map/while/body/eval_jaxpr/while/body/eval_jaxpr/gather | solution.py:191
  180.4 13.2 %gather_fusion = f32[4096,9]{1,0:T(8,128)S(1)} fusion(f32[9,10240]{0,1:T(8,128)} %get-tuple-element.492, s32[4096]{0:T(1024)S(1)} %bitcast_clamp_fusion.2), kind=kCustom, calls=%fused_computation.clone.clone.1 | custom fusion | bytes 311296 | tf_op jit(solution)/shard_map/while/body/eval_jaxpr/while/body/eval_jaxpr/gather | solution.py:191
  199.2 8.0 %fusion.95 = f32[32,256,128]{2,1,0:T(8,128)S(1)} fusion(f32[32,128]{1,0:T(8,128)S(1)} %bitcast.84, f32[32,128]{1,0:T(8,128)S(1)} %bitcast.87, f32[32,256]{1,0:T(8,128)S(1)} %get-tuple-element.494, f32[32,128]{1,0:T(8,128)S(1)} %bitcast.90, f32[32,128]{1,0:T(8,128)S(1)} %bitcast.93, f32[32,256]{1,0:T(8,128)S(1)} %get-tuple-element.493, ...), kind=kOutput, calls=%fused_computation.20.clone.1 | convolution fusion | flops 1625292800 | bytes 4427776 | tf_op jit(solution)/shard_map/while/body/eval_jaxpr/while/body/eval_jaxpr/tpk,kj->tpj/dot_general | solution.py:194
  215.0 13.2 %gather_fusion = f32[4096,9]{1,0:T(8,128)S(1)} fusion(f32[9,10240]{0,1:T(8,128)} %get-tuple-element.492, s32[4096]{0:T(1024)S(1)} %bitcast_clamp_fusion.2), kind=kCustom, calls=%fused_computation.clone.clone.1 | custom fusion | bytes 311296 | tf_op jit(solution)/shard_map/while/body/eval_jaxpr/while/body/eval_jaxpr/gather | solution.py:191
  233.9 8.0 %fusion.95 = f32[32,256,128]{2,1,0:T(8,128)S(1)} fusion(f32[32,128]{1,0:T(8,128)S(1)} %bitcast.84, f32[32,128]{1,0:T(8,128)S(1)} %bitcast.87, f32[32,256]{1,0:T(8,128)S(1)} %get-tuple-element.494, f32[32,128]{1,0:T(8,128)S(1)} %bitcast.90, f32[32,128]{1,0:T(8,128)S(1)} %bitcast.93, f32[32,256]{1,0:T(8,128)S(1)} %get-tuple-element.493, ...), kind=kOutput, calls=%fused_computation.20.clone.1 | convolution fusion | flops 1625292800 | bytes 4427776 | tf_op jit(solution)/shard_map/while/body/eval_jaxpr/while/body/eval_jaxpr/tpk,kj->tpj/dot_general | solution.py:194
  249.6 13.2 %gather_fusion = f32[4096,9]{1,0:T(8,128)S(1)} fusion(f32[9,10240]{0,1:T(8,128)} %get-tuple-element.492, s32[4096]{0:T(1024)S(1)} %bitcast_clamp_fusion.2), kind=kCustom, calls=%fused_computation.clone.clone.1 | custom fusion | bytes 311296 | tf_op jit(solution)/shard_map/while/body/eval_jaxpr/while/body/eval_jaxpr/gather | solution.py:191
  268.5 8.0 %fusion.95 = f32[32,256,128]{2,1,0:T(8,128)S(1)} fusion(f32[32,128]{1,0:T(8,128)S(1)} %bitcast.84, f32[32,128]{1,0:T(8,128)S(1)} %bitcast.87, f32[32,256]{1,0:T(8,128)S(1)} %get-tuple-element.494, f32[32,128]{1,0:T(8,128)S(1)} %bitcast.90, f32[32,128]{1,0:T(8,128)S(1)} %bitcast.93, f32[32,256]{1,0:T(8,128)S(1)} %get-tuple-element.493, ...), kind=kOutput, calls=%fused_computation.20.clone.1 | convolution fusion | flops 1625292800 | bytes 4427776 | tf_op jit(solution)/shard_map/while/body/eval_jaxpr/while/body/eval_jaxpr/tpk,kj->tpj/dot_general | solution.py:194
  285.7 138.4 %while.30 = (s32[]{:T(128)}, f32[32,256]{1,0:T(8,128)S(1)}, f32[3,32,256]{2,0,1:T(4,128)S(1)}, s32[32,512]{1,0:T(8,128)S(1)}, f32[9,10240]{0,1:T(8,128)}, /*inde...) while((s32[]{:T(128)}, f32[32,256]{1,0:T(8,128)S(1)}, ...), condition=%wide.region_5.5_spmd.clone, body=%wide.region_3.4_spmd.clone.sunk | while | flops 1694568448 | bytes 10305726 | solution.py:206
  285.8 13.2 %gather_fusion = f32[4096,9]{1,0:T(8,128)S(1)} fusion(f32[9,10240]{0,1:T(8,128)} %get-tuple-element.492, s32[4096]{0:T(1024)S(1)} %bitcast_clamp_fusion.2), kind=kCustom, calls=%fused_computation.clone.clone.1 | custom fusion | bytes 311296 | tf_op jit(solution)/shard_map/while/body/eval_jaxpr/while/body/eval_jaxpr/gather | solution.py:191
  304.6 8.0 %fusion.95 = f32[32,256,128]{2,1,0:T(8,128)S(1)} fusion(f32[32,128]{1,0:T(8,128)S(1)} %bitcast.84, f32[32,128]{1,0:T(8,128)S(1)} %bitcast.87, f32[32,256]{1,0:T(8,128)S(1)} %get-tuple-element.494, f32[32,128]{1,0:T(8,128)S(1)} %bitcast.90, f32[32,128]{1,0:T(8,128)S(1)} %bitcast.93, f32[32,256]{1,0:T(8,128)S(1)} %get-tuple-element.493, ...), kind=kOutput, calls=%fused_computation.20.clone.1 | convolution fusion | flops 1625292800 | bytes 4427776 | tf_op jit(solution)/shard_map/while/body/eval_jaxpr/while/body/eval_jaxpr/tpk,kj->tpj/dot_general | solution.py:194
  320.4 13.2 %gather_fusion = f32[4096,9]{1,0:T(8,128)S(1)} fusion(f32[9,10240]{0,1:T(8,128)} %get-tuple-element.492, s32[4096]{0:T(1024)S(1)} %bitcast_clamp_fusion.2), kind=kCustom, calls=%fused_computation.clone.clone.1 | custom fusion | bytes 311296 | tf_op jit(solution)/shard_map/while/body/eval_jaxpr/while/body/eval_jaxpr/gather | solution.py:191
  339.2 8.0 %fusion.95 = f32[32,256,128]{2,1,0:T(8,128)S(1)} fusion(f32[32,128]{1,0:T(8,128)S(1)} %bitcast.84, f32[32,128]{1,0:T(8,128)S(1)} %bitcast.87, f32[32,256]{1,0:T(8,128)S(1)} %get-tuple-element.494, f32[32,128]{1,0:T(8,128)S(1)} %bitcast.90, f32[32,128]{1,0:T(8,128)S(1)} %bitcast.93, f32[32,256]{1,0:T(8,128)S(1)} %get-tuple-element.493, ...), kind=kOutput, calls=%fused_computation.20.clone.1 | convolution fusion | flops 1625292800 | bytes 4427776 | tf_op jit(solution)/shard_map/while/body/eval_jaxpr/while/body/eval_jaxpr/tpk,kj->tpj/dot_general | solution.py:194
  355.0 13.2 %gather_fusion = f32[4096,9]{1,0:T(8,128)S(1)} fusion(f32[9,10240]{0,1:T(8,128)} %get-tuple-element.492, s32[4096]{0:T(1024)S(1)} %bitcast_clamp_fusion.2), kind=kCustom, calls=%fused_computation.clone.clone.1 | custom fusion | bytes 311296 | tf_op jit(solution)/shard_map/while/body/eval_jaxpr/while/body/eval_jaxpr/gather | solution.py:191
  389.6 13.2 %gather_fusion = f32[4096,9]{1,0:T(8,128)S(1)} fusion(f32[9,10240]{0,1:T(8,128)} %get-tuple-element.492, s32[4096]{0:T(1024)S(1)} %bitcast_clamp_fusion.2), kind=kCustom, calls=%fused_computation.clone.clone.1 | custom fusion | bytes 311296 | tf_op jit(solution)/shard_map/while/body/eval_jaxpr/while/body/eval_jaxpr/gather | solution.py:191
  425.7 138.4 %while.30 = (s32[]{:T(128)}, f32[32,256]{1,0:T(8,128)S(1)}, f32[3,32,256]{2,0,1:T(4,128)S(1)}, s32[32,512]{1,0:T(8,128)S(1)}, f32[9,10240]{0,1:T(8,128)}, /*inde...) while((s32[]{:T(128)}, f32[32,256]{1,0:T(8,128)S(1)}, ...), condition=%wide.region_5.5_spmd.clone, body=%wide.region_3.4_spmd.clone.sunk | while | flops 1694568448 | bytes 10305726 | solution.py:206
  425.7 13.2 %gather_fusion = f32[4096,9]{1,0:T(8,128)S(1)} fusion(f32[9,10240]{0,1:T(8,128)} %get-tuple-element.492, s32[4096]{0:T(1024)S(1)} %bitcast_clamp_fusion.2), kind=kCustom, calls=%fused_computation.clone.clone.1 | custom fusion | bytes 311296 | tf_op jit(solution)/shard_map/while/body/eval_jaxpr/while/body/eval_jaxpr/gather | solution.py:191
  444.6 8.0 %fusion.95 = f32[32,256,128]{2,1,0:T(8,128)S(1)} fusion(f32[32,128]{1,0:T(8,128)S(1)} %bitcast.84, f32[32,128]{1,0:T(8,128)S(1)} %bitcast.87, f32[32,256]{1,0:T(8,128)S(1)} %get-tuple-element.494, f32[32,128]{1,0:T(8,128)S(1)} %bitcast.90, f32[32,128]{1,0:T(8,128)S(1)} %bitcast.93, f32[32,256]{1,0:T(8,128)S(1)} %get-tuple-element.493, ...), kind=kOutput, calls=%fused_computation.20.clone.1 | convolution fusion | flops 1625292800 | bytes 4427776 | tf_op jit(solution)/shard_map/while/body/eval_jaxpr/while/body/eval_jaxpr/tpk,kj->tpj/dot_general | solution.py:194
  460.3 13.2 %gather_fusion = f32[4096,9]{1,0:T(8,128)S(1)} fusion(f32[9,10240]{0,1:T(8,128)} %get-tuple-element.492, s32[4096]{0:T(1024)S(1)} %bitcast_clamp_fusion.2), kind=kCustom, calls=%fused_computation.clone.clone.1 | custom fusion | bytes 311296 | tf_op jit(solution)/shard_map/while/body/eval_jaxpr/while/body/eval_jaxpr/gather | solution.py:191
  494.9 13.2 %gather_fusion = f32[4096,9]{1,0:T(8,128)S(1)} fusion(f32[9,10240]{0,1:T(8,128)} %get-tuple-element.492, s32[4096]{0:T(1024)S(1)} %bitcast_clamp_fusion.2), kind=kCustom, calls=%fused_computation.clone.clone.1 | custom fusion | bytes 311296 | tf_op jit(solution)/shard_map/while/body/eval_jaxpr/while/body/eval_jaxpr/gather | solution.py:191
  529.5 13.2 %gather_fusion = f32[4096,9]{1,0:T(8,128)S(1)} fusion(f32[9,10240]{0,1:T(8,128)} %get-tuple-element.492, s32[4096]{0:T(1024)S(1)} %bitcast_clamp_fusion.2), kind=kCustom, calls=%fused_computation.clone.clone.1 | custom fusion | bytes 311296 | tf_op jit(solution)/shard_map/while/body/eval_jaxpr/while/body/eval_jaxpr/gather | solution.py:191
  565.7 138.4 %while.30 = (s32[]{:T(128)}, f32[32,256]{1,0:T(8,128)S(1)}, f32[3,32,256]{2,0,1:T(4,128)S(1)}, s32[32,512]{1,0:T(8,128)S(1)}, f32[9,10240]{0,1:T(8,128)}, /*inde...) while((s32[]{:T(128)}, f32[32,256]{1,0:T(8,128)S(1)}, ...), condition=%wide.region_5.5_spmd.clone, body=%wide.region_3.4_spmd.clone.sunk | while | flops 1694568448 | bytes 10305726 | solution.py:206
  565.7 13.2 %gather_fusion = f32[4096,9]{1,0:T(8,128)S(1)} fusion(f32[9,10240]{0,1:T(8,128)} %get-tuple-element.492, s32[4096]{0:T(1024)S(1)} %bitcast_clamp_fusion.2), kind=kCustom, calls=%fused_computation.clone.clone.1 | custom fusion | bytes 311296 | tf_op jit(solution)/shard_map/while/body/eval_jaxpr/while/body/eval_jaxpr/gather | solution.py:191
  584.6 8.0 %fusion.95 = f32[32,256,128]{2,1,0:T(8,128)S(1)} fusion(f32[32,128]{1,0:T(8,128)S(1)} %bitcast.84, f32[32,128]{1,0:T(8,128)S(1)} %bitcast.87, f32[32,256]{1,0:T(8,128)S(1)} %get-tuple-element.494, f32[32,128]{1,0:T(8,128)S(1)} %bitcast.90, f32[32,128]{1,0:T(8,128)S(1)} %bitcast.93, f32[32,256]{1,0:T(8,128)S(1)} %get-tuple-element.493, ...), kind=kOutput, calls=%fused_computation.20.clone.1 | convolution fusion | flops 1625292800 | bytes 4427776 | tf_op jit(solution)/shard_map/while/body/eval_jaxpr/while/body/eval_jaxpr/tpk,kj->tpj/dot_general | solution.py:194
  600.3 13.2 %gather_fusion = f32[4096,9]{1,0:T(8,128)S(1)} fusion(f32[9,10240]{0,1:T(8,128)} %get-tuple-element.492, s32[4096]{0:T(1024)S(1)} %bitcast_clamp_fusion.2), kind=kCustom, calls=%fused_computation.clone.clone.1 | custom fusion | bytes 311296 | tf_op jit(solution)/shard_map/while/body/eval_jaxpr/while/body/eval_jaxpr/gather | solution.py:191
  634.9 13.2 %gather_fusion = f32[4096,9]{1,0:T(8,128)S(1)} fusion(f32[9,10240]{0,1:T(8,128)} %get-tuple-element.492, s32[4096]{0:T(1024)S(1)} %bitcast_clamp_fusion.2), kind=kCustom, calls=%fused_computation.clone.clone.1 | custom fusion | bytes 311296 | tf_op jit(solution)/shard_map/while/body/eval_jaxpr/while/body/eval_jaxpr/gather | solution.py:191
  669.5 13.2 %gather_fusion = f32[4096,9]{1,0:T(8,128)S(1)} fusion(f32[9,10240]{0,1:T(8,128)} %get-tuple-element.492, s32[4096]{0:T(1024)S(1)} %bitcast_clamp_fusion.2), kind=kCustom, calls=%fused_computation.clone.clone.1 | custom fusion | bytes 311296 | tf_op jit(solution)/shard_map/while/body/eval_jaxpr/while/body/eval_jaxpr/gather | solution.py:191
  732.6 8.6 %fusion.30 = f32[15,266,128]{2,1,0:T(8,128)S(1)} fusion(f32[3,138,266]{2,1,0:T(8,128)S(1)} %get-tuple-element.315, f32[3,138,266]{2,1,0:T(8,128)S(1)} %get-tuple-element.316, f32[3,138,266]{2,1,0:T(8,128)S(1)} %get-tuple-element.314, f32[6,5,266]{2,1,0:T(8,128)S(1)} %collective-permute-done.3, f32[6,128,5]{2,1,0:T(8,128)S(1)} %collective-permute-done.1, ...), kind=kOutput, calls=%fused_computation.40 | convolution fusion | flops 849606656 | bytes 4316016 | tf_op jit(solution)/shard_map/ij,cjw->ciw/dot_general | solution.py:230
  (232 shorter events, 372.2 us)
Async XLA Ops:
  43.6 64.1 %all-to-all-start = ((f32[59,128,80]{2,0,1:T(8,128)}), f32[59,128,80]{2,0,1:T(8,128)}, u32[]{:S(2)}, u32[]{:S(2)}) async-start(f32[59,128,80]{2,0,1:T(8,128)} %copy.70), calls=%async_computation | async-start | bytes 8388608 | tf_op jit(solution)/shard_map/all_to_all | solution.py:167
  56.5 1.2 copy-start.5
  126.5 8.2 %copy-start = (f32[3,16,10240]{2,1,0:T(8,128)S(1)}, f32[3,16,10240]{2,1,0:T(8,128)}, u32[]{:S(2)}) copy-start(f32[3,16,10240]{2,1,0:T(8,128)} %reshape.630) | copy-start | bytes 5898244
  126.5 8.7 %copy-start.3 = (f32[4,10240]{1,0:T(4,128)S(1)}, f32[4,10240]{1,0:T(4,128)}, u32[]{:S(2)}) copy-start(f32[4,10240]{1,0:T(4,128)} %slice.168) | copy-start | bytes 491524
  706.9 5.7 copy-start.4
  709.7 21.5 %copy-start.6 = (f32[11]{0:T(128)S(1)}, f32[11]{0:T(128)}, u32[]{:S(2)}) copy-start(f32[11]{0:T(128)} %copy-done.5) | copy-start | bytes 136
  712.5 19.9 %copy-start.1 = (f32[3,128,256]{2,1,0:T(8,128)}, f32[3,128,256]{2,1,0:T(8,128)S(1)}, u32[]{:S(2)}) copy-start(f32[3,128,256]{2,1,0:T(8,128)S(1)} %reshape.632) | copy-start | bytes 1179652
  712.8 12.5 %collective-permute-start.1 = (f32[6,128,5]{2,1,0:T(8,128)S(1)}, f32[6,128,5]{2,1,0:T(8,128)S(1)}, u32[]{:S(2)}, u32[]{:S(2)}) collective-permute-start(f32[6,128,5]{2,1,0:T(8,128)S(1)} %get-tuple-element.318), channel_id=1, source_target_pairs={{8,0},{16,8},{24,16},{32,24},{40,32},{48,40},{56,48},{64,56},{72,6... | collective-permute-start | bytes 46088 | tf_op jit(solution)/shard_map/ppermute | solution.py:41
  714.1 12.4 %collective-permute-start = (f32[6,128,5]{2,1,0:T(8,128)S(1)}, f32[6,128,5]{2,1,0:T(8,128)S(1)}, u32[]{:S(2)}, u32[]{:S(2)}) collective-permute-start(f32[6,128,5]{2,1,0:T(8,128)S(1)} %get-tuple-element.317), channel_id=1, source_target_pairs={{0,8},{8,16},{16,24},{24,32},{32,40},{40,48},{48,56},{56,64},{64,7... | collective-permute-start | bytes 46088 | tf_op jit(solution)/shard_map/ppermute | solution.py:40
  726.6 4.7 collective-permute-start.3
  727.9 3.9 collective-permute-start.2
  732.6 8.6 %copy-start.2 = (f32[256,266]{0,1:T(8,128)S(1)}, f32[256,266]{0,1:T(8,128)}, u32[]{:S(2)}) copy-start(f32[256,266]{0,1:T(8,128)} %select_reduce_fusion) | copy-start | bytes 817156
where the time goes:
time: 753 us; the launch traced here: 747 us
  local copies, waits for them, and re-layouts  304 us (40%)
  matrix products  265 us (35%)
  other arithmetic  95.5 us (13%)
  waiting for transfers between devices  58.1 us (8%)
  starting transfers between devices  22.1 us (3%)
    gather x32, local copies, waits for them, and re-layouts, blend_block(): block_params = splats[:, jnp.maximum(block_lists, 0)]  222 us
    dot_general x16, matrix products, blend_block(): jnp.einsum('tpk,kj->tpj', log_keep, strict, precision=lax.Precision.HIGHEST)  128 us
    dot_general x16, matrix products, blend_block(): jnp.einsum('tpk,ctk->ctp', weight, block_params[6:9], precision=lax.Preci...  123 us
    reduce_sum x16, other arithmetic, blend_block(): return (log_left + jnp.sum(log_keep, axis=2), colour)  77.7 us
    all_to_all x1, waiting for transfers between devices, on_device(): lax.all_to_all(outgoing, ('gs', 'img'), split_axis=1, concat_axis=1, tile...  49.8 us
    gather x1, local copies, waits for them, and re-layouts, on_device(): outgoing = gaussians[:, local_index]  34.3 us
  transfers between devices with their start and end apart: 5, of which 4 were waited for; matrix products, arithmetic and copies ran while one was open for 0% of the time, Pallas kernels for 0%

commit v1 on v0

v1 whole, which is shorter than its diff:
```python
import functools
import math

import jax
import jax.numpy as jnp
import numpy as np
from jax import lax
from jax.experimental import pallas as pl
from jax.experimental.pallas import tpu as pltpu
from jax.sharding import PartitionSpec as P

TILE = 16
LANES = 128
CAP = 80
SPLAT = 9
GROUP = 8
STEP = LANES // GROUP
LOG2E = 1.0 / math.log(2.0)
VMEM = pltpu.VMEM


coef_zero = 0.28209479177387814
coef_one = 0.4886025119029199
coef_two = [
    1.0925484305920792,
    -1.0925484305920792,
    0.31539156525252005,
    -1.0925484305920792,
    0.5462742152960396,
]
coef_three = [
    -0.5900435899266435,
    2.890611442640554,
    -0.4570457994644658,
    0.3731763325901154,
    -0.4570457994644658,
    1.445305721320277,
    -0.5900435899266435,
]
camera_z = -3000.0
ssim_share = 0.2
stable_one = 0.0001
stable_two = 0.0009


def extended(value, sides, width):
    for axis, dim in sides:
        size, length = (lax.axis_size(axis), value.shape[dim])
        up = [(i, (i + 1) % size) for i in range(size - 1)]
        down = [(j, i) for i, j in up]
        last = lax.slice_in_dim(value, length - width, length, axis=dim)
        first = lax.slice_in_dim(value, 0, width, axis=dim)
        before = lax.ppermute(last, axis, up)
        after = lax.ppermute(first, axis, down)
        value = jnp.concatenate([before, value, after], axis=dim)
    return value


def window():
    offsets = jnp.arange(11, dtype=jnp.float32) - 5.0
    weights = jnp.exp(-offsets * offsets / 4.5)
    return weights / jnp.sum(weights)


def band_matrix(outputs, inputs_len, sign):
    difference = sign * (
        jnp.arange(inputs_len, dtype=jnp.int32)[None, :]
        - jnp.arange(outputs, dtype=jnp.int32)[:, None]
    )
    offsets = jnp.arange(11, dtype=jnp.int32)
    return jnp.sum(
        jnp.where(difference[:, :, None] == offsets[None, None, :], window()[None, None, :], 0.0),
        axis=2,
    )


def loss_from(filtered, rendered, truth):
    mean_r, mean_t = (filtered[0:3], filtered[3:6])
    variance_r = filtered[6:9] - mean_r * mean_r
    variance_t = filtered[9:12] - mean_t * mean_t
    covariance = filtered[12:15] - mean_r * mean_t
    similarity = (
        (2.0 * mean_r * mean_t + stable_one)
        * (2.0 * covariance + stable_two)
        / (
            (mean_r * mean_r + mean_t * mean_t + stable_one)
            * (variance_r + variance_t + stable_two)
        )
    )
    return (1.0 - ssim_share) * jnp.mean(jnp.abs(rendered - truth), axis=0) + ssim_share * (
        1.0 - jnp.mean(similarity, axis=0)
    )


def project_chunk(gauss):
    row = lambda i: gauss[i : i + 1]
    mean_x, mean_y, mean_z = (row(0), row(1), row(2))
    squared = jnp.exp(2.0 * gauss[3:6])
    sq_0, sq_1, sq_2 = (squared[0:1], squared[1:2], squared[2:3])
    inv = 1.0 / jnp.sqrt(row(6) * row(6) + row(7) * row(7) + row(8) * row(8) + row(9) * row(9))
    quat_w, quat_x, quat_y, quat_z = (row(6) * inv, row(7) * inv, row(8) * inv, row(9) * inv)
    first_a = 1.0 - 2.0 * (quat_y * quat_y + quat_z * quat_z)
    first_b = 2.0 * (quat_x * quat_y - quat_w * quat_z)
    first_c = 2.0 * (quat_x * quat_z + quat_w * quat_y)
    second_a = 2.0 * (quat_x * quat_y + quat_w * quat_z)
    second_b = 1.0 - 2.0 * (quat_x * quat_x + quat_z * quat_z)
    second_c = 2.0 * (quat_y * quat_z - quat_w * quat_x)
    cov_xx = first_a * first_a * sq_0 + first_b * first_b * sq_1 + first_c * first_c * sq_2 + 0.3
    cov_xy = first_a * second_a * sq_0 + first_b * second_b * sq_1 + first_c * second_c * sq_2
    cov_yy = second_a * second_a * sq_0 + second_b * second_b * sq_1 + second_c * second_c * sq_2 + 0.3
    determinant = cov_xx * cov_yy - cov_xy * cov_xy
    opacity = 1.0 / (1.0 + jnp.exp(-row(10)))
    delta_z = mean_z - camera_z
    length = jnp.sqrt(mean_x * mean_x + mean_y * mean_y + delta_z * delta_z)
    dir_x, dir_y, dir_z = (mean_x / length, mean_y / length, delta_z / length)
    sq_x, sq_y, sq_z = (dir_x * dir_x, dir_y * dir_y, dir_z * dir_z)
    prod_xy, prod_yz, prod_xz = (dir_x * dir_y, dir_y * dir_z, dir_x * dir_z)
    basis = jnp.concatenate(
        [
            coef_zero * jnp.ones_like(dir_x),
            -coef_one * dir_y,
            coef_one * dir_z,
            -coef_one * dir_x,
            coef_two[0] * prod_xy,
            coef_two[1] * prod_yz,
            coef_two[2] * (2.0 * sq_z - sq_x - sq_y),
            coef_two[3] * prod_xz,
            coef_two[4] * (sq_x - sq_y),
            coef_three[0] * dir_y * (3.0 * sq_x - sq_y),
            coef_three[1] * prod_xy * dir_z,
            coef_three[2] * dir_y * (4.0 * sq_z - sq_x - sq_y),
            coef_three[3] * dir_z * (2.0 * sq_z - 3.0 * sq_x - 3.0 * sq_y),
            coef_three[4] * dir_x * (4.0 * sq_z - sq_x - sq_y),
            coef_three[5] * dir_z * (sq_x - sq_y),
            coef_three[6] * dir_x * (sq_x - 3.0 * sq_y),
        ],
        axis=0,
    )
    colour = []
    for channel in range(3):
        weights = gauss[11 + 16 * channel : 27 + 16 * channel]
        colour.append(jnp.maximum(jnp.sum(weights * basis, axis=0, keepdims=True) + 0.5, 0.0))
    return [
        mean_x,
        mean_y,
        cov_yy / determinant,
        -cov_xy / determinant,
        cov_xx / determinant,
        opacity,
    ] + colour


def lookup(tables, code, blocks, unroll):
    row = lax.shift_right_arithmetic(code, 7)
    lane = jnp.bitwise_and(code, LANES - 1)

    def one(block, found):
        hit = row == block
        out = []
        for p in range(SPLAT):
            line = jnp.broadcast_to(tables[p, pl.ds(block, 1), :], code.shape)
            taken = jnp.take_along_axis(line, lane, axis=1, mode="promise_in_bounds")
            out.append(jnp.where(hit, taken, found[p]))
        return tuple(out)

    zero = jnp.zeros(code.shape, jnp.float32)
    return lax.fori_loop(0, blocks, one, (zero,) * SPLAT, unroll=unroll)


def outgoing_kernel(gauss_ref, code_ref, out_ref, table):
    blocks = gauss_ref.shape[1] // LANES
    for block in range(blocks):
        rows = project_chunk(gauss_ref[:, block * LANES : (block + 1) * LANES])
        for p in range(SPLAT):
            table[p, block : block + 1, :] = rows[p]

    def dest(i, carry):
        where = pl.ds(pl.multiple_of(i * 8, 8), 8)
        found = lookup(table, code_ref[where, :], blocks, 8)
        for p in range(SPLAT):
            out_ref[p, where, :] = found[p]
        return carry

    lax.fori_loop(0, code_ref.shape[0] // 8, dest, 0)


def outgoing_splats(gaussians, codes):
    devices = codes.shape[0]
    return pl.pallas_call(
        outgoing_kernel,
        out_shape=jax.ShapeDtypeStruct((SPLAT, devices, LANES), jnp.float32),
        in_specs=[pl.BlockSpec(memory_space=VMEM)] * 2,
        out_specs=pl.BlockSpec(memory_space=VMEM),
        scratch_shapes=[VMEM((SPLAT, gaussians.shape[1] // LANES, LANES), jnp.float32)],
        compiler_params=pltpu.CompilerParams(vmem_limit_bytes=32 << 20),
        name="outgoing_splats",
    )(gaussians, codes)


def monomials():
    pixel = np.arange(TILE * TILE)
    x = (pixel % TILE) - 7.5
    y = (pixel // TILE) - 7.5
    rows = np.stack([x * x, y * y, x * y, x, y, np.ones_like(x)])
    return np.concatenate([rows, rows, rows, np.zeros((14, TILE * TILE))]).astype(np.float32)


COEFS = 32


def blend_kernel(groups, counts, starts, order, arrived, codes, centre_x, centre_y, mono, out_ref,
                 table, packed, packed_x, packed_y, coefs, power_a, power_b):
    rows_per_group = codes.shape[1]
    for p in range(SPLAT):
        table[p] = jnp.transpose(arrived[p])[0:CAP]
    for g in range(groups):
        here = pl.ds(starts[g], rows_per_group)
        packed[here, :] = codes[g]
        packed_x[here, :] = jnp.broadcast_to(centre_x[g : g + 1, :], (rows_per_group, LANES))
        packed_y[here, :] = jnp.broadcast_to(centre_y[g : g + 1, :], (rows_per_group, LANES))
    total = starts[groups]
    packed[pl.ds(total, 8), :] = jnp.full((8, LANES), -1, jnp.int32)
    packed_x[pl.ds(total, 8), :] = jnp.zeros((8, LANES), jnp.float32)
    packed_y[pl.ds(total, 8), :] = jnp.zeros((8, LANES), jnp.float32)

    def prepare(i, carry):
        where = pl.ds(pl.multiple_of(i * 8, 8), 8)
        code = packed[where, :]
        m_x, m_y, a, b, c, o, red, green, blue = lookup(table, code, CAP, 8)
        live = code >= 0
        u, v = (m_x - packed_x[where, :], m_y - packed_y[where, :])
        level = LOG2E * (-0.5 * (a * u * u + c * v * v) - b * u * v)
        values = [
            (-0.5 * LOG2E) * a,
            (-0.5 * LOG2E) * c,
            -LOG2E * b,
            LOG2E * (a * u + b * v),
            LOG2E * (c * v + b * u),
            jnp.where(live, level + jnp.log2(o), -1e30),
        ]
        base = i * (8 * COEFS)
        for j, value in enumerate(values):
            for part in range(3):
                rounded = value.astype(jnp.bfloat16).astype(jnp.float32)
                value = value - rounded
                coefs[pl.ds(base + part * 6 + j, 8, stride=COEFS), :] = rounded
        zero = jnp.zeros_like(red)
        for j in range(18, 24):
            coefs[pl.ds(base + j, 8, stride=COEFS), :] = zero
        for j, value in enumerate([red, green, blue, zero, zero, zero, zero, zero]):
            coefs[pl.ds(base + 24 + j, 8, stride=COEFS), :] = value
        return carry

    lax.fori_loop(0, (total + 7) // 8, prepare, 0)

    sub = lax.broadcasted_iota(jnp.int32, (GROUP, LANES), 0)

    def exponents(row):
        left = coefs[pl.ds(pl.multiple_of(row * COEFS, 8), COEFS), :].astype(jnp.bfloat16)
        return lax.dot_general(left, mono[...], (((0,), (0,)), ((), ())), preferred_element_type=jnp.float32)

    def blend(row, power, state):
        left, colour = state[0:2], state[2:8]
        left, colour = list(left), list(colour)
        lines = [
            jnp.broadcast_to(coefs[pl.ds(row * COEFS + 24 + ch, 1), :], (GROUP, LANES)) for ch in range(3)
        ]
        for k in range(STEP):
            tints = [
                jnp.take_along_axis(line, sub + GROUP * k, axis=1, mode="promise_in_bounds") for line in lines
            ]
            for half in range(2):
                alpha = jnp.exp2(power[k * GROUP : (k + 1) * GROUP, half * LANES : (half + 1) * LANES])
                weight = left[half] * alpha
                left[half] = left[half] - weight
                for ch in range(3):
                    colour[ch * 2 + half] = colour[ch * 2 + half] + weight * tints[ch]
        return tuple(left) + tuple(colour)

    ones = jnp.ones((GROUP, LANES), jnp.float32)
    nothing = jnp.zeros((GROUP, LANES), jnp.float32)

    def one_group(g, carry):
        start = starts[g]
        pairs = (counts[g] + 1) // 2

        def two_rows(i, state):
            row = start + 2 * i
            power_b[...] = exponents(row + 1)
            state = blend(row, power_a, state)
            power_a[...] = exponents(row + 2)
            return blend(row + 1, power_b, state)

        power_a[...] = exponents(start)
        state = lax.fori_loop(0, pairs, two_rows, (ones, ones) + (nothing,) * 6)
        for t in range(GROUP):
            tile = order[g * GROUP + t]
            for ch in range(3):
                for half in range(2):
                    place = (ch * 2 + half) * (groups * GROUP) + tile
                    out_ref[pl.ds(place, 1), :] = state[2 + ch * 2 + half][t : t + 1]
        return carry

    lax.fori_loop(0, groups, one_group, 0)


def blend_tiles(counts, starts, order, arrived, codes, centre_x, centre_y):
    groups, rows_per_group = codes.shape[0], codes.shape[1]
    most = groups * rows_per_group + 16
    smem = pl.BlockSpec(memory_space=pltpu.SMEM)
    vmem = pl.BlockSpec(memory_space=VMEM)
    return pl.pallas_call(
        functools.partial(blend_kernel, groups),
        out_shape=jax.ShapeDtypeStruct((6 * groups * GROUP, LANES), jnp.float32),
        in_specs=[smem] * 3 + [vmem] * 5,
        out_specs=vmem,
        scratch_shapes=[
            VMEM((SPLAT, CAP, LANES), jnp.float32),
            VMEM((most, LANES), jnp.int32),
            VMEM((most, LANES), jnp.float32),
            VMEM((most, LANES), jnp.float32),
            VMEM((most * COEFS, LANES), jnp.float32),
            VMEM((LANES, TILE * TILE), jnp.float32),
            VMEM((LANES, TILE * TILE), jnp.float32),
        ],
        compiler_params=pltpu.CompilerParams(vmem_limit_bytes=48 << 20),
        name="blend_tiles",
    )(counts, starts, order, arrived, codes, centre_x, centre_y, jnp.asarray(monomials()).astype(jnp.bfloat16))


def arrange(tile_lists):
    rows_here, cols_here, list_len = tile_lists.shape
    tiles = rows_here * cols_here
    lists = tile_lists.reshape(tiles, list_len)
    live = jnp.sum((lists >= 0).astype(jnp.int32), axis=1)
    number = jnp.arange(tiles, dtype=jnp.int32)
    ahead = (live[None, :] > live[:, None]) | ((live[None, :] == live[:, None]) & (number[None, :] < number[:, None]))
    rank = jnp.sum(ahead.astype(jnp.int32), axis=1)
    hot = rank[None, :] == number[:, None]
    order = jnp.sum(jnp.where(hot, number[None, :], 0), axis=1)
    sorted_live = jnp.sum(jnp.where(hot, live[None, :], 0), axis=1)
    groups = tiles // GROUP
    counts = (jnp.max(sorted_live.reshape(groups, GROUP), axis=1) + STEP - 1) // STEP
    counts = (counts + 1) // 2 * 2
    ends = jnp.sum(jnp.where(jnp.arange(groups)[None, :] <= jnp.arange(groups)[:, None], counts[None, :], 0), axis=1)
    starts = jnp.concatenate([jnp.zeros((1,), jnp.int32), ends.astype(jnp.int32)])
    code = jnp.where(lists >= 0, lists % CAP * LANES + lists // CAP, -1)[order]
    code = code.reshape(groups, GROUP, list_len).transpose(0, 2, 1).reshape(groups, list_len // STEP, LANES)
    tile_row = lax.axis_index("img") * rows_here + order // cols_here
    tile_col = lax.axis_index("gs") * cols_here + order % cols_here
    spread = lambda v: jnp.tile((v * TILE + TILE // 2).astype(jnp.float32).reshape(groups, GROUP), (1, STEP))
    return counts, starts, order, code, spread(tile_col), spread(tile_row)


def on_device(gaussians, send_slots, tile_lists, truth):
    rows_here, cols_here, list_len = tile_lists.shape
    devices = send_slots.shape[1] // CAP
    codes = jnp.pad(send_slots.reshape(devices, CAP), ((0, 0), (0, LANES - CAP)))
    outgoing = outgoing_splats(gaussians, codes)
    arrived = lax.all_to_all(outgoing, ("gs", "img"), split_axis=1, concat_axis=1, tiled=True)
    counts, starts, order, code, centre_x, centre_y = arrange(tile_lists)
    colours = blend_tiles(counts, starts, order, arrived, code, centre_x, centre_y)
    rendered = colours.reshape(3, 2, rows_here, cols_here, TILE // 2, TILE).transpose(0, 2, 1, 4, 3, 5)
    rendered = rendered.reshape(3, rows_here * TILE, cols_here * TILE)
    stacked = jnp.concatenate([rendered, truth])
    padded = extended(stacked, (("gs", 2), ("img", 1)), 5)
    rim_r, rim_t = (padded[0:3], padded[3:6])
    quantities = jnp.concatenate([rim_r, rim_t, rim_r * rim_r, rim_t * rim_t, rim_r * rim_t])
    img_height, img_width = (rendered.shape[1], rendered.shape[2])
    band_rows = band_matrix(img_height, img_height + 10, 1)
    band_cols = band_matrix(img_width, img_width + 10, 1).T
    filtered = jnp.einsum("ij,cjw->ciw", band_rows, quantities, precision=lax.Precision.HIGHEST)
    filtered = jnp.einsum("ciw,wv->civ", filtered, band_cols, precision=lax.Precision.HIGHEST)
    return (rendered, loss_from(filtered, rendered, truth))


def solution(mesh):
    return jax.shard_map(
        on_device,
        mesh=mesh,
        in_specs=(
            P(None, ("gs", "img")),
            P(("gs", "img"), None),
            P("img", "gs", None),
            P(None, "img", "gs"),
        ),
        out_specs=(P(None, "img", "gs"), P("img", "gs")),
        check_vma=False,
    )
```

time: 753 us -> 162 us (0.22)
  the two profiles are of different devices: /device:TPU:0 before, /device:TPU:3 now
where the time goes in v1:
time: 162 us
  Pallas kernels  70.1 us (43%)
  starting transfers between devices  31.4 us (19%)
  waiting for transfers between devices  24.9 us (15%)
  local copies, waits for them, and re-layouts  14.1 us (9%)
  matrix products  13.6 us (8%)
  other arithmetic  7.04 us (4%)
    pallas_call x1, Pallas kernels, blend_tiles(): pl.pallas_call(functools.partial(blend_kernel, groups), out_shape=jax.Sha...  56.9 us
    ppermute x2, starting transfers between devices, extended(): before = lax.ppermute(last, axis, up)  17.2 us
    pallas_call x1, Pallas kernels, outgoing_splats(): pl.pallas_call(outgoing_kernel, out_shape=jax.ShapeDtypeStruct((SPLAT, de...  13.1 us
    ppermute x2, waiting for transfers between devices, extended(): after = lax.ppermute(first, axis, down)  11.5 us
    all_to_all x1, starting transfers between devices, on_device(): lax.all_to_all(outgoing, ('gs', 'img'), split_axis=1, concat_axis=1, tile...  10.8 us
    all_to_all x1, waiting for transfers between devices, on_device(): lax.all_to_all(outgoing, ('gs', 'img'), split_axis=1, concat_axis=1, tile...  9.97 us
    dot_general x1, matrix products, on_device(): jnp.einsum('ij,cjw->ciw', band_rows, quantities, precision=lax.Precision....  8.6 us
    dot_general x1, matrix products, on_device(): jnp.einsum('ciw,wv->civ', filtered, band_cols, precision=lax.Precision.HI...  5 us
  transfers between devices with their start and end apart: 5, of which 4 were waited for; matrix products, arithmetic and copies ran while one was open for 5% of the time, Pallas kernels for 0%

profile of v1, /device:TPU:3, one launch (start us, length us, event | category | flops | bytes accessed | tf_op | source)
XLA Modules:
  0.0 162.0 jit_solution(18048614041803720869)
XLA Ops:
  0.6 0.5 broadcast.303
  1.2 1.5 reduce.4
  2.8 1.3 copy-done
  4.1 13.1 %outgoing_splats.1 = f32[9,128,128]{2,1,0:T(8,128)S(1)} custom-call(f32[59,5120]{1,0:T(8,128)S(1)} %copy-done, s32[128,128]{1,0:T(8,128)S(1)} %pad.4.code_ref), custom_call_target="tpu_custom_call" | custom-call | tf_op jit(solution)/shard_map/outgoing_splats/pallas_call | solution.py:189
  17.2 1.4 copy.34
  18.6 10.8 %all-to-all-start = ((f32[9,128,128]{2,0,1:T(8,128)}), f32[9,128,128]{2,0,1:T(8,128)S(1)}, u32[]{:S(2)}, u32[]{:S(2)}) async-start(f32[9,128,128]{2,0,1:T(8,128)} %copy.34), calls=%async_computation | async-start | bytes 2097152 | tf_op jit(solution)/shard_map/all_to_all | solution.py:360
  29.5 0.3 convert_reduce_fusion
  29.8 0.2 convert_reduce_fusion.1
  30.3 0.6 fusion.48
  31.4 0.7 broadcast_divide_fusion.1
  32.2 1.5 gather_fusion
  33.7 1.8 %copy.35 = s32[16,8,512]{0,1,2:T(8,128)S(1)} copy(s32[16,8,512]{2,1,0:T(8,128)} %bitcast.44) | data formatting | bytes 524288 | tf_op jit(solution)/shard_map/reshape | solution.py:348
  35.5 0.6 copy.41.codes
  36.3 1.1 select_reduce_fusion
  37.4 10.0 %all-to-all-done = f32[9,128,128]{2,0,1:T(8,128)S(1)} async-done(((f32[9,128,128]{2,0,1:T(8,128)}), f32[9,128,128]{2,0,1:T(8,128)S(1)}, u32[]{:S(2)}, u32[]{:S(2)}) %all-to-all-start) | async-done | bytes 589856 | tf_op jit(solution)/shard_map/all_to_all | solution.py:360
  47.4 0.2 copy.40.arrived
  47.6 56.9 %blend_tiles.1 = f32[768,128]{1,0:T(8,128)S(1)} custom-call(s32[16]{0:T(128)S(1)} %fusion.47.counts, s32[17]{0:T(128)S(1)} %pad_add_fusion.starts, s32[128]{0:T(128)S(1)} %get-tuple-element.2.order, f32[9,128,128]{2,1,0:T(8,128)S(1)} %copy.40.arrived, s32[16,32,128]{2,1,0:T(8,128)S(1)} %copy.41.codes, f32[16,128]{1,0:T(8,128)S(1)} %copy.42.centre_x, ...), custom_call_target="tpu_custom_call" | custom-call | tf_op jit(solution)/shard_map/blend_tiles/pallas_call | solution.py:312
  104.5 0.9 reshape.186
  105.5 2.3 %copy.44 = f32[3,8,2,8,16,16]{5,4,3,2,1,0:T(8,128)} copy(f32[3,8,2,8,16,16]{5,3,4,1,2,0:T(8,128)S(1)} %bitcast.42) | data formatting | bytes 786432 | tf_op jit(solution)/shard_map/transpose | solution.py:363
  107.8 2.8 %reshape.187 = f32[3,128,256]{2,1,0:T(8,128)S(1)} reshape(f32[3,8,2,8,16,16]{5,4,3,2,1,0:T(8,128)} %copy.44) | data formatting | bytes 786432 | tf_op jit(solution)/shard_map/reshape | solution.py:364
  110.9 9.3 %collective-permute-start = (f32[6,128,5]{2,1,0:T(8,128)S(1)}, f32[6,128,5]{2,1,0:T(8,128)S(1)}, u32[]{:S(2)}, u32[]{:S(2)}) collective-permute-start(f32[6,128,5]{2,1,0:T(8,128)S(1)} %get-tuple-element.11), channel_id=1, source_target_pairs={{0,8},{8,16},{16,24},{24,32},{32,40},{40,48},{48,56},{56,64},{64,7... | collective-permute-start | bytes 46088 | tf_op jit(solution)/shard_map/ppermute | solution.py:53
  120.2 1.3 collective-permute-start.1
  121.6 3.4 %collective-permute-done = f32[6,128,5]{2,1,0:T(8,128)S(1)} collective-permute-done((f32[6,128,5]{2,1,0:T(8,128)S(1)}, f32[6,128,5]{2,1,0:T(8,128)S(1)}, u32[]{:S(2)}, u32[]{:S(2)}) %collective-permute-start) | collective-permute-done | bytes 15392 | tf_op jit(solution)/shard_map/ppermute | solution.py:53
  124.9 8.1 %collective-permute-done.1 = f32[6,128,5]{2,1,0:T(8,128)S(1)} collective-permute-done((f32[6,128,5]{2,1,0:T(8,128)S(1)}, f32[6,128,5]{2,1,0:T(8,128)S(1)}, u32[]{:S(2)}, u32[]{:S(2)}) %collective-permute-start.1) | collective-permute-done | bytes 15392 | tf_op jit(solution)/shard_map/ppermute | solution.py:54
  133.2 7.9 %collective-permute-start.2 = (f32[6,5,266]{2,1,0:T(8,128)S(1)}, f32[6,5,266]{2,1,0:T(8,128)S(1)}, u32[]{:S(2)}, u32[]{:S(2)}) collective-permute-start(f32[6,5,266]{2,1,0:T(8,128)S(1)} %get-tuple-element.6), channel_id=1, source_target_pairs={{0,1},{1,2},{2,3},{3,4},{4,5},{5,6},{6,7},{8,9},{9,10},{10,11},{11... | collective-permute-start | bytes 95768 | tf_op jit(solution)/shard_map/ppermute | solution.py:53
  141.1 2.1 %collective-permute-start.3 = (f32[6,5,266]{2,1,0:T(8,128)S(1)}, f32[6,5,266]{2,1,0:T(8,128)S(1)}, u32[]{:S(2)}, u32[]{:S(2)}) collective-permute-start(f32[6,5,266]{2,1,0:T(8,128)S(1)} %get-tuple-element.7), channel_id=1, source_target_pairs={{1,0},{2,1},{3,2},{4,3},{5,4},{6,5},{7,6},{9,8},{10,9},{11,10},{12... | collective-permute-start | bytes 95768 | tf_op jit(solution)/shard_map/ppermute | solution.py:54
  143.3 3.4 %collective-permute-done.3 = f32[6,5,266]{2,1,0:T(8,128)S(1)} collective-permute-done((f32[6,5,266]{2,1,0:T(8,128)S(1)}, f32[6,5,266]{2,1,0:T(8,128)S(1)}, u32[]{:S(2)}, u32[]{:S(2)}) %collective-permute-start.3) | collective-permute-done | bytes 31952 | tf_op jit(solution)/shard_map/ppermute | solution.py:54
  146.7 0.5 pad_maximum_fusion
  147.4 8.6 %fusion = f32[15,266,128]{2,1,0:T(8,128)S(1)} fusion(f32[3,138,266]{2,1,0:T(8,128)S(1)} %get-tuple-element.9, f32[3,138,266]{2,1,0:T(8,128)S(1)} %get-tuple-element.10, f32[3,138,266]{2,1,0:T(8,128)S(1)} %get-tuple-element.8, f32[6,5,266]{2,1,0:T(8,128)S(1)} %collective-permute-done.3, f32[6,128,5]{2,1,0:T(8,128)S(1)} %collective-permute-done.1, ...), kind=kOutput, calls=%fused_computation.1 | convolution fusion | flops 849606656 | bytes 4316016 | tf_op jit(solution)/shard_map/ij,cjw->ciw/dot_general | solution.py:372
  156.0 5.0 %fusion.16 = f32[15,128,256]{2,1,0:T(8,128)S(1)} fusion(f32[15,266,128]{2,1,0:T(8,128)S(1)} %fusion, f32[256,266]{0,1:T(8,128)S(1)} %copy-done.3), kind=kOutput, calls=%fused_computation.19 | convolution fusion | flops 1568931840 | bytes 4281344 | tf_op jit(solution)/shard_map/ciw,wv->civ/dot_general | solution.py:373
  161.0 0.3 fusion.25
  161.3 0.7 multiply_add_fusion
  (39 shorter events, 2.0 us)
Async XLA Ops:
  0.6 28.8 %copy-start.4 = (s32[8,16,512]{2,1,0:T(8,128)S(1)}, s32[8,16,512]{2,1,0:T(8,128)}, u32[]{:S(2)}) copy-start(s32[8,16,512]{2,1,0:T(8,128)} %param.7) | copy-start | bytes 786436
  2.8 1.3 copy-start
  18.6 28.8 %all-to-all-start = ((f32[9,128,128]{2,0,1:T(8,128)}), f32[9,128,128]{2,0,1:T(8,128)S(1)}, u32[]{:S(2)}, u32[]{:S(2)}) async-start(f32[9,128,128]{2,0,1:T(8,128)} %copy.34), calls=%async_computation | async-start | bytes 2097152 | tf_op jit(solution)/shard_map/all_to_all | solution.py:360
  33.7 13.9 %copy-start.1 = (bf16[32,256]{1,0:T(8,128)(2,1)S(1)}, bf16[32,256]{1,0:T(8,128)(2,1)}, u32[]{:S(2)}) copy-start(bf16[32,256]{1,0:T(8,128)(2,1)} %constant.125.mono) | copy-start | bytes 49156
  107.8 2.9 %copy-start.5 = (f32[3,128,256]{2,1,0:T(8,128)S(1)}, f32[3,128,256]{2,1,0:T(8,128)}, u32[]{:S(2)}) copy-start(f32[3,128,256]{2,1,0:T(8,128)} %param.8) | copy-start | bytes 1179652
  110.6 36.6 %copy-start.2 = (f32[3,128,256]{2,1,0:T(8,128)}, f32[3,128,256]{2,1,0:T(8,128)S(1)}, u32[]{:S(2)}) copy-start(f32[3,128,256]{2,1,0:T(8,128)S(1)} %reshape.187) | copy-start | bytes 1179652
  110.9 14.0 %collective-permute-start = (f32[6,128,5]{2,1,0:T(8,128)S(1)}, f32[6,128,5]{2,1,0:T(8,128)S(1)}, u32[]{:S(2)}, u32[]{:S(2)}) collective-permute-start(f32[6,128,5]{2,1,0:T(8,128)S(1)} %get-tuple-element.11), channel_id=1, source_target_pairs={{0,8},{8,16},{16,24},{24,32},{32,40},{40,48},{48,56},{56,64},{64,7... | collective-permute-start | bytes 46088 | tf_op jit(solution)/shard_map/ppermute | solution.py:53
  120.2 12.8 %collective-permute-start.1 = (f32[6,128,5]{2,1,0:T(8,128)S(1)}, f32[6,128,5]{2,1,0:T(8,128)S(1)}, u32[]{:S(2)}, u32[]{:S(2)}) collective-permute-start(f32[6,128,5]{2,1,0:T(8,128)S(1)} %get-tuple-element.12), channel_id=1, source_target_pairs={{8,0},{16,8},{24,16},{32,24},{40,32},{48,40},{56,48},{64,56},{72,6... | collective-permute-start | bytes 46088 | tf_op jit(solution)/shard_map/ppermute | solution.py:54
  133.2 10.1 %collective-permute-start.2 = (f32[6,5,266]{2,1,0:T(8,128)S(1)}, f32[6,5,266]{2,1,0:T(8,128)S(1)}, u32[]{:S(2)}, u32[]{:S(2)}) collective-permute-start(f32[6,5,266]{2,1,0:T(8,128)S(1)} %get-tuple-element.6), channel_id=1, source_target_pairs={{0,1},{1,2},{2,3},{3,4},{4,5},{5,6},{6,7},{8,9},{9,10},{10,11},{11... | collective-permute-start | bytes 95768 | tf_op jit(solution)/shard_map/ppermute | solution.py:53
  141.1 5.7 %collective-permute-start.3 = (f32[6,5,266]{2,1,0:T(8,128)S(1)}, f32[6,5,266]{2,1,0:T(8,128)S(1)}, u32[]{:S(2)}, u32[]{:S(2)}) collective-permute-start(f32[6,5,266]{2,1,0:T(8,128)S(1)} %get-tuple-element.7), channel_id=1, source_target_pairs={{1,0},{2,1},{3,2},{4,3},{5,4},{6,5},{7,6},{9,8},{10,9},{11,10},{12... | collective-permute-start | bytes 95768 | tf_op jit(solution)/shard_map/ppermute | solution.py:54
  147.4 8.6 %copy-start.3 = (f32[256,266]{0,1:T(8,128)S(1)}, f32[256,266]{0,1:T(8,128)}, u32[]{:S(2)}) copy-start(f32[256,266]{0,1:T(8,128)} %select_reduce_fusion) | copy-start | bytes 817156

commit v2 on v1

--- a/solution.py
+++ b/solution.py
@@ -13,8 +13,6 @@
 LANES = 128
 CAP = 80
 SPLAT = 9
-GROUP = 8
-STEP = LANES // GROUP
 LOG2E = 1.0 / math.log(2.0)
 VMEM = pltpu.VMEM
 
@@ -197,38 +195,102 @@
     )(gaussians, codes)
 
 
+SEG = 32
+ROWS = 40
+BLOCK = 8
+COEFS = 32
+PIXELS = TILE * TILE
+CHUNK = 64
+
+
 def monomials():
-    pixel = np.arange(TILE * TILE)
+    pixel = np.arange(PIXELS)
     x = (pixel % TILE) - 7.5
     y = (pixel // TILE) - 7.5
-    rows = np.stack([x * x, y * y, x * y, x, y, np.ones_like(x)])
-    return np.concatenate([rows, rows, rows, np.zeros((14, TILE * TILE))]).astype(np.float32)
-
-
-COEFS = 32
-
-
-def blend_kernel(groups, counts, starts, order, arrived, codes, centre_x, centre_y, mono, out_ref,
-                 table, packed, packed_x, packed_y, coefs, power_a, power_b):
-    rows_per_group = codes.shape[1]
+    cols = np.stack([x * x, y * y, x * y, x, y, np.ones_like(x)], axis=1)
+    return np.concatenate([cols, cols, cols, np.zeros((PIXELS, COEFS - 18))], axis=1).astype(np.float32)
+
+
+def split(value, parts):
+    out = []
+    for _ in range(parts):
+        rounded = value.astype(jnp.bfloat16)
+        out.append(rounded)
+        value = value - rounded.astype(jnp.float32)
+    return out
+
+
+def lane_pick(value, index, axis):
+    return jnp.take_along_axis(value, index, axis=axis, mode="promise_in_bounds")
+
+
+def blend_kernel(cols_here, first, base, arrived, lists, owner, mono, out_ref,
+                 table_a, table_b, table, packed, codes, params, coefs, power_a, power_b, state, total_ref,
+                 carry_ref, carry_owner):
+    tiles = first.shape[0] - 1
+    runs = lists.shape[0] // tiles
+    groups = (first[tiles] + LANES - 1) // LANES
+    per_group = SEG // BLOCK
+
     for p in range(SPLAT):
-        table[p] = jnp.transpose(arrived[p])[0:CAP]
-    for g in range(groups):
-        here = pl.ds(starts[g], rows_per_group)
-        packed[here, :] = codes[g]
-        packed_x[here, :] = jnp.broadcast_to(centre_x[g : g + 1, :], (rows_per_group, LANES))
-        packed_y[here, :] = jnp.broadcast_to(centre_y[g : g + 1, :], (rows_per_group, LANES))
-    total = starts[groups]
-    packed[pl.ds(total, 8), :] = jnp.full((8, LANES), -1, jnp.int32)
-    packed_x[pl.ds(total, 8), :] = jnp.zeros((8, LANES), jnp.float32)
-    packed_y[pl.ds(total, 8), :] = jnp.zeros((8, LANES), jnp.float32)
-
-    def prepare(i, carry):
-        where = pl.ds(pl.multiple_of(i * 8, 8), 8)
-        code = packed[where, :]
-        m_x, m_y, a, b, c, o, red, green, blue = lookup(table, code, CAP, 8)
-        live = code >= 0
-        u, v = (m_x - packed_x[where, :], m_y - packed_y[where, :])
+        flat = jnp.transpose(arrived[p])
+        for half, ref in enumerate((table_a, table_b)):
+            value = flat[half * ROWS : (half + 1) * ROWS]
+            if p < 8:
+                ref[pl.ds(p, ROWS, stride=8), :] = value
+            else:
+                ref[8 * ROWS : 9 * ROWS, :] = value
+    for half, ref in enumerate((table_a, table_b)):
+        for part, value in enumerate(split(ref[...], 3)):
+            table[:, part * 256 + half * LANES : part * 256 + (half + 1) * LANES] = value
+
+    packed[...] = jnp.full(packed.shape, -1, jnp.int32)
+    for t in range(tiles):
+        packed[pl.ds(first[t], runs), :] = lists[t * runs : (t + 1) * runs, :]
+
+    def turn(g, carry):
+        lanes = jnp.transpose(packed[pl.ds(pl.multiple_of(g * LANES, LANES), LANES), :])
+        codes[pl.ds(pl.multiple_of(g * SEG, SEG), SEG), :] = lanes[0:SEG]
+        return carry
+
+    lax.fori_loop(0, groups, turn, 0)
+    total_ref[...] = jnp.zeros_like(total_ref)
+    carry_ref[...] = jnp.ones_like(carry_ref)
+    carry_owner[...] = jnp.full(carry_owner.shape, -1, jnp.int32)
+
+    column = lax.broadcasted_iota(jnp.int32, (256, 256), 0)
+    table_row = lax.broadcasted_iota(jnp.int32, (ROWS, 256), 0)
+
+    def lookup(block, j):
+        slot = (block % 3) * 72
+        where = block * BLOCK + 2 * j
+        code = jnp.concatenate([codes[pl.ds(where, 1), :], codes[pl.ds(where + 1, 1), :]], axis=1)
+        col = jnp.bitwise_and(code, 255)
+        row = lax.shift_right_arithmetic(code, 8)
+        hot = jnp.where(column == col, 1.0, 0.0).astype(jnp.bfloat16)
+        found = jnp.dot(table[...], jnp.concatenate([hot, hot, hot], axis=0), preferred_element_type=jnp.float32)
+        picked = jnp.zeros((8, 256), jnp.float32)
+        rows8 = jnp.broadcast_to(row, (8, 256))
+        for r in range(ROWS):
+            picked = jnp.where(rows8 == r, found[r * 8 : (r + 1) * 8], picked)
+        ninth = jnp.sum(jnp.where(table_row == row, found[8 * ROWS :], 0.0), axis=0, keepdims=True)
+        return slot, picked, ninth
+
+    def keep(j, slot, picked, ninth):
+        for e in range(2):
+            lanes = slice(e * LANES, (e + 1) * LANES)
+            params[pl.ds(pl.multiple_of(slot + (2 * j + e) * 8, 8), 8), :] = picked[:, lanes]
+            params[pl.ds(slot + 64 + 2 * j + e, 1), :] = ninth[:, lanes]
+
+    def expand(block):
+        slot = (block % 3) * 72
+        m_x, m_y, a, b, c, o = [params[pl.ds(slot + p, BLOCK, stride=8), :] for p in range(6)]
+        live = codes[pl.ds(pl.multiple_of(block * BLOCK, BLOCK), BLOCK), :] >= 0
+        tile = owner[pl.ds(block // per_group, 1), :]
+        tile_y = lax.shift_right_logical(tile, cols_here.bit_length() - 1)
+        tile_x = jnp.bitwise_and(tile, cols_here - 1)
+        u = m_x - (tile_x * TILE + base[0]).astype(jnp.float32)
+        v = m_y - (tile_y * TILE + base[1]).astype(jnp.float32)
         level = LOG2E * (-0.5 * (a * u * u + c * v * v) - b * u * v)
         values = [
             (-0.5 * LOG2E) * a,
@@ -238,118 +300,166 @@
             LOG2E * (c * v + b * u),
             jnp.where(live, level + jnp.log2(o), -1e30),
         ]
-        base = i * (8 * COEFS)
-        for j, value in enumerate(values):
-            for part in range(3):
-                rounded = value.astype(jnp.bfloat16).astype(jnp.float32)
-                value = value - rounded
-                coefs[pl.ds(base + part * 6 + j, 8, stride=COEFS), :] = rounded
-        zero = jnp.zeros_like(red)
-        for j in range(18, 24):
-            coefs[pl.ds(base + j, 8, stride=COEFS), :] = zero
-        for j, value in enumerate([red, green, blue, zero, zero, zero, zero, zero]):
-            coefs[pl.ds(base + 24 + j, 8, stride=COEFS), :] = value
+        for i, value in enumerate(values):
+            for part, rounded in enumerate(split(value, 3)):
+                coefs[pl.ds(part * 6 + i, BLOCK, stride=COEFS), :] = rounded.astype(jnp.float32)
+
+    def exponents(j):
+        pair = [
+            coefs[pl.ds((2 * j + e) * COEFS, COEFS), :].astype(jnp.bfloat16) for e in range(2)
+        ]
+        return jnp.dot(mono[...], jnp.concatenate(pair, axis=1), preferred_element_type=jnp.float32)
+
+    def blend(block, j, power):
+        slot = (block % 3) * 72
+        at = lambda q, i: pl.ds(q * PIXELS + j * CHUNK + i * 8, 8)
+        pieces = range(CHUNK // 8)
+        left = [state[at(0, i), :] for i in pieces]
+        colour = [[state[at(1 + ch, i), :] for i in pieces] for ch in range(3)]
+        for k in range(BLOCK):
+            rows = (slot + k * 8 + 6, slot + k * 8 + 7, slot + 64 + k)
+            tints = [jnp.broadcast_to(params[pl.ds(r, 1), :], (8, LANES)) for r in rows]
+            for i in pieces:
+                alpha = jnp.exp2(power[k // 2, at(0, i), (k % 2) * LANES : (k % 2 + 1) * LANES])
+                weight = left[i] * alpha
+                left[i] = left[i] - weight
+                for ch in range(3):
+                    colour[ch][i] = colour[ch][i] + weight * tints[ch]
+        for i in pieces:
+            state[at(0, i), :] = left[i]
+            for ch in range(3):
+                state[at(1 + ch, i), :] = colour[ch][i]
+
+    lane = lax.broadcasted_iota(jnp.int32, (8, LANES), 1)
+
+    def flush(g):
+        tile = jnp.broadcast_to(owner[pl.ds(g, 1), :], (8, LANES))
+        left = state[0:PIXELS, :]
+        same = []
+        for d in (1, 2, 4, 8):
+            same.append(((pltpu.roll(tile, d, 1) == tile) & (lane >= d))[0:1])
+        for d, mask in zip((1, 2, 4, 8), same):
+            left = left * jnp.where(mask, pltpu.roll(left, d, 1), 1.0)
+        before = jnp.where(same[0], pltpu.roll(left, 1, 1), 1.0)
+        goes_on = (tile == carry_owner[...])[0:1]
+        behind = jnp.where(goes_on, carry_ref[...], 1.0)
+        before = before * behind
+        carry_ref[...] = jnp.broadcast_to((left * behind)[:, LANES - 1 :], (PIXELS, LANES))
+        carry_owner[...] = jnp.broadcast_to(tile[:, LANES - 1 :], (8, LANES))
+        member = lax.broadcasted_iota(jnp.int32, (tiles, LANES), 0) == tile[0:1]
+        member = jnp.where(member, 1.0, 0.0).astype(jnp.bfloat16)
+        member = jnp.concatenate([member, member], axis=1)
+        for ch in range(3):
+            part = before * state[(1 + ch) * PIXELS : (2 + ch) * PIXELS, :]
+            pair = jnp.concatenate(split(part, 2), axis=1)
+            total_ref[ch] += lax.dot_general(
+                member, pair, (((1,), (1,)), ((), ())), preferred_element_type=jnp.float32
+            )
+
+    coefs[...] = jnp.zeros_like(coefs)
+    steps = BLOCK // 2
+
+    def look_ahead(block):
+        for j, found in enumerate([lookup(block, j) for j in range(steps)]):
+            keep(j, *found)
+        expand(block)
+
+    look_ahead(0)
+    for j in range(steps):
+        power_a[j] = exponents(j)
+    look_ahead(1)
+
+    def one_group(g, carry):
+        state[0:PIXELS, :] = jnp.ones((PIXELS, LANES), jnp.float32)
+        state[PIXELS:, :] = jnp.zeros((3 * PIXELS, LANES), jnp.float32)
+
+        def two_blocks(i, carry):
+            for which in range(2):
+                block = g * per_group + 2 * i + which
+                now, later = ((power_a, power_b), (power_b, power_a))[which]
+
+                found = [lookup(block + 2, j) for j in range(steps)]
+                for j in range(steps):
+                    later[j] = exponents(j)
+                for j in range(steps):
+                    blend(block, j, now)
+                for j in range(steps):
+                    keep(j, *found[j])
+                expand(block + 2)
+            return carry
+
+        lax.fori_loop(0, per_group // 2, two_blocks, 0)
+        flush(g)
         return carry
 
-    lax.fori_loop(0, (total + 7) // 8, prepare, 0)
-
-    sub = lax.broadcasted_iota(jnp.int32, (GROUP, LANES), 0)
-
-    def exponents(row):
-        left = coefs[pl.ds(pl.multiple_of(row * COEFS, 8), COEFS), :].astype(jnp.bfloat16)
-        return lax.dot_general(left, mono[...], (((0,), (0,)), ((), ())), preferred_element_type=jnp.float32)
-
-    def blend(row, power, state):
-        left, colour = state[0:2], state[2:8]
-        left, colour = list(left), list(colour)
-        lines = [
-            jnp.broadcast_to(coefs[pl.ds(row * COEFS + 24 + ch, 1), :], (GROUP, LANES)) for ch in range(3)
-        ]
-        for k in range(STEP):
-            tints = [
-                jnp.take_along_axis(line, sub + GROUP * k, axis=1, mode="promise_in_bounds") for line in lines
-            ]
-            for half in range(2):
-                alpha = jnp.exp2(power[k * GROUP : (k + 1) * GROUP, half * LANES : (half + 1) * LANES])
-                weight = left[half] * alpha
-                left[half] = left[half] - weight
-                for ch in range(3):
-                    colour[ch * 2 + half] = colour[ch * 2 + half] + weight * tints[ch]
-        return tuple(left) + tuple(colour)
-
-    ones = jnp.ones((GROUP, LANES), jnp.float32)
-    nothing = jnp.zeros((GROUP, LANES), jnp.float32)
-
-    def one_group(g, carry):
-        start = starts[g]
-        pairs = (counts[g] + 1) // 2
-
-        def two_rows(i, state):
-            row = start + 2 * i
-            power_b[...] = exponents(row + 1)
-            state = blend(row, power_a, state)
-            power_a[...] = exponents(row + 2)
-            return blend(row + 1, power_b, state)
-
-        power_a[...] = exponents(start)
-        state = lax.fori_loop(0, pairs, two_rows, (ones, ones) + (nothing,) * 6)
-        for t in range(GROUP):
-            tile = order[g * GROUP + t]
-            for ch in range(3):
-                for half in range(2):
-                    place = (ch * 2 + half) * (groups * GROUP) + tile
-                    out_ref[pl.ds(place, 1), :] = state[2 + ch * 2 + half][t : t + 1]
-        return carry
-
     lax.fori_loop(0, groups, one_group, 0)
 
-
-def blend_tiles(counts, starts, order, arrived, codes, centre_x, centre_y):
-    groups, rows_per_group = codes.shape[0], codes.shape[1]
-    most = groups * rows_per_group + 16
+    piece = lax.broadcasted_iota(jnp.int32, (8, LANES), 1)
+    inner, outer = piece % TILE, piece // TILE
+    sub = lax.broadcasted_iota(jnp.int32, (8, LANES), 0)
+    skew = (outer + 8 - sub) % 8 * TILE + inner
+    down = (outer + 8 - sub) % 8
+    back = (outer + sub) % 8 * TILE + inner
+    for ch in range(3):
+        for r in range(tiles // cols_here):
+            for q in range(cols_here // 8):
+                for h in range(2):
+                    x = total_ref[ch, r * cols_here + q * 8 : r * cols_here + q * 8 + 8, h * LANES : (h + 1) * LANES]
+                    x = lane_pick(lane_pick(lane_pick(x, skew, 1), down, 0), back, 1)
+                    out_ref[ch, r * TILE + h * 8 : r * TILE + h * 8 + 8, q * LANES : (q + 1) * LANES] = x
+
+
+def blend_tiles(first, base, arrived, lists, owner, cols_here):
+    tiles = first.shape[0] - 1
+    most = lists.shape[0] // LANES
     smem = pl.BlockSpec(memory_space=pltpu.SMEM)
     vmem = pl.BlockSpec(memory_space=VMEM)
+    f32 = jnp.float32
     return pl.pallas_call(
-        functools.partial(blend_kernel, groups),
-        out_shape=jax.ShapeDtypeStruct((6 * groups * GROUP, LANES), jnp.float32),
-        in_specs=[smem] * 3 + [vmem] * 5,
+        functools.partial(blend_kernel, cols_here),
+        out_shape=jax.ShapeDtypeStruct((3, tiles // cols_here * TILE, cols_here * TILE), f32),
+        in_specs=[smem] * 2 + [vmem] * 4,
         out_specs=vmem,
         scratch_shapes=[
-            VMEM((SPLAT, CAP, LANES), jnp.float32),
-            VMEM((most, LANES), jnp.int32),
-            VMEM((most, LANES), jnp.float32),
-            VMEM((most, LANES), jnp.float32),
-            VMEM((most * COEFS, LANES), jnp.float32),
-            VMEM((LANES, TILE * TILE), jnp.float32),
-            VMEM((LANES, TILE * TILE), jnp.float32),
+            VMEM((9 * ROWS, LANES), f32),
+            VMEM((9 * ROWS, LANES), f32),
+            VMEM((9 * ROWS, 768), jnp.bfloat16),
+            VMEM((lists.shape[0] + LANES, LANES), jnp.int32),
+            VMEM(((most + 1) * SEG, LANES), jnp.int32),
+            VMEM((3 * 72, LANES), f32),
+            VMEM((BLOCK * COEFS, LANES), f32),
+            VMEM((BLOCK // 2, PIXELS, 256), f32),
+            VMEM((BLOCK // 2, PIXELS, 256), f32),
+            VMEM((4 * PIXELS, LANES), f32),
+            VMEM((3, tiles, PIXELS), f32),
+            VMEM((PIXELS, LANES), f32),
+            VMEM((8, LANES), jnp.int32),
         ],
         compiler_params=pltpu.CompilerParams(vmem_limit_bytes=48 << 20),
         name="blend_tiles",
-    )(counts, starts, order, arrived, codes, centre_x, centre_y, jnp.asarray(monomials()).astype(jnp.bfloat16))
+    )(first, base, arrived, lists, owner, jnp.asarray(monomials()).astype(jnp.bfloat16))
 
 
 def arrange(tile_lists):
     rows_here, cols_here, list_len = tile_lists.shape
     tiles = rows_here * cols_here
     lists = tile_lists.reshape(tiles, list_len)
-    live = jnp.sum((lists >= 0).astype(jnp.int32), axis=1)
+    runs = list_len // SEG
+    live = (jnp.sum((lists >= 0).astype(jnp.int32), axis=1) + SEG - 1) // SEG
     number = jnp.arange(tiles, dtype=jnp.int32)
-    ahead = (live[None, :] > live[:, None]) | ((live[None, :] == live[:, None]) & (number[None, :] < number[:, None]))
-    rank = jnp.sum(ahead.astype(jnp.int32), axis=1)
-    hot = rank[None, :] == number[:, None]
-    order = jnp.sum(jnp.where(hot, number[None, :], 0), axis=1)
-    sorted_live = jnp.sum(jnp.where(hot, live[None, :], 0), axis=1)
-    groups = tiles // GROUP
-    counts = (jnp.max(sorted_live.reshape(groups, GROUP), axis=1) + STEP - 1) // STEP
-    counts = (counts + 1) // 2 * 2
-    ends = jnp.sum(jnp.where(jnp.arange(groups)[None, :] <= jnp.arange(groups)[:, None], counts[None, :], 0), axis=1)
-    starts = jnp.concatenate([jnp.zeros((1,), jnp.int32), ends.astype(jnp.int32)])
-    code = jnp.where(lists >= 0, lists % CAP * LANES + lists // CAP, -1)[order]
-    code = code.reshape(groups, GROUP, list_len).transpose(0, 2, 1).reshape(groups, list_len // STEP, LANES)
-    tile_row = lax.axis_index("img") * rows_here + order // cols_here
-    tile_col = lax.axis_index("gs") * cols_here + order % cols_here
-    spread = lambda v: jnp.tile((v * TILE + TILE // 2).astype(jnp.float32).reshape(groups, GROUP), (1, STEP))
-    return counts, starts, order, code, spread(tile_col), spread(tile_row)
+    ends = jnp.sum(jnp.where(number[None, :] <= number[:, None], live[None, :], 0), axis=1).astype(jnp.int32)
+    first = jnp.concatenate([jnp.zeros((1,), jnp.int32), ends])
+    most = tiles * runs
+    segment = jnp.arange(most + LANES, dtype=jnp.int32)
+    owner = jnp.sum((ends[None, :] <= segment[:, None]).astype(jnp.int32), axis=1).reshape(-1, LANES)
+    slot, source = lists % CAP, lists // CAP
+    code = jnp.where(lists >= 0, slot % ROWS * 256 + slot // ROWS * LANES + source, -1)
+    code = jnp.pad(code.reshape(most, SEG), ((0, 0), (0, LANES - SEG)), constant_values=-1)
+    half = TILE // 2
+    base = jnp.stack(
+        [lax.axis_index("gs") * (cols_here * TILE) + half, lax.axis_index("img") * (rows_here * TILE) + half]
+    ).astype(jnp.int32)
+    return first, base, code, owner
 
 
 def on_device(gaussians, send_slots, tile_lists, truth):
@@ -358,10 +468,8 @@
     codes = jnp.pad(send_slots.reshape(devices, CAP), ((0, 0), (0, LANES - CAP)))
     outgoing = outgoing_splats(gaussians, codes)
     arrived = lax.all_to_all(outgoing, ("gs", "img"), split_axis=1, concat_axis=1, tiled=True)
-    counts, starts, order, code, centre_x, centre_y = arrange(tile_lists)
-    colours = blend_tiles(counts, starts, order, arrived, code, centre_x, centre_y)
-    rendered = colours.reshape(3, 2, rows_here, cols_here, TILE // 2, TILE).transpose(0, 2, 1, 4, 3, 5)
-    rendered = rendered.reshape(3, rows_here * TILE, cols_here * TILE)
+    first, base, code, owner = arrange(tile_lists)
+    rendered = blend_tiles(first, base, arrived, code, owner, cols_here)
     stacked = jnp.concatenate([rendered, truth])
     padded = extended(stacked, (("gs", 2), ("img", 1)), 5)
     rim_r, rim_t = (padded[0:3], padded[3:6])

time: 162 us -> 118 us (0.73)
  the two profiles are of different devices: /device:TPU:3 before, /device:TPU:27 now
where the time goes in v2:
time: 118 us; the launch traced here: 117 us
  Pallas kernels  44 us (37%)
  waiting for transfers between devices  21.7 us (18%)
  starting transfers between devices  21.1 us (18%)
  matrix products  13.4 us (11%)
  other arithmetic  10.6 us (9%)
  local copies, waits for them, and re-layouts  5.57 us (5%)
    pallas_call x1, Pallas kernels, blend_tiles(): pl.pallas_call(functools.partial(blend_kernel, cols_here), out_shape=jax....  30.8 us
    pallas_call x1, Pallas kernels, outgoing_splats(): pl.pallas_call(outgoing_kernel, out_shape=jax.ShapeDtypeStruct((SPLAT, de...  13.1 us
    all_to_all x1, starting transfers between devices, on_device(): lax.all_to_all(outgoing, ('gs', 'img'), split_axis=1, concat_axis=1, tile...  10.6 us
    ppermute x2, waiting for transfers between devices, extended(): after = lax.ppermute(first, axis, down)  9.36 us
    all_to_all x1, waiting for transfers between devices, on_device(): lax.all_to_all(outgoing, ('gs', 'img'), split_axis=1, concat_axis=1, tile...  8.7 us
    dot_general x1, matrix products, on_device(): jnp.einsum('ij,cjw->ciw', band_rows, quantities, precision=lax.Precision....  8.46 us
    ppermute x2, starting transfers between devices, extended(): after = lax.ppermute(first, axis, down)  5.46 us
    ppermute x2, starting transfers between devices, extended(): before = lax.ppermute(last, axis, up)  5.04 us
  transfers between devices with their start and end apart: 5, of which 4 were waited for; matrix products, arithmetic and copies ran while one was open for 6% of the time, Pallas kernels for 0%

profile of v2, /device:TPU:27, one launch (start us, length us, event | category | flops | bytes accessed | tf_op | source)
XLA Modules:
  0.0 117.3 jit_solution(9971808518660080327)
XLA Ops:
  0.6 0.5 broadcast.168
  1.1 1.5 %reduce.4 = s32[10240]{0:T(1024)S(1)} reduce(s32[1,10240]{1,0:T(1,128)} %param.6, s32[]{:T(128)} %broadcast.168), dimensions={0}, to_apply=%param.6.reduce_sub_computation.3 | reduce | bytes 81924 | tf_op args[1]
  2.8 1.3 %copy-done = f32[59,5120]{1,0:T(8,128)S(1)} copy-done((f32[59,5120]{1,0:T(8,128)S(1)}, f32[59,5120]{1,0:T(8,128)}, u32[]{:S(2)}) %copy-start) | copy-done | bytes 1208344
  4.1 13.1 %outgoing_splats.1 = f32[9,128,128]{2,1,0:T(8,128)S(1)} custom-call(f32[59,5120]{1,0:T(8,128)S(1)} %copy-done, s32[128,128]{1,0:T(8,128)S(1)} %pad.8.code_ref), custom_call_target="tpu_custom_call" | custom-call | tf_op jit(solution)/shard_map/outgoing_splats/pallas_call | solution.py:187
  17.2 1.4 %copy.9 = f32[9,128,128]{2,0,1:T(8,128)} copy(f32[9,128,128]{2,1,0:T(8,128)S(1)} %outgoing_splats.1) | data formatting | bytes 1179648 | tf_op jit(solution)/shard_map/outgoing_splats/pallas_call | solution.py:187
  18.6 10.6 %all-to-all-start = ((f32[9,128,128]{2,0,1:T(8,128)}), f32[9,128,128]{2,0,1:T(8,128)S(1)}, u32[]{:S(2)}, u32[]{:S(2)}) async-start(f32[9,128,128]{2,0,1:T(8,128)} %copy.9), calls=%async_computation | async-start | bytes 2097152 | tf_op jit(solution)/shard_map/all_to_all | solution.py:470
  29.2 0.3 convert_reduce_fusion.1
  29.5 0.6 fusion.39
  30.1 0.3 div.58
  30.4 0.3 rem.53
  30.7 0.3 ge.10
  31.1 1.0 ne.75
  32.3 0.6 broadcast_divide_fusion.1
  33.0 2.6 %fusion.23 = s32[2048,32]{1,0:T(8,128)S(1)} fusion(pred[2048,32]{1,0:T(8,128)(4,1)S(1)} %ge.10, s32[2048,32]{1,0:T(8,128)S(1)} %div.58, pred[2048,32]{1,0:T(8,128)(4,1)} %ne.75, s32[2048,32]{1,0:T(8,128)S(1)} %rem.53), kind=kLoop, calls=%fused_computation.32 | loop fusion | flops 1638400 | bytes 917504 | tf_op jit(solution)/shard_map/jit(_where)/select_n | solution.py:456
  35.8 0.4 convert_reduce_fusion
  36.2 0.4 select_reduce_fusion
  36.6 8.7 %all-to-all-done = f32[9,128,128]{2,0,1:T(8,128)S(1)} async-done(((f32[9,128,128]{2,0,1:T(8,128)}), f32[9,128,128]{2,0,1:T(8,128)S(1)}, u32[]{:S(2)}, u32[]{:S(2)}) %all-to-all-start) | async-done | bytes 589856 | tf_op jit(solution)/shard_map/all_to_all | solution.py:470
  45.5 30.8 %blend_tiles.1 = f32[3,128,256]{2,1,0:T(8,128)} custom-call(s32[129]{0:T(256)S(1)} %pad_add_fusion.first, s32[2]{0:T(128)S(1)} %pad_add_fusion.1.base, f32[9,128,128]{2,1,0:T(8,128)S(1)} %copy.10.arrived, s32[2048,128]{1,0:T(8,128)S(1)} %pad.9.lists, s32[17,128]{1,0:T(8,128)S(1)} %bitcast.12, bf16[256,32]{1,0:T(8,128)(2,1)S(1)} %copy-done.1), custom_call_target="tpu_custom_call" | custom-call | tf_op jit(solution)/shard_map/blend_tiles/pallas_call | solution.py:418
  76.3 1.2 %fusion.26 = (f32[6,128,5]{2,1,0:T(8,128)S(1)}, f32[6,128,5]{2,1,0:T(8,128)S(1)}) fusion(f32[3,128,256]{2,1,0:T(8,128)} %blend_tiles.1, f32[3,128,256]{2,1,0:T(8,128)S(1)} %copy-done.3), kind=kLoop, calls=%fused_computation.44 | loop fusion | flops 7680 | bytes 817152 | tf_op jit(solution)/shard_map/concatenate | solution.py:473
  77.5 1.9 %collective-permute-start = (f32[6,128,5]{2,1,0:T(8,128)S(1)}, f32[6,128,5]{2,1,0:T(8,128)S(1)}, u32[]{:S(2)}, u32[]{:S(2)}) collective-permute-start(f32[6,128,5]{2,1,0:T(8,128)S(1)} %get-tuple-element.9), channel_id=1, source_target_pairs={{0,8},{8,16},{16,24},{24,32},{32,40},{40,48},{48,56},{56,64},{64,7... | collective-permute-start | bytes 46088 | tf_op jit(solution)/shard_map/ppermute | solution.py:51
  79.5 3.4 %collective-permute-start.1 = (f32[6,128,5]{2,1,0:T(8,128)S(1)}, f32[6,128,5]{2,1,0:T(8,128)S(1)}, u32[]{:S(2)}, u32[]{:S(2)}) collective-permute-start(f32[6,128,5]{2,1,0:T(8,128)S(1)} %get-tuple-element.10), channel_id=1, source_target_pairs={{8,0},{16,8},{24,16},{32,24},{40,32},{48,40},{56,48},{64,56},{72,6... | collective-permute-start | bytes 46088 | tf_op jit(solution)/shard_map/ppermute | solution.py:52
  83.0 3.6 %collective-permute-done = f32[6,128,5]{2,1,0:T(8,128)S(1)} collective-permute-done((f32[6,128,5]{2,1,0:T(8,128)S(1)}, f32[6,128,5]{2,1,0:T(8,128)S(1)}, u32[]{:S(2)}, u32[]{:S(2)}) %collective-permute-start) | collective-permute-done | bytes 15392 | tf_op jit(solution)/shard_map/ppermute | solution.py:51
  86.6 5.9 %collective-permute-done.1 = f32[6,128,5]{2,1,0:T(8,128)S(1)} collective-permute-done((f32[6,128,5]{2,1,0:T(8,128)S(1)}, f32[6,128,5]{2,1,0:T(8,128)S(1)}, u32[]{:S(2)}, u32[]{:S(2)}) %collective-permute-start.1) | collective-permute-done | bytes 15392 | tf_op jit(solution)/shard_map/ppermute | solution.py:52
  92.5 0.9 pad_maximum_fusion.5
  93.4 3.1 %collective-permute-start.2 = (f32[6,5,266]{2,1,0:T(8,128)S(1)}, f32[6,5,266]{2,1,0:T(8,128)S(1)}, u32[]{:S(2)}, u32[]{:S(2)}) collective-permute-start(f32[6,5,266]{2,1,0:T(8,128)S(1)} %get-tuple-element.4), channel_id=1, source_target_pairs={{0,1},{1,2},{2,3},{3,4},{4,5},{5,6},{6,7},{8,9},{9,10},{10,11},{11... | collective-permute-start | bytes 95768 | tf_op jit(solution)/shard_map/ppermute | solution.py:51
  96.5 2.1 %collective-permute-start.3 = (f32[6,5,266]{2,1,0:T(8,128)S(1)}, f32[6,5,266]{2,1,0:T(8,128)S(1)}, u32[]{:S(2)}, u32[]{:S(2)}) collective-permute-start(f32[6,5,266]{2,1,0:T(8,128)S(1)} %get-tuple-element.5), channel_id=1, source_target_pairs={{1,0},{2,1},{3,2},{4,3},{5,4},{6,5},{7,6},{9,8},{10,9},{11,10},{12... | collective-permute-start | bytes 95768 | tf_op jit(solution)/shard_map/ppermute | solution.py:52
  98.7 3.5 %collective-permute-done.3 = f32[6,5,266]{2,1,0:T(8,128)S(1)} collective-permute-done((f32[6,5,266]{2,1,0:T(8,128)S(1)}, f32[6,5,266]{2,1,0:T(8,128)S(1)}, u32[]{:S(2)}, u32[]{:S(2)}) %collective-permute-start.3) | collective-permute-done | bytes 31952 | tf_op jit(solution)/shard_map/ppermute | solution.py:52
  102.2 0.5 pad_maximum_fusion
  102.9 8.5 %fusion = f32[15,266,128]{2,1,0:T(8,128)S(1)} fusion(f32[3,138,266]{2,1,0:T(8,128)S(1)} %get-tuple-element.7, f32[3,138,266]{2,1,0:T(8,128)S(1)} %get-tuple-element.8, f32[3,138,266]{2,1,0:T(8,128)S(1)} %get-tuple-element.6, f32[6,5,266]{2,1,0:T(8,128)S(1)} %collective-permute-done.3, f32[6,128,5]{2,1,0:T(8,128)S(1)} %collective-permute-done.1, ...), kind=kOutput, calls=%fused_computation | convolution fusion | flops 850157312 | bytes 4316016 | tf_op jit(solution)/shard_map/ij,cjw->ciw/dot_general | solution.py:480
  111.3 5.0 %fusion.18 = f32[15,128,256]{2,1,0:T(8,128)S(1)} fusion(f32[15,266,128]{2,1,0:T(8,128)S(1)} %fusion, f32[256,266]{0,1:T(8,128)S(1)} %select_reduce_fusion), kind=kOutput, calls=%fused_computation.20 | convolution fusion | flops 1568931840 | bytes 4281344 | tf_op jit(solution)/shard_map/ciw,wv->civ/dot_general | solution.py:481
  116.3 0.3 fusion.34
  116.6 0.7 multiply_add_fusion
  (26 shorter events, 1.2 us)
Async XLA Ops:
  2.8 1.3 %copy-start = (f32[59,5120]{1,0:T(8,128)S(1)}, f32[59,5120]{1,0:T(8,128)}, u32[]{:S(2)}) copy-start(f32[59,5120]{1,0:T(8,128)} %gauss_ref.1) | copy-start | bytes 3624964
  17.2 12.0 %copy-start.4 = (s32[8,16,512]{2,1,0:T(8,128)S(1)}, s32[8,16,512]{2,1,0:T(8,128)}, u32[]{:S(2)}) copy-start(s32[8,16,512]{2,1,0:T(8,128)} %param.7) | copy-start | bytes 786436
  18.6 26.7 %all-to-all-start = ((f32[9,128,128]{2,0,1:T(8,128)}), f32[9,128,128]{2,0,1:T(8,128)S(1)}, u32[]{:S(2)}, u32[]{:S(2)}) async-start(f32[9,128,128]{2,0,1:T(8,128)} %copy.9), calls=%async_computation | async-start | bytes 2097152 | tf_op jit(solution)/shard_map/all_to_all | solution.py:470
  35.7 9.8 %copy-start.1 = (bf16[256,32]{1,0:T(8,128)(2,1)S(1)}, bf16[256,32]{1,0:T(8,128)(2,1)}, u32[]{:S(2)}) copy-start(bf16[256,32]{1,0:T(8,128)(2,1)} %constant.104.mono) | copy-start | bytes 49156
  36.2 40.1 %copy-start.3 = (f32[3,128,256]{2,1,0:T(8,128)S(1)}, f32[3,128,256]{2,1,0:T(8,128)}, u32[]{:S(2)}) copy-start(f32[3,128,256]{2,1,0:T(8,128)} %param.8) | copy-start | bytes 1179652
  76.3 22.3 %copy-start.2 = (f32[3,128,256]{2,1,0:T(8,128)S(1)}, f32[3,128,256]{2,1,0:T(8,128)}, u32[]{:S(2)}) copy-start(f32[3,128,256]{2,1,0:T(8,128)} %blend_tiles.1) | copy-start | bytes 1179652
  77.5 9.1 %collective-permute-start = (f32[6,128,5]{2,1,0:T(8,128)S(1)}, f32[6,128,5]{2,1,0:T(8,128)S(1)}, u32[]{:S(2)}, u32[]{:S(2)}) collective-permute-start(f32[6,128,5]{2,1,0:T(8,128)S(1)} %get-tuple-element.9), channel_id=1, source_target_pairs={{0,8},{8,16},{16,24},{24,32},{32,40},{40,48},{48,56},{56,64},{64,7... | collective-permute-start | bytes 46088 | tf_op jit(solution)/shard_map/ppermute | solution.py:51
  79.5 13.0 %collective-permute-start.1 = (f32[6,128,5]{2,1,0:T(8,128)S(1)}, f32[6,128,5]{2,1,0:T(8,128)S(1)}, u32[]{:S(2)}, u32[]{:S(2)}) collective-permute-start(f32[6,128,5]{2,1,0:T(8,128)S(1)} %get-tuple-element.10), channel_id=1, source_target_pairs={{8,0},{16,8},{24,16},{32,24},{40,32},{48,40},{56,48},{64,56},{72,6... | collective-permute-start | bytes 46088 | tf_op jit(solution)/shard_map/ppermute | solution.py:52
  93.4 5.3 %collective-permute-start.2 = (f32[6,5,266]{2,1,0:T(8,128)S(1)}, f32[6,5,266]{2,1,0:T(8,128)S(1)}, u32[]{:S(2)}, u32[]{:S(2)}) collective-permute-start(f32[6,5,266]{2,1,0:T(8,128)S(1)} %get-tuple-element.4), channel_id=1, source_target_pairs={{0,1},{1,2},{2,3},{3,4},{4,5},{5,6},{6,7},{8,9},{9,10},{10,11},{11... | collective-permute-start | bytes 95768 | tf_op jit(solution)/shard_map/ppermute | solution.py:51
  96.5 5.7 %collective-permute-start.3 = (f32[6,5,266]{2,1,0:T(8,128)S(1)}, f32[6,5,266]{2,1,0:T(8,128)S(1)}, u32[]{:S(2)}, u32[]{:S(2)}) collective-permute-start(f32[6,5,266]{2,1,0:T(8,128)S(1)} %get-tuple-element.5), channel_id=1, source_target_pairs={{1,0},{2,1},{3,2},{4,3},{5,4},{6,5},{7,6},{9,8},{10,9},{11,10},{12... | collective-permute-start | bytes 95768 | tf_op jit(solution)/shard_map/ppermute | solution.py:52

commit v3 on v2

--- a/solution.py
+++ b/solution.py
@@ -39,55 +39,6 @@
 ssim_share = 0.2
 stable_one = 0.0001
 stable_two = 0.0009
-
-
-def extended(value, sides, width):
-    for axis, dim in sides:
-        size, length = (lax.axis_size(axis), value.shape[dim])
-        up = [(i, (i + 1) % size) for i in range(size - 1)]
-        down = [(j, i) for i, j in up]
-        last = lax.slice_in_dim(value, length - width, length, axis=dim)
-        first = lax.slice_in_dim(value, 0, width, axis=dim)
-        before = lax.ppermute(last, axis, up)
-        after = lax.ppermute(first, axis, down)
-        value = jnp.concatenate([before, value, after], axis=dim)
-    return value
-
-
-def window():
-    offsets = jnp.arange(11, dtype=jnp.float32) - 5.0
-    weights = jnp.exp(-offsets * offsets / 4.5)
-    return weights / jnp.sum(weights)
-
-
-def band_matrix(outputs, inputs_len, sign):
-    difference = sign * (
-        jnp.arange(inputs_len, dtype=jnp.int32)[None, :]
-        - jnp.arange(outputs, dtype=jnp.int32)[:, None]
-    )
-    offsets = jnp.arange(11, dtype=jnp.int32)
-    return jnp.sum(
-        jnp.where(difference[:, :, None] == offsets[None, None, :], window()[None, None, :], 0.0),
-        axis=2,
-    )
-
-
-def loss_from(filtered, rendered, truth):
-    mean_r, mean_t = (filtered[0:3], filtered[3:6])
-    variance_r = filtered[6:9] - mean_r * mean_r
-    variance_t = filtered[9:12] - mean_t * mean_t
-    covariance = filtered[12:15] - mean_r * mean_t
-    similarity = (
-        (2.0 * mean_r * mean_t + stable_one)
-        * (2.0 * covariance + stable_two)
-        / (
-            (mean_r * mean_r + mean_t * mean_t + stable_one)
-            * (variance_r + variance_t + stable_two)
-        )
-    )
-    return (1.0 - ssim_share) * jnp.mean(jnp.abs(rendered - truth), axis=0) + ssim_share * (
-        1.0 - jnp.mean(similarity, axis=0)
-    )
 
 
 def project_chunk(gauss):
@@ -462,6 +413,189 @@
     return first, base, code, owner
 
 
+EDGE = 8
+TAPS = 5
+
+
+def halo_kernel(rendered, truth, row_out, col_out, row_buf, col_buf, row_sem, col_sem, row_done, col_done):
+    n_gs, n_img = lax.axis_size("gs"), lax.axis_size("img")
+    g, i = lax.axis_index("gs"), lax.axis_index("img")
+    place = lambda dg, di: {"gs": lax.rem(g + n_gs + dg, n_gs), "img": lax.rem(i + n_img + di, n_img)}
+    around = [(dg, di) for dg in (-1, 0, 1) for di in (-1, 0, 1) if (dg, di) != (0, 0)]
+    barrier = pltpu.get_barrier_semaphore()
+    for dg, di in around:
+        pl.semaphore_signal(barrier, inc=1, device_id=place(dg, di), device_id_type=pl.DeviceIdType.MESH)
+
+    height, width = rendered.shape[1:]
+    for c in range(6):
+        source = (rendered, truth)[c // 3]
+        image = source[c % 3]
+        for side in range(2):
+            edge = image[0:EDGE] if side == 0 else image[height - EDGE :]
+            for half in range(2):
+                row_buf[side, c, half] = edge[:, half * LANES : (half + 1) * LANES]
+            columns = image[:, 0:LANES] if side == 0 else image[:, width - LANES :]
+            turned = jnp.transpose(columns)
+            col_buf[side, c] = turned[0:EDGE] if side == 0 else turned[LANES - EDGE :]
+
+    pl.semaphore_wait(barrier, len(around))
+    copies = []
+    for side in range(2):
+        step = -1 if side == 0 else 1
+        copies.append(
+            pltpu.make_async_remote_copy(
+                src_ref=row_buf.at[side],
+                dst_ref=row_out.at[side],
+                send_sem=row_sem.at[side],
+                recv_sem=row_done.at[side],
+                device_id=place(0, step),
+                device_id_type=pl.DeviceIdType.MESH,
+            )
+        )
+        for di in (-1, 0, 1):
+            copies.append(
+                pltpu.make_async_remote_copy(
+                    src_ref=col_buf.at[side],
+                    dst_ref=col_out.at[side * 3 + di + 1],
+                    send_sem=col_sem.at[side * 3 + di + 1],
+                    recv_sem=col_done.at[side * 3 + di + 1],
+                    device_id=place(step, di),
+                    device_id_type=pl.DeviceIdType.MESH,
+                )
+            )
+    for copy in copies:
+        copy.start()
+    for copy in copies:
+        copy.wait()
+
+
+def exchange_halos(rendered, truth):
+    vmem = pl.BlockSpec(memory_space=VMEM)
+    rows = (2, 6, 2, EDGE, LANES)
+    f32 = jnp.float32
+    return pl.pallas_call(
+        halo_kernel,
+        out_shape=(jax.ShapeDtypeStruct(rows, f32), jax.ShapeDtypeStruct((6, 6, EDGE, LANES), f32)),
+        in_specs=[vmem] * 2,
+        out_specs=(vmem, vmem),
+        scratch_shapes=[
+            VMEM(rows, f32),
+            VMEM((2, 6, EDGE, LANES), f32),
+            pltpu.SemaphoreType.DMA((2,)),
+            pltpu.SemaphoreType.DMA((6,)),
+            pltpu.SemaphoreType.DMA((2,)),
+            pltpu.SemaphoreType.DMA((6,)),
+        ],
+        compiler_params=pltpu.CompilerParams(collective_id=1, has_side_effects=True, vmem_limit_bytes=16 << 20),
+        name="exchange_halos",
+    )(rendered, truth)
+
+
+def window():
+    offsets = np.arange(11, dtype=np.float32) - 5.0
+    weights = np.exp(-offsets * offsets / np.float32(4.5))
+    return [float(w) for w in weights / np.sum(weights)]
+
+
+def loss_kernel(has, rendered, truth, rows, cols, out_ref, maps):
+    height = rendered.shape[1]
+    tall = height + 2 * EDGE
+    start = lambda q, part: (q * 3 + part) * tall
+    left, right, above, below = [has[n] > 0 for n in range(4)]
+    keep = lambda flag, value: jnp.where(flag, value, 0.0)
+    lane = lax.broadcasted_iota(jnp.int32, (EDGE, LANES), 1)
+    gap = jnp.zeros((LANES - 2 * EDGE, LANES), jnp.float32)
+    for c in range(6):
+        image = (rendered, truth)[c // 3]
+        for half in range(2):
+            base = start(c, half)
+            maps[base : base + EDGE, :] = keep(above, rows[1, c, half])
+            maps[base + EDGE : base + EDGE + height, :] = image[c % 3, :, half * LANES : (half + 1) * LANES]
+            maps[base + EDGE + height : base + tall, :] = keep(below, rows[0, c, half])
+        base = start(c, 2)
+        after = keep(right, cols[1, c])
+        before = keep(left, cols[4, c])
+        maps[base + EDGE : base + EDGE + height, :] = jnp.transpose(jnp.concatenate([after, gap, before], axis=0))
+        mixed = []
+        for flag, side in ((right, 0), (left, 3)):
+            upper = keep(flag & above, cols[side + 2, c])
+            lower = keep(flag & below, cols[side + 0, c])
+            mixed.append(jnp.where(lane < LANES // 2, lower, upper))
+        turned = jnp.transpose(jnp.concatenate([mixed[0], gap, mixed[1]], axis=0))
+        maps[base : base + EDGE, :] = turned[LANES - EDGE :]
+        maps[base + EDGE + height : base + tall, :] = turned[0:EDGE]
+
+    def products(n, carry):
+        for ch in range(3):
+            for part in range(3):
+                at = lambda q: pl.ds(pl.multiple_of(start(q + ch, part) + n * 8, 8), 8)
+                r, t = maps[at(0), :], maps[at(3), :]
+                maps[at(6), :] = r * r + t * t
+                maps[at(9), :] = r * t
+        return carry
+
+    lax.fori_loop(0, tall // 8, products, 0)
+    weights = window()
+
+    def filtered(q, n):
+        parts = []
+        for part in range(3):
+            row = lambda d: maps[pl.ds(start(q, part) + EDGE + n * 8 + d, 8), :]
+            total = weights[TAPS] * row(0)
+            for d in range(1, TAPS + 1):
+                total = total + weights[TAPS + d] * (row(d) + row(-d))
+            parts.append(total)
+        first, second, outside = parts
+        sums = [weights[TAPS] * first, weights[TAPS] * second]
+        for d in range(1, TAPS + 1):
+            ahead = [pltpu.roll(x, LANES - d, 1) for x in (first, second, outside)]
+            back = [pltpu.roll(x, d, 1) for x in (outside, first, second)]
+            inside_ahead, inside_back = lane < LANES - d, lane >= d
+            for half in range(2):
+                pair = jnp.where(inside_ahead, ahead[half], ahead[half + 1])
+                pair = pair + jnp.where(inside_back, back[half + 1], back[half])
+                sums[half] = sums[half] + weights[TAPS + d] * pair
+        return sums
+
+    def one_block(n, carry):
+        difference = [0.0, 0.0]
+        alike = [0.0, 0.0]
+        where = pl.ds(pl.multiple_of(n * 8, 8), 8)
+        for ch in range(3):
+            means_r, means_t, squares, products_rt = [filtered(q + ch, n) for q in (0, 3, 6, 9)]
+            for half in range(2):
+                mean_r, mean_t = means_r[half], means_t[half]
+                both = mean_r * mean_t
+                squared = mean_r * mean_r + mean_t * mean_t
+                above_line = (2.0 * both + stable_one) * (2.0 * (products_rt[half] - both) + stable_two)
+                below_line = (squared + stable_one) * (squares[half] - squared + stable_two)
+                alike[half] = alike[half] + above_line / below_line
+                at = pl.ds(pl.multiple_of(start(ch, half) + EDGE + n * 8, 8), 8)
+                at_t = pl.ds(pl.multiple_of(start(ch + 3, half) + EDGE + n * 8, 8), 8)
+                difference[half] = difference[half] + jnp.abs(maps[at, :] - maps[at_t, :])
+        for half in range(2):
+            out_ref[where, half * LANES : (half + 1) * LANES] = (1.0 - ssim_share) * (
+                difference[half] * (1.0 / 3.0)
+            ) + ssim_share * (1.0 - alike[half] * (1.0 / 3.0))
+        return carry
+
+    lax.fori_loop(0, height // 8, one_block, 0)
+
+
+def pixel_loss(has, rendered, truth, rows, cols):
+    vmem = pl.BlockSpec(memory_space=VMEM)
+    height, width = rendered.shape[1:]
+    return pl.pallas_call(
+        loss_kernel,
+        out_shape=jax.ShapeDtypeStruct((height, width), jnp.float32),
+        in_specs=[pl.BlockSpec(memory_space=pltpu.SMEM)] + [vmem] * 4,
+        out_specs=vmem,
+        scratch_shapes=[VMEM((12 * 3 * (height + 2 * EDGE), LANES), jnp.float32)],
+        compiler_params=pltpu.CompilerParams(vmem_limit_bytes=32 << 20),
+        name="pixel_loss",
+    )(has, rendered, truth, rows, cols)
+
+
 def on_device(gaussians, send_slots, tile_lists, truth):
     rows_here, cols_here, list_len = tile_lists.shape
     devices = send_slots.shape[1] // CAP
@@ -470,16 +604,10 @@
     arrived = lax.all_to_all(outgoing, ("gs", "img"), split_axis=1, concat_axis=1, tiled=True)
     first, base, code, owner = arrange(tile_lists)
     rendered = blend_tiles(first, base, arrived, code, owner, cols_here)
-    stacked = jnp.concatenate([rendered, truth])
-    padded = extended(stacked, (("gs", 2), ("img", 1)), 5)
-    rim_r, rim_t = (padded[0:3], padded[3:6])
-    quantities = jnp.concatenate([rim_r, rim_t, rim_r * rim_r, rim_t * rim_t, rim_r * rim_t])
-    img_height, img_width = (rendered.shape[1], rendered.shape[2])
-    band_rows = band_matrix(img_height, img_height + 10, 1)
-    band_cols = band_matrix(img_width, img_width + 10, 1).T
-    filtered = jnp.einsum("ij,cjw->ciw", band_rows, quantities, precision=lax.Precision.HIGHEST)
-    filtered = jnp.einsum("ciw,wv->civ", filtered, band_cols, precision=lax.Precision.HIGHEST)
-    return (rendered, loss_from(filtered, rendered, truth))
+    rows, cols = exchange_halos(rendered, truth)
+    g, i = lax.axis_index("gs"), lax.axis_index("img")
+    has = jnp.stack([g > 0, g < lax.axis_size("gs") - 1, i > 0, i < lax.axis_size("img") - 1]).astype(jnp.int32)
+    return (rendered, pixel_loss(has, rendered, truth, rows, cols))
 
 
 def solution(mesh):

time: 118 us -> 101 us (0.86)
  the two profiles are of different devices: /device:TPU:27 before, /device:TPU:1 now
where the time goes in v3:
time: 101 us; the launch traced here: 100 us
  Pallas kernels  60.5 us (60%)
  waiting for transfers between devices  13.2 us (13%)
  starting transfers between devices  12 us (12%)
  local copies, waits for them, and re-layouts  8.82 us (9%)
  other arithmetic  5.18 us (5%)
    pallas_call x1, Pallas kernels, blend_tiles(): pl.pallas_call(functools.partial(blend_kernel, cols_here), out_shape=jax....  26.3 us
    all_to_all x1, waiting for transfers between devices, on_device(): lax.all_to_all(outgoing, ('gs', 'img'), split_axis=1, concat_axis=1, tile...  13.2 us
    pallas_call x1, Pallas kernels, outgoing_splats(): pl.pallas_call(outgoing_kernel, out_shape=jax.ShapeDtypeStruct((SPLAT, de...  13.1 us
    all_to_all x1, starting transfers between devices, on_device(): lax.all_to_all(outgoing, ('gs', 'img'), split_axis=1, concat_axis=1, tile...  12 us
    pallas_call x1, Pallas kernels, exchange_halos(): pl.pallas_call(halo_kernel, out_shape=(jax.ShapeDtypeStruct(rows, f32), j...  11.8 us
    pallas_call x1, Pallas kernels, pixel_loss(): pl.pallas_call(loss_kernel, out_shape=jax.ShapeDtypeStruct((height, width...  9.28 us
    unnamed x13, local copies, waits for them, and re-layouts  3.83 us
    select_n x1, other arithmetic, arrange(): jnp.where(lists >= 0, slot % ROWS * 256 + slot // ROWS * LANES + source, -1)  2.61 us
  transfers between devices with their start and end apart: 1, of which 1 were waited for; matrix products, arithmetic and copies ran while one was open for 6% of the time, Pallas kernels for 0%

profile of v3, /device:TPU:1, one launch (start us, length us, event | category | flops | bytes accessed | tf_op | source)
XLA Modules:
  0.0 100.4 jit_solution(17586915658722356522)
XLA Ops:
  0.6 0.5 broadcast.103
  1.1 1.5 %reduce.4 = s32[10240]{0:T(1024)S(1)} reduce(s32[1,10240]{1,0:T(1,128)} %param.6, s32[]{:T(128)} %broadcast.103), dimensions={0}, to_apply=%param.6.reduce_sub_computation.3 | reduce | bytes 81924 | tf_op args[1]
  2.7 0.1 reshape.47
  2.8 0.0 copy-start.3
  2.8 1.3 %copy-done.3 = f32[59,5120]{1,0:T(8,128)S(1)} copy-done((f32[59,5120]{1,0:T(8,128)S(1)}, f32[59,5120]{1,0:T(8,128)}, u32[]{:S(2)}) %copy-start.3) | copy-done | bytes 1208344
  4.1 13.1 %outgoing_splats.1 = f32[9,128,128]{2,1,0:T(8,128)S(1)} custom-call(f32[59,5120]{1,0:T(8,128)S(1)} %copy-done.3, s32[128,128]{1,0:T(8,128)S(1)} %pad.8.code_ref), custom_call_target="tpu_custom_call" | custom-call | tf_op jit(solution)/shard_map/outgoing_splats/pallas_call | solution.py:138
  17.2 1.4 %copy.9 = f32[9,128,128]{2,0,1:T(8,128)} copy(f32[9,128,128]{2,1,0:T(8,128)S(1)} %outgoing_splats.1) | data formatting | bytes 1179648 | tf_op jit(solution)/shard_map/outgoing_splats/pallas_call | solution.py:138
  18.6 12.0 %all-to-all-start = ((f32[9,128,128]{2,0,1:T(8,128)}), f32[9,128,128]{2,0,1:T(8,128)}, u32[]{:S(2)}, u32[]{:S(2)}) async-start(f32[9,128,128]{2,0,1:T(8,128)} %copy.9), calls=%async_computation | async-start | bytes 2097152 | tf_op jit(solution)/shard_map/all_to_all | solution.py:604
  30.6 0.3 convert_reduce_fusion.1
  30.9 0.1 sign_compare_fusion.1
  30.9 0.3 div.33
  31.2 0.3 rem.53
  31.5 0.3 ge.10
  31.9 1.0 %ne.75 = pred[2048,32]{1,0:T(8,128)(4,1)} reshape(pred[8,16,512]{2,1,0:T(8,128)(4,1)S(1)} %sign_compare_fusion.1) | data formatting | bytes 131072 | tf_op jit(solution)/shard_map/jit(floor_divide)/ne | solution.py:406
  32.9 0.1 pad_add_fusion.1.base
  33.0 2.6 %fusion.3 = s32[2048,32]{1,0:T(8,128)S(1)} fusion(pred[2048,32]{1,0:T(8,128)(4,1)S(1)} %ge.10, s32[2048,32]{1,0:T(8,128)S(1)} %div.33, pred[2048,32]{1,0:T(8,128)(4,1)} %ne.75, s32[2048,32]{1,0:T(8,128)S(1)} %rem.53), kind=kLoop, calls=%fused_computation.9 | loop fusion | flops 1638400 | bytes 917504 | tf_op jit(solution)/shard_map/jit(_where)/select_n | solution.py:407
  35.6 0.1 add_convert_fusion.has
  35.7 0.1 sub.28
  35.7 0.1 pad.9.lists
  35.8 0.0 copy-start.4
  35.9 0.1 select_reduce_fusion
  36.0 0.1 pad_add_fusion.first
  36.0 0.4 convert_reduce_fusion
  36.4 13.2 %all-to-all-done = f32[9,128,128]{2,0,1:T(8,128)} async-done(((f32[9,128,128]{2,0,1:T(8,128)}), f32[9,128,128]{2,0,1:T(8,128)}, u32[]{:S(2)}, u32[]{:S(2)}) %all-to-all-start) | async-done | bytes 589856 | tf_op jit(solution)/shard_map/all_to_all | solution.py:604
  49.6 1.4 %copy.10.arrived = f32[9,128,128]{2,1,0:T(8,128)S(1)} copy(f32[9,128,128]{2,0,1:T(8,128)} %all-to-all-done) | data formatting | bytes 1179648 | tf_op jit(solution)/shard_map/all_to_all | solution.py:604
  51.0 0.0 copy-start.2
  51.0 26.3 %blend_tiles.1.rendered = f32[3,128,256]{2,1,0:T(8,128)} custom-call(s32[129]{0:T(256)S(1)} %pad_add_fusion.first, s32[2]{0:T(128)S(1)} %pad_add_fusion.1.base, f32[9,128,128]{2,1,0:T(8,128)S(1)} %copy.10.arrived, s32[2048,128]{1,0:T(8,128)S(1)} %pad.9.lists, s32[17,128]{1,0:T(8,128)S(1)} %bitcast.7, bf16[256,32]{1,0:T(8,128)(2,1)S(1)} %copy-done.4), custom_call_target="tpu_custom_call" | custom-call | tf_op jit(solution)/shard_map/blend_tiles/pallas_call | solution.py:369
  77.3 1.0 copy-done
  78.3 11.8 %exchange_halos.1 = (f32[2,6,2,8,128]{4,3,2,1,0:T(8,128)S(1)}, f32[6,6,8,128]{3,2,1,0:T(8,128)S(1)}) custom-call(f32[3,128,256]{2,1,0:T(8,128)S(1)} %copy-done, f32[3,128,256]{2,1,0:T(8,128)S(1)} %copy-done.2), custom_call_target="tpu_custom_call" | custom-call | tf_op jit(solution)/shard_map/exchange_halos/pallas_call | solution.py:476
  90.1 0.0 copy-start.1
  90.1 1.0 copy-done.1
  91.1 9.3 %pixel_loss.1 = f32[128,256]{1,0:T(8,128)} custom-call(s32[4]{0:T(128)S(1)} %add_convert_fusion.has, f32[3,128,256]{2,1,0:T(8,128)S(1)} %copy-done.1, f32[3,128,256]{2,1,0:T(8,128)S(1)} %copy-done.2, f32[2,6,2,8,128]{4,3,2,1,0:T(8,128)S(1)} %get-tuple-element.4.rows, f32[6,6,8,128]{3,2,1,0:T(8,128)S(1)} %get-tuple-element.5.cols), custom_call_target="tpu_custom_call" | custom-call | tf_op jit(solution)/shard_map/pixel_loss/pallas_call | solution.py:588
  (8 shorter events, 0.0 us)
Async XLA Ops:
  2.8 1.3 %copy-start.3 = (f32[59,5120]{1,0:T(8,128)S(1)}, f32[59,5120]{1,0:T(8,128)}, u32[]{:S(2)}) copy-start(f32[59,5120]{1,0:T(8,128)} %gauss_ref.1) | copy-start | bytes 3624964
  18.6 12.0 %copy-start.5 = (s32[8,16,512]{2,1,0:T(8,128)S(1)}, s32[8,16,512]{2,1,0:T(8,128)}, u32[]{:S(2)}) copy-start(s32[8,16,512]{2,1,0:T(8,128)} %param.7) | copy-start | bytes 786436
  18.6 31.0 %all-to-all-start = ((f32[9,128,128]{2,0,1:T(8,128)}), f32[9,128,128]{2,0,1:T(8,128)}, u32[]{:S(2)}, u32[]{:S(2)}) async-start(f32[9,128,128]{2,0,1:T(8,128)} %copy.9), calls=%async_computation | async-start | bytes 2097152 | tf_op jit(solution)/shard_map/all_to_all | solution.py:604
  35.8 15.2 %copy-start.4 = (bf16[256,32]{1,0:T(8,128)(2,1)S(1)}, bf16[256,32]{1,0:T(8,128)(2,1)}, u32[]{:S(2)}) copy-start(bf16[256,32]{1,0:T(8,128)(2,1)} %constant.83.mono) | copy-start | bytes 49156
  51.0 26.3 %copy-start.2 = (f32[3,128,256]{2,1,0:T(8,128)S(1)}, f32[3,128,256]{2,1,0:T(8,128)}, u32[]{:S(2)}) copy-start(f32[3,128,256]{2,1,0:T(8,128)} %truth.3) | copy-start | bytes 1179652
  77.3 1.0 copy-start
  90.1 1.0 copy-start.1

commit v4 on v3

--- a/solution.py
+++ b/solution.py
@@ -99,69 +99,6 @@
     ] + colour
 
 
-def lookup(tables, code, blocks, unroll):
-    row = lax.shift_right_arithmetic(code, 7)
-    lane = jnp.bitwise_and(code, LANES - 1)
-
-    def one(block, found):
-        hit = row == block
-        out = []
-        for p in range(SPLAT):
-            line = jnp.broadcast_to(tables[p, pl.ds(block, 1), :], code.shape)
-            taken = jnp.take_along_axis(line, lane, axis=1, mode="promise_in_bounds")
-            out.append(jnp.where(hit, taken, found[p]))
-        return tuple(out)
-
-    zero = jnp.zeros(code.shape, jnp.float32)
-    return lax.fori_loop(0, blocks, one, (zero,) * SPLAT, unroll=unroll)
-
-
-def outgoing_kernel(gauss_ref, code_ref, out_ref, table):
-    blocks = gauss_ref.shape[1] // LANES
-    for block in range(blocks):
-        rows = project_chunk(gauss_ref[:, block * LANES : (block + 1) * LANES])
-        for p in range(SPLAT):
-            table[p, block : block + 1, :] = rows[p]
-
-    def dest(i, carry):
-        where = pl.ds(pl.multiple_of(i * 8, 8), 8)
-        found = lookup(table, code_ref[where, :], blocks, 8)
-        for p in range(SPLAT):
-            out_ref[p, where, :] = found[p]
-        return carry
-
-    lax.fori_loop(0, code_ref.shape[0] // 8, dest, 0)
-
-
-def outgoing_splats(gaussians, codes):
-    devices = codes.shape[0]
-    return pl.pallas_call(
-        outgoing_kernel,
-        out_shape=jax.ShapeDtypeStruct((SPLAT, devices, LANES), jnp.float32),
-        in_specs=[pl.BlockSpec(memory_space=VMEM)] * 2,
-        out_specs=pl.BlockSpec(memory_space=VMEM),
-        scratch_shapes=[VMEM((SPLAT, gaussians.shape[1] // LANES, LANES), jnp.float32)],
-        compiler_params=pltpu.CompilerParams(vmem_limit_bytes=32 << 20),
-        name="outgoing_splats",
-    )(gaussians, codes)
-
-
-SEG = 32
-ROWS = 40
-BLOCK = 8
-COEFS = 32
-PIXELS = TILE * TILE
-CHUNK = 64
-
-
-def monomials():
-    pixel = np.arange(PIXELS)
-    x = (pixel % TILE) - 7.5
-    y = (pixel // TILE) - 7.5
-    cols = np.stack([x * x, y * y, x * y, x, y, np.ones_like(x)], axis=1)
-    return np.concatenate([cols, cols, cols, np.zeros((PIXELS, COEFS - 18))], axis=1).astype(np.float32)
-
-
 def split(value, parts):
     out = []
     for _ in range(parts):
@@ -169,6 +106,168 @@
         out.append(rounded)
         value = value - rounded.astype(jnp.float32)
     return out
+
+
+def fill_table(table, halves):
+    for half, ref in enumerate(halves):
+        for part, value in enumerate(split(ref[...], 3)):
+            table[:, part * 256 + half * LANES : part * 256 + (half + 1) * LANES] = value
+
+
+def lookup(table, code):
+    rows = table.shape[0] // SPLAT
+    column = lax.broadcasted_iota(jnp.int32, (256, 256), 0)
+    col = jnp.bitwise_and(code, 255)
+    row = lax.shift_right_arithmetic(code, 8)
+    hot = jnp.where(column == col, 1.0, 0.0).astype(jnp.bfloat16)
+    found = jnp.dot(table[...], jnp.concatenate([hot, hot, hot], axis=0), preferred_element_type=jnp.float32)
+    picked = jnp.zeros((8, 256), jnp.float32)
+    rows8 = jnp.broadcast_to(row, (8, 256))
+    for r in range(rows):
+        picked = jnp.where(rows8 == r, found[r * 8 : (r + 1) * 8], picked)
+    table_row = lax.broadcasted_iota(jnp.int32, (rows, 256), 0)
+    ninth = jnp.sum(jnp.where(table_row == row, found[8 * rows :], 0.0), axis=0, keepdims=True)
+    return picked, ninth
+
+
+def outgoing_kernel(gauss_ref, code_ref, out_ref, table_a, table_b, table, eight, ninth):
+    blocks = gauss_ref.shape[1] // LANES
+    rows = blocks // 2
+    for block in range(blocks):
+        splat = project_chunk(gauss_ref[:, block * LANES : (block + 1) * LANES])
+        ref = (table_a, table_b)[block // rows]
+        r = block % rows
+        ref[r * 8 : r * 8 + 8, :] = jnp.concatenate(splat[:8], axis=0)
+        ref[8 * rows + r : 8 * rows + r + 1, :] = splat[8]
+    fill_table(table, (table_a, table_b))
+
+    def eight_slots(i, carry):
+        where = pl.multiple_of(i * 8, 8)
+        codes = code_ref[pl.ds(where, 8), :]
+        found = [
+            lookup(table, jnp.concatenate([codes[2 * j : 2 * j + 1], codes[2 * j + 1 : 2 * j + 2]], axis=1))
+            for j in range(4)
+        ]
+        for j, (first, last) in enumerate(found):
+            for e in range(2):
+                lanes = slice(e * LANES, (e + 1) * LANES)
+                eight[pl.ds(where * 8 + (2 * j + e) * 8, 8), :] = first[:, lanes]
+                ninth[pl.ds(where + 2 * j + e, 1), :] = last[:, lanes]
+        return carry
+
+    eight[CAP * 8 :, :] = jnp.zeros((eight.shape[0] - CAP * 8, LANES), jnp.float32)
+    ninth[CAP:, :] = jnp.zeros((LANES - CAP, LANES), jnp.float32)
+    lax.fori_loop(0, CAP // 8, eight_slots, 0)
+    for p in range(SPLAT):
+        out_ref[p] = jnp.transpose(eight[pl.ds(p, LANES, stride=8), :] if p < 8 else ninth[...])
+
+
+def outgoing_splats(gaussians, codes):
+    devices = codes.shape[1]
+    rows = gaussians.shape[1] // (2 * LANES)
+    f32 = jnp.float32
+    return pl.pallas_call(
+        outgoing_kernel,
+        out_shape=jax.ShapeDtypeStruct((SPLAT, devices, LANES), f32),
+        in_specs=[pl.BlockSpec(memory_space=VMEM)] * 2,
+        out_specs=pl.BlockSpec(memory_space=VMEM),
+        scratch_shapes=[
+            VMEM((SPLAT * rows, LANES), f32),
+            VMEM((SPLAT * rows, LANES), f32),
+            VMEM((SPLAT * rows, 768), jnp.bfloat16),
+            VMEM((8 * LANES, LANES), f32),
+            VMEM((LANES, LANES), f32),
+        ],
+        compiler_params=pltpu.CompilerParams(vmem_limit_bytes=32 << 20),
+        name="outgoing_splats",
+    )(gaussians, codes)
+
+
+def deal_kernel(out_ref, in_ref, held, send_1, done_1, send_2, done_2, local_sem):
+    n_gs, n_img = lax.axis_size("gs"), lax.axis_size("img")
+    g, i = lax.axis_index("gs"), lax.axis_index("img")
+    mesh_id = pl.DeviceIdType.MESH
+    barrier = pltpu.get_barrier_semaphore()
+    other_g = [lax.rem(g + d, n_gs) for d in range(1, n_gs)]
+    other_i = [lax.rem(i + d, n_img) for d in range(1, n_img)]
+    for to in other_g:
+        pl.semaphore_signal(barrier, inc=1, device_id={"gs": to, "img": i}, device_id_type=mesh_id)
+    for to in other_i:
+        pl.semaphore_signal(barrier, inc=1, device_id={"gs": g, "img": to}, device_id_type=mesh_id)
+    pl.semaphore_wait(barrier, n_gs + n_img - 2)
+    first = [
+        pltpu.make_async_remote_copy(
+            src_ref=out_ref.at[:, to],
+            dst_ref=held.at[:, g],
+            send_sem=send_1.at[d],
+            recv_sem=done_1.at[d],
+            device_id={"gs": to, "img": i},
+            device_id_type=mesh_id,
+        )
+        for d, to in enumerate(other_g)
+    ]
+    for copy in first:
+        copy.start()
+    own = pltpu.make_async_copy(out_ref.at[:, g], held.at[:, g], local_sem.at[0])
+    own.start()
+    own.wait()
+    for copy in first:
+        copy.wait_recv()
+    second = [
+        pltpu.make_async_remote_copy(
+            src_ref=held.at[:, :, to],
+            dst_ref=in_ref.at[:, :, i],
+            send_sem=send_2.at[d],
+            recv_sem=done_2.at[d],
+            device_id={"gs": g, "img": to},
+            device_id_type=mesh_id,
+        )
+        for d, to in enumerate(other_i)
+    ]
+    for copy in second:
+        copy.start()
+    own = pltpu.make_async_copy(held.at[:, :, i], in_ref.at[:, :, i], local_sem.at[1])
+    own.start()
+    own.wait()
+    for copy in first:
+        copy.wait_send()
+    for copy in second:
+        copy.wait()
+
+
+def deal(outgoing):
+    n_gs, n_img = lax.axis_size("gs"), lax.axis_size("img")
+    shape = (SPLAT, n_gs, n_img, LANES)
+    vmem = pl.BlockSpec(memory_space=VMEM)
+    dma = pltpu.SemaphoreType.DMA
+    arrived = pl.pallas_call(
+        deal_kernel,
+        out_shape=jax.ShapeDtypeStruct(shape, jnp.float32),
+        in_specs=[vmem],
+        out_specs=vmem,
+        scratch_shapes=[
+            VMEM(shape, jnp.float32), dma((n_gs - 1,)), dma((n_gs - 1,)), dma((n_img - 1,)), dma((n_img - 1,)), dma((2,))
+        ],
+        compiler_params=pltpu.CompilerParams(collective_id=2, has_side_effects=True, vmem_limit_bytes=16 << 20),
+        name="deal_splats",
+    )(outgoing.reshape(shape))
+    return arrived.reshape(outgoing.shape)
+
+
+SEG = 32
+ROWS = 40
+BLOCK = 8
+COEFS = 32
+PIXELS = TILE * TILE
+CHUNK = 64
+
+
+def monomials():
+    pixel = np.arange(PIXELS)
+    x = (pixel % TILE) - 7.5
+    y = (pixel // TILE) - 7.5
+    cols = np.stack([x * x, y * y, x * y, x, y, np.ones_like(x)], axis=1)
+    return np.concatenate([cols, cols, cols, np.zeros((PIXELS, COEFS - 18))], axis=1).astype(np.float32)
 
 
 def lane_pick(value, index, axis):
@@ -191,9 +290,7 @@
                 ref[pl.ds(p, ROWS, stride=8), :] = value
             else:
                 ref[8 * ROWS : 9 * ROWS, :] = value
-    for half, ref in enumerate((table_a, table_b)):
-        for part, value in enumerate(split(ref[...], 3)):
-            table[:, part * 256 + half * LANES : part * 256 + (half + 1) * LANES] = value
+    fill_table(table, (table_a, table_b))
 
     packed[...] = jnp.full(packed.shape, -1, jnp.int32)
     for t in range(tiles):
@@ -209,23 +306,10 @@
     carry_ref[...] = jnp.ones_like(carry_ref)
     carry_owner[...] = jnp.full(carry_owner.shape, -1, jnp.int32)
 
-    column = lax.broadcasted_iota(jnp.int32, (256, 256), 0)
-    table_row = lax.broadcasted_iota(jnp.int32, (ROWS, 256), 0)
-
-    def lookup(block, j):
-        slot = (block % 3) * 72
+    def look(block, j):
         where = block * BLOCK + 2 * j
         code = jnp.concatenate([codes[pl.ds(where, 1), :], codes[pl.ds(where + 1, 1), :]], axis=1)
-        col = jnp.bitwise_and(code, 255)
-        row = lax.shift_right_arithmetic(code, 8)
-        hot = jnp.where(column == col, 1.0, 0.0).astype(jnp.bfloat16)
-        found = jnp.dot(table[...], jnp.concatenate([hot, hot, hot], axis=0), preferred_element_type=jnp.float32)
-        picked = jnp.zeros((8, 256), jnp.float32)
-        rows8 = jnp.broadcast_to(row, (8, 256))
-        for r in range(ROWS):
-            picked = jnp.where(rows8 == r, found[r * 8 : (r + 1) * 8], picked)
-        ninth = jnp.sum(jnp.where(table_row == row, found[8 * ROWS :], 0.0), axis=0, keepdims=True)
-        return slot, picked, ninth
+        return ((block % 3) * 72,) + lookup(table, code)
 
     def keep(j, slot, picked, ninth):
         for e in range(2):
@@ -311,7 +395,7 @@
     steps = BLOCK // 2
 
     def look_ahead(block):
-        for j, found in enumerate([lookup(block, j) for j in range(steps)]):
+        for j, found in enumerate([look(block, j) for j in range(steps)]):
             keep(j, *found)
         expand(block)
 
@@ -329,7 +413,7 @@
                 block = g * per_group + 2 * i + which
                 now, later = ((power_a, power_b), (power_b, power_a))[which]
 
-                found = [lookup(block + 2, j) for j in range(steps)]
+                found = [look(block + 2, j) for j in range(steps)]
                 for j in range(steps):
                     later[j] = exponents(j)
                 for j in range(steps):
@@ -599,9 +683,10 @@
 def on_device(gaussians, send_slots, tile_lists, truth):
     rows_here, cols_here, list_len = tile_lists.shape
     devices = send_slots.shape[1] // CAP
-    codes = jnp.pad(send_slots.reshape(devices, CAP), ((0, 0), (0, LANES - CAP)))
-    outgoing = outgoing_splats(gaussians, codes)
-    arrived = lax.all_to_all(outgoing, ("gs", "img"), split_axis=1, concat_axis=1, tiled=True)
+    half = gaussians.shape[1] // 2
+    picks = send_slots.reshape(devices, CAP).T
+    codes = picks % half // LANES * 256 + picks // half * LANES + picks % LANES
+    arrived = deal(outgoing_splats(gaussians, codes))
     first, base, code, owner = arrange(tile_lists)
     rendered = blend_tiles(first, base, arrived, code, owner, cols_here)
     rows, cols = exchange_halos(rendered, truth)

time: 101 us -> 89.7 us (0.89)
  the two profiles are of different devices: /device:TPU:1 before, /device:TPU:0 now
where the time goes in v4:
time: 89.7 us; the launch traced here: 89.4 us
  Pallas kernels  79.7 us (89%)
  other arithmetic  4.5 us (5%)
  local copies, waits for them, and re-layouts  4.39 us (5%)
    pallas_call x1, Pallas kernels, blend_tiles(): pl.pallas_call(functools.partial(blend_kernel, cols_here), out_shape=jax....  26.3 us
    pallas_call x1, Pallas kernels, deal(): pl.pallas_call(deal_kernel, out_shape=jax.ShapeDtypeStruct(shape, jnp.flo...  24.3 us
    pallas_call x1, Pallas kernels, exchange_halos(): pl.pallas_call(halo_kernel, out_shape=(jax.ShapeDtypeStruct(rows, f32), j...  13 us
    pallas_call x1, Pallas kernels, pixel_loss(): pl.pallas_call(loss_kernel, out_shape=jax.ShapeDtypeStruct((height, width...  9.28 us
    pallas_call x1, Pallas kernels, outgoing_splats(): pl.pallas_call(outgoing_kernel, out_shape=jax.ShapeDtypeStruct((SPLAT, de...  6.81 us
    unnamed x15, local copies, waits for them, and re-layouts  2.85 us

profile of v4, /device:TPU:0, one launch (start us, length us, event | category | flops | bytes accessed | tf_op | source)
XLA Modules:
  0.0 89.4 jit_solution(14893576659951200209)
XLA Ops:
  0.6 1.2 %convert_reduce_fusion.1 = (s32[8,16]{1,0:T(8,128)S(1)}, pred[8,16,512]{2,1,0:T(8,128)(4,1)S(1)}, s32[8,16,512]{2,1,0:T(8,128)S(1)}, s32[8,16,512]{2,1,0:T(8,128)S(1)}) fusion(s32[8,16,512]{2,1,0:T(8,128)} %param.7), kind=kLoop, calls=%fused_computation.15 | loop fusion | flops 327552 | bytes 852480 | tf_op jit(solution)/shard_map/reduce_sum | solution.py:483
  1.8 0.3 div.54
  2.1 0.0 copy-start.5
  2.1 0.3 rem.113
  2.4 0.3 ge.10
  2.8 0.3 copy-done.5
  3.1 0.1 sign_compare_fusion.1
  3.1 0.3 ne.114
  3.5 1.7 %fusion.3 = s32[2048,32]{1,0:T(8,128)S(1)} fusion(pred[2048,32]{1,0:T(8,128)(4,1)S(1)} %ge.10, s32[2048,32]{1,0:T(8,128)S(1)} %div.54, pred[2048,32]{1,0:T(8,128)(4,1)S(1)} %ne.114, s32[2048,32]{1,0:T(8,128)S(1)} %rem.113), kind=kLoop, calls=%fused_computation.9 | loop fusion | flops 1638400 | bytes 917504 | tf_op jit(solution)/shard_map/jit(_where)/select_n | solution.py:491
  5.2 0.0 copy-start.6
  5.2 0.0 copy-start.3
  5.2 0.1 pad.4.lists
  5.3 0.1 pad_add_fusion.1.base
  5.3 0.1 sub.38
  5.4 0.1 select_reduce_fusion
  5.6 0.4 convert_reduce_fusion
  5.9 0.1 pad_add_fusion.first
  6.0 0.5 broadcast.116
  6.5 0.7 reduce.4
  7.3 0.1 reshape.53
  7.4 0.1 copy.8
  7.5 0.1 fusion.9.code_ref
  7.6 0.0 copy-start.4
  7.6 6.8 %outgoing_splats.1 = f32[9,128,128]{2,1,0:T(8,128)S(1)} custom-call(f32[59,5120]{1,0:T(8,128)S(1)} %copy-done.3, s32[80,128]{1,0:T(8,128)S(1)} %fusion.9.code_ref), custom_call_target="tpu_custom_call" | custom-call | tf_op jit(solution)/shard_map/outgoing_splats/pallas_call | solution.py:169
  14.4 24.3 %deal_splats.1 = f32[9,16,8,128]{3,2,1,0:T(8,128)S(1)} custom-call(f32[9,16,8,128]{3,2,1,0:T(8,128)S(1)} %bitcast.35), custom_call_target="tpu_custom_call" | custom-call | tf_op jit(solution)/shard_map/deal_splats/pallas_call | solution.py:243
  38.7 0.0 copy-start.2
  38.7 26.3 %blend_tiles.1.rendered = f32[3,128,256]{2,1,0:T(8,128)} custom-call(s32[129]{0:T(256)S(1)} %pad_add_fusion.first, s32[2]{0:T(128)S(1)} %pad_add_fusion.1.base, f32[9,128,128]{2,1,0:T(8,128)S(1)} %bitcast.34, s32[2048,128]{1,0:T(8,128)S(1)} %pad.4.lists, s32[17,128]{1,0:T(8,128)S(1)} %bitcast.36, bf16[256,32]{1,0:T(8,128)(2,1)S(1)} %copy-done.4), custom_call_target="tpu_custom_call" | custom-call | tf_op jit(solution)/shard_map/blend_tiles/pallas_call | solution.py:453
  65.1 1.0 %copy-done = f32[3,128,256]{2,1,0:T(8,128)S(1)} copy-done((f32[3,128,256]{2,1,0:T(8,128)S(1)}, f32[3,128,256]{2,1,0:T(8,128)}, u32[]{:S(2)}) %copy-start) | copy-done | bytes 393240
  66.0 13.0 %exchange_halos.1 = (f32[2,6,2,8,128]{4,3,2,1,0:T(8,128)S(1)}, f32[6,6,8,128]{3,2,1,0:T(8,128)S(1)}) custom-call(f32[3,128,256]{2,1,0:T(8,128)S(1)} %copy-done, f32[3,128,256]{2,1,0:T(8,128)S(1)} %copy-done.2), custom_call_target="tpu_custom_call" | custom-call | tf_op jit(solution)/shard_map/exchange_halos/pallas_call | solution.py:560
  79.0 0.1 add_convert_fusion.has
  79.1 1.0 %copy-done.1 = f32[3,128,256]{2,1,0:T(8,128)S(1)} copy-done((f32[3,128,256]{2,1,0:T(8,128)S(1)}, f32[3,128,256]{2,1,0:T(8,128)}, u32[]{:S(2)}) %copy-start.1) | copy-done | bytes 393240
  80.1 9.3 %pixel_loss.1 = f32[128,256]{1,0:T(8,128)} custom-call(s32[4]{0:T(128)S(1)} %add_convert_fusion.has, f32[3,128,256]{2,1,0:T(8,128)S(1)} %copy-done.1, f32[3,128,256]{2,1,0:T(8,128)S(1)} %copy-done.2, f32[2,6,2,8,128]{4,3,2,1,0:T(8,128)S(1)} %get-tuple-element.4.rows, f32[6,6,8,128]{3,2,1,0:T(8,128)S(1)} %get-tuple-element.5.cols), custom_call_target="tpu_custom_call" | custom-call | tf_op jit(solution)/shard_map/pixel_loss/pallas_call | solution.py:672
  (8 shorter events, 0.0 us)
Async XLA Ops:
  2.1 1.0 %copy-start.5 = (s32[8,16,512]{2,1,0:T(8,128)S(1)}, s32[8,16,512]{2,1,0:T(8,128)}, u32[]{:S(2)}) copy-start(s32[8,16,512]{2,1,0:T(8,128)} %param.7) | copy-start | bytes 786436
  5.2 1.4 %copy-start.6 = (s32[1,10240]{1,0:T(1,128)S(1)}, s32[1,10240]{1,0:T(1,128)}, u32[]{:S(2)}) copy-start(s32[1,10240]{1,0:T(1,128)} %param.6) | copy-start | bytes 122884
  5.2 2.4 %copy-start.3 = (f32[59,5120]{1,0:T(8,128)S(1)}, f32[59,5120]{1,0:T(8,128)}, u32[]{:S(2)}) copy-start(f32[59,5120]{1,0:T(8,128)} %gauss_ref.1) | copy-start | bytes 3624964
  7.6 31.1 %copy-start.4 = (bf16[256,32]{1,0:T(8,128)(2,1)S(1)}, bf16[256,32]{1,0:T(8,128)(2,1)}, u32[]{:S(2)}) copy-start(bf16[256,32]{1,0:T(8,128)(2,1)} %constant.117.mono) | copy-start | bytes 49156
  38.7 26.4 %copy-start.2 = (f32[3,128,256]{2,1,0:T(8,128)S(1)}, f32[3,128,256]{2,1,0:T(8,128)}, u32[]{:S(2)}) copy-start(f32[3,128,256]{2,1,0:T(8,128)} %truth.3) | copy-start | bytes 1179652
  65.1 1.0 %copy-start = (f32[3,128,256]{2,1,0:T(8,128)S(1)}, f32[3,128,256]{2,1,0:T(8,128)}, u32[]{:S(2)}) copy-start(f32[3,128,256]{2,1,0:T(8,128)} %blend_tiles.1.rendered) | copy-start | bytes 1179652
  79.1 1.0 %copy-start.1 = (f32[3,128,256]{2,1,0:T(8,128)S(1)}, f32[3,128,256]{2,1,0:T(8,128)}, u32[]{:S(2)}) copy-start(f32[3,128,256]{2,1,0:T(8,128)} %blend_tiles.1.rendered) | copy-start | bytes 1179652

commit v5 on v4

--- a/solution.py
+++ b/solution.py
@@ -13,6 +13,7 @@
 LANES = 128
 CAP = 80
 SPLAT = 9
+ROWS = CAP // 2
 LOG2E = 1.0 / math.log(2.0)
 VMEM = pltpu.VMEM
 
@@ -130,7 +131,7 @@
     return picked, ninth
 
 
-def outgoing_kernel(gauss_ref, code_ref, out_ref, table_a, table_b, table, eight, ninth):
+def outgoing_kernel(gauss_ref, code_ref, out_ref, table_a, table_b, table, eight):
     blocks = gauss_ref.shape[1] // LANES
     rows = blocks // 2
     for block in range(blocks):
@@ -152,14 +153,14 @@
             for e in range(2):
                 lanes = slice(e * LANES, (e + 1) * LANES)
                 eight[pl.ds(where * 8 + (2 * j + e) * 8, 8), :] = first[:, lanes]
-                ninth[pl.ds(where + 2 * j + e, 1), :] = last[:, lanes]
+                k = where + 2 * j + e
+                eight[pl.ds((CAP + k % ROWS) * 8 + k // ROWS, 1), :] = last[:, lanes]
         return carry
 
     eight[CAP * 8 :, :] = jnp.zeros((eight.shape[0] - CAP * 8, LANES), jnp.float32)
-    ninth[CAP:, :] = jnp.zeros((LANES - CAP, LANES), jnp.float32)
     lax.fori_loop(0, CAP // 8, eight_slots, 0)
-    for p in range(SPLAT):
-        out_ref[p] = jnp.transpose(eight[pl.ds(p, LANES, stride=8), :] if p < 8 else ninth[...])
+    for p in range(8):
+        out_ref[pl.ds(p, LANES, stride=8), :] = jnp.transpose(eight[pl.ds(p, LANES, stride=8), :])
 
 
 def outgoing_splats(gaussians, codes):
@@ -168,7 +169,7 @@
     f32 = jnp.float32
     return pl.pallas_call(
         outgoing_kernel,
-        out_shape=jax.ShapeDtypeStruct((SPLAT, devices, LANES), f32),
+        out_shape=jax.ShapeDtypeStruct((devices * 8, LANES), f32),
         in_specs=[pl.BlockSpec(memory_space=VMEM)] * 2,
         out_specs=pl.BlockSpec(memory_space=VMEM),
         scratch_shapes=[
@@ -176,78 +177,57 @@
             VMEM((SPLAT * rows, LANES), f32),
             VMEM((SPLAT * rows, 768), jnp.bfloat16),
             VMEM((8 * LANES, LANES), f32),
-            VMEM((LANES, LANES), f32),
         ],
         compiler_params=pltpu.CompilerParams(vmem_limit_bytes=32 << 20),
         name="outgoing_splats",
     )(gaussians, codes)
 
 
-def deal_kernel(out_ref, in_ref, held, send_1, done_1, send_2, done_2, local_sem):
+def deal_kernel(out_ref, in_ref, send_sem, done_sem, local_sem):
     n_gs, n_img = lax.axis_size("gs"), lax.axis_size("img")
-    g, i = lax.axis_index("gs"), lax.axis_index("img")
-    mesh_id = pl.DeviceIdType.MESH
+    devices = n_gs * n_img
+    me = lax.axis_index("gs") * n_img + lax.axis_index("img")
+    place = lambda d: {"gs": lax.div(d, n_img), "img": lax.rem(d, n_img)}
     barrier = pltpu.get_barrier_semaphore()
-    other_g = [lax.rem(g + d, n_gs) for d in range(1, n_gs)]
-    other_i = [lax.rem(i + d, n_img) for d in range(1, n_img)]
-    for to in other_g:
-        pl.semaphore_signal(barrier, inc=1, device_id={"gs": to, "img": i}, device_id_type=mesh_id)
-    for to in other_i:
-        pl.semaphore_signal(barrier, inc=1, device_id={"gs": g, "img": to}, device_id_type=mesh_id)
-    pl.semaphore_wait(barrier, n_gs + n_img - 2)
-    first = [
+
+    def greet(d, carry):
+        to = lax.rem(me + d, devices)
+        pl.semaphore_signal(barrier, inc=1, device_id=place(to), device_id_type=pl.DeviceIdType.MESH)
+        return carry
+
+    def send(d, carry):
+        to = lax.rem(me + d, devices)
         pltpu.make_async_remote_copy(
-            src_ref=out_ref.at[:, to],
-            dst_ref=held.at[:, g],
-            send_sem=send_1.at[d],
-            recv_sem=done_1.at[d],
-            device_id={"gs": to, "img": i},
-            device_id_type=mesh_id,
-        )
-        for d, to in enumerate(other_g)
-    ]
-    for copy in first:
-        copy.start()
-    own = pltpu.make_async_copy(out_ref.at[:, g], held.at[:, g], local_sem.at[0])
+            src_ref=out_ref.at[to],
+            dst_ref=in_ref.at[me],
+            send_sem=send_sem,
+            recv_sem=done_sem,
+            device_id=place(to),
+            device_id_type=pl.DeviceIdType.MESH,
+        ).start()
+        return carry
+
+    lax.fori_loop(1, devices, greet, 0)
+    own = pltpu.make_async_copy(out_ref.at[me], in_ref.at[me], local_sem)
     own.start()
     own.wait()
-    for copy in first:
-        copy.wait_recv()
-    second = [
-        pltpu.make_async_remote_copy(
-            src_ref=held.at[:, :, to],
-            dst_ref=in_ref.at[:, :, i],
-            send_sem=send_2.at[d],
-            recv_sem=done_2.at[d],
-            device_id={"gs": g, "img": to},
-            device_id_type=mesh_id,
-        )
-        for d, to in enumerate(other_i)
-    ]
-    for copy in second:
-        copy.start()
-    own = pltpu.make_async_copy(held.at[:, :, i], in_ref.at[:, :, i], local_sem.at[1])
-    own.start()
-    own.wait()
-    for copy in first:
-        copy.wait_send()
-    for copy in second:
-        copy.wait()
+    pl.semaphore_wait(barrier, devices - 1)
+    lax.fori_loop(1, devices, send, 0)
+    others = pl.ds(0, devices - 1)
+    pltpu.make_async_copy(out_ref.at[others], out_ref.at[others], send_sem).wait()
+    pltpu.make_async_copy(in_ref.at[others], in_ref.at[others], done_sem).wait()
 
 
 def deal(outgoing):
-    n_gs, n_img = lax.axis_size("gs"), lax.axis_size("img")
-    shape = (SPLAT, n_gs, n_img, LANES)
+    devices = lax.axis_size("gs") * lax.axis_size("img")
+    shape = (devices, 8, LANES)
     vmem = pl.BlockSpec(memory_space=VMEM)
-    dma = pltpu.SemaphoreType.DMA
     arrived = pl.pallas_call(
         deal_kernel,
         out_shape=jax.ShapeDtypeStruct(shape, jnp.float32),
         in_specs=[vmem],
         out_specs=vmem,
-        scratch_shapes=[
-            VMEM(shape, jnp.float32), dma((n_gs - 1,)), dma((n_gs - 1,)), dma((n_img - 1,)), dma((n_img - 1,)), dma((2,))
-        ],
+        scratch_shapes=[pltpu.SemaphoreType.DMA] * 3,
         compiler_params=pltpu.CompilerParams(collective_id=2, has_side_effects=True, vmem_limit_bytes=16 << 20),
         name="deal_splats",
     )(outgoing.reshape(shape))
@@ -255,7 +235,6 @@
 
 
 SEG = 32
-ROWS = 40
 BLOCK = 8
 COEFS = 32
 PIXELS = TILE * TILE
@@ -282,14 +261,12 @@
     groups = (first[tiles] + LANES - 1) // LANES
     per_group = SEG // BLOCK
 
-    for p in range(SPLAT):
-        flat = jnp.transpose(arrived[p])
+    for p in range(8):
+        flat = jnp.transpose(arrived[pl.ds(p, LANES, stride=8), :])
         for half, ref in enumerate((table_a, table_b)):
-            value = flat[half * ROWS : (half + 1) * ROWS]
-            if p < 8:
-                ref[pl.ds(p, ROWS, stride=8), :] = value
-            else:
-                ref[8 * ROWS : 9 * ROWS, :] = value
+            ref[pl.ds(p, ROWS, stride=8), :] = flat[half * ROWS : (half + 1) * ROWS]
+            if p == half:
+                ref[8 * ROWS :, :] = flat[CAP : CAP + ROWS]
     fill_table(table, (table_a, table_b))
 
     packed[...] = jnp.full(packed.shape, -1, jnp.int32)

time: 89.7 us -> 83.9 us (0.935)
  Pallas kernels: 79.7 us -> 74 us
    pallas_call x1, Pallas kernels: 24.3 us -> 18.5 us  [deal(): pl.pallas_call(deal_kernel, out_shape=jax.ShapeDtypeStruct(shape, jnp.flo...]
where the time goes in v5:
time: 83.9 us; the launch traced here: 83.7 us
  Pallas kernels  74 us (88%)
  other arithmetic  4.5 us (5%)
  local copies, waits for them, and re-layouts  4.39 us (5%)
    pallas_call x1, Pallas kernels, blend_tiles(): pl.pallas_call(functools.partial(blend_kernel, cols_here), out_shape=jax....  26.3 us
    pallas_call x1, Pallas kernels, deal(): pl.pallas_call(deal_kernel, out_shape=jax.ShapeDtypeStruct(shape, jnp.flo...  18.5 us
    pallas_call x1, Pallas kernels, exchange_halos(): pl.pallas_call(halo_kernel, out_shape=(jax.ShapeDtypeStruct(rows, f32), j...  13.1 us
    pallas_call x1, Pallas kernels, pixel_loss(): pl.pallas_call(loss_kernel, out_shape=jax.ShapeDtypeStruct((height, width...  9.28 us
    pallas_call x1, Pallas kernels, outgoing_splats(): pl.pallas_call(outgoing_kernel, out_shape=jax.ShapeDtypeStruct((devices *...  6.79 us
    unnamed x15, local copies, waits for them, and re-layouts  2.85 us

profile of v5, /device:TPU:0, one launch (start us, length us, event | category | flops | bytes accessed | tf_op | source)
XLA Modules:
  0.0 83.7 jit_solution(11921437508241366540)
XLA Ops:
  0.6 1.2 %convert_reduce_fusion.1 = (s32[8,16]{1,0:T(8,128)S(1)}, pred[8,16,512]{2,1,0:T(8,128)(4,1)S(1)}, s32[8,16,512]{2,1,0:T(8,128)S(1)}, s32[8,16,512]{2,1,0:T(8,128)S(1)}) fusion(s32[8,16,512]{2,1,0:T(8,128)} %param.7), kind=kLoop, calls=%fused_computation.15 | loop fusion | flops 327552 | bytes 852480 | tf_op jit(solution)/shard_map/reduce_sum | solution.py:460
  1.8 0.3 div.54
  2.1 0.0 copy-start.5
  2.1 0.3 rem.113
  2.4 0.3 ge.10
  2.8 0.3 copy-done.5
  3.1 0.1 sign_compare_fusion.1
  3.1 0.3 ne.114
  3.5 1.7 %fusion.3 = s32[2048,32]{1,0:T(8,128)S(1)} fusion(pred[2048,32]{1,0:T(8,128)(4,1)S(1)} %ge.10, s32[2048,32]{1,0:T(8,128)S(1)} %div.54, pred[2048,32]{1,0:T(8,128)(4,1)S(1)} %ne.114, s32[2048,32]{1,0:T(8,128)S(1)} %rem.113), kind=kLoop, calls=%fused_computation.9 | loop fusion | flops 1638400 | bytes 917504 | tf_op jit(solution)/shard_map/jit(_where)/select_n | solution.py:468
  5.2 0.0 copy-start.6
  5.2 0.0 copy-start.3
  5.2 0.1 pad.4.lists
  5.3 0.1 pad_add_fusion.1.base
  5.3 0.1 sub.38
  5.4 0.1 select_reduce_fusion
  5.6 0.4 convert_reduce_fusion
  5.9 0.1 pad_add_fusion.first
  6.0 0.5 broadcast.116
  6.5 0.7 reduce.4
  7.3 0.1 reshape.53
  7.4 0.1 copy.8
  7.5 0.1 fusion.9.code_ref
  7.6 0.0 copy-start.4
  7.6 6.8 %outgoing_splats.1 = f32[1024,128]{1,0:T(8,128)S(1)} custom-call(f32[59,5120]{1,0:T(8,128)S(1)} %copy-done.3, s32[80,128]{1,0:T(8,128)S(1)} %fusion.9.code_ref), custom_call_target="tpu_custom_call" | custom-call | tf_op jit(solution)/shard_map/outgoing_splats/pallas_call | solution.py:170
  14.4 18.5 %deal_splats.1 = f32[128,8,128]{2,1,0:T(8,128)S(1)} custom-call(f32[128,8,128]{2,1,0:T(8,128)S(1)} %bitcast.34), custom_call_target="tpu_custom_call" | custom-call | tf_op jit(solution)/shard_map/deal_splats/pallas_call | solution.py:225
  32.9 0.0 copy-start.2
  32.9 26.3 %blend_tiles.1.rendered = f32[3,128,256]{2,1,0:T(8,128)} custom-call(s32[129]{0:T(256)S(1)} %pad_add_fusion.first, s32[2]{0:T(128)S(1)} %pad_add_fusion.1.base, f32[1024,128]{1,0:T(8,128)S(1)} %bitcast.35, s32[2048,128]{1,0:T(8,128)S(1)} %pad.4.lists, s32[17,128]{1,0:T(8,128)S(1)} %bitcast.36, bf16[256,32]{1,0:T(8,128)(2,1)S(1)} %copy-done.4), custom_call_target="tpu_custom_call" | custom-call | tf_op jit(solution)/shard_map/blend_tiles/pallas_call | solution.py:430
  59.2 1.0 %copy-done = f32[3,128,256]{2,1,0:T(8,128)S(1)} copy-done((f32[3,128,256]{2,1,0:T(8,128)S(1)}, f32[3,128,256]{2,1,0:T(8,128)}, u32[]{:S(2)}) %copy-start) | copy-done | bytes 393240
  60.2 13.1 %exchange_halos.1 = (f32[2,6,2,8,128]{4,3,2,1,0:T(8,128)S(1)}, f32[6,6,8,128]{3,2,1,0:T(8,128)S(1)}) custom-call(f32[3,128,256]{2,1,0:T(8,128)S(1)} %copy-done, f32[3,128,256]{2,1,0:T(8,128)S(1)} %copy-done.2), custom_call_target="tpu_custom_call" | custom-call | tf_op jit(solution)/shard_map/exchange_halos/pallas_call | solution.py:537
  73.3 0.1 add_convert_fusion.has
  73.4 1.0 %copy-done.1 = f32[3,128,256]{2,1,0:T(8,128)S(1)} copy-done((f32[3,128,256]{2,1,0:T(8,128)S(1)}, f32[3,128,256]{2,1,0:T(8,128)}, u32[]{:S(2)}) %copy-start.1) | copy-done | bytes 393240
  74.4 9.3 %pixel_loss.1 = f32[128,256]{1,0:T(8,128)} custom-call(s32[4]{0:T(128)S(1)} %add_convert_fusion.has, f32[3,128,256]{2,1,0:T(8,128)S(1)} %copy-done.1, f32[3,128,256]{2,1,0:T(8,128)S(1)} %copy-done.2, f32[2,6,2,8,128]{4,3,2,1,0:T(8,128)S(1)} %get-tuple-element.4.rows, f32[6,6,8,128]{3,2,1,0:T(8,128)S(1)} %get-tuple-element.5.cols), custom_call_target="tpu_custom_call" | custom-call | tf_op jit(solution)/shard_map/pixel_loss/pallas_call | solution.py:649
  (8 shorter events, 0.0 us)
Async XLA Ops:
  2.1 1.0 %copy-start.5 = (s32[8,16,512]{2,1,0:T(8,128)S(1)}, s32[8,16,512]{2,1,0:T(8,128)}, u32[]{:S(2)}) copy-start(s32[8,16,512]{2,1,0:T(8,128)} %param.7) | copy-start | bytes 786436
  5.2 1.4 %copy-start.6 = (s32[1,10240]{1,0:T(1,128)S(1)}, s32[1,10240]{1,0:T(1,128)}, u32[]{:S(2)}) copy-start(s32[1,10240]{1,0:T(1,128)} %param.6) | copy-start | bytes 122884
  5.2 2.4 %copy-start.3 = (f32[59,5120]{1,0:T(8,128)S(1)}, f32[59,5120]{1,0:T(8,128)}, u32[]{:S(2)}) copy-start(f32[59,5120]{1,0:T(8,128)} %gauss_ref.1) | copy-start | bytes 3624964
  7.6 25.3 %copy-start.4 = (bf16[256,32]{1,0:T(8,128)(2,1)S(1)}, bf16[256,32]{1,0:T(8,128)(2,1)}, u32[]{:S(2)}) copy-start(bf16[256,32]{1,0:T(8,128)(2,1)} %constant.117.mono) | copy-start | bytes 49156
  32.9 26.3 %copy-start.2 = (f32[3,128,256]{2,1,0:T(8,128)S(1)}, f32[3,128,256]{2,1,0:T(8,128)}, u32[]{:S(2)}) copy-start(f32[3,128,256]{2,1,0:T(8,128)} %truth.3) | copy-start | bytes 1179652
  59.2 1.0 %copy-start = (f32[3,128,256]{2,1,0:T(8,128)S(1)}, f32[3,128,256]{2,1,0:T(8,128)}, u32[]{:S(2)}) copy-start(f32[3,128,256]{2,1,0:T(8,128)} %blend_tiles.1.rendered) | copy-start | bytes 1179652
  73.4 1.0 %copy-start.1 = (f32[3,128,256]{2,1,0:T(8,128)S(1)}, f32[3,128,256]{2,1,0:T(8,128)}, u32[]{:S(2)}) copy-start(f32[3,128,256]{2,1,0:T(8,128)} %blend_tiles.1.rendered) | copy-start | bytes 1179652

commit v6 on v5

--- a/solution.py
+++ b/solution.py
@@ -109,29 +109,37 @@
     return out
 
 
-def fill_table(table, halves):
+def fill_table(table, third, halves):
+    rows = third.shape[0] // 2
     for half, ref in enumerate(halves):
-        for part, value in enumerate(split(ref[...], 3)):
+        lanes = slice(half * LANES, (half + 1) * LANES)
+        for part, value in enumerate(split(ref[...], 2)):
             table[:, part * 256 + half * LANES : part * 256 + (half + 1) * LANES] = value
-
-
-def lookup(table, code):
+        for p in range(2):
+            third[p * rows : (p + 1) * rows, lanes] = split(ref[pl.ds(p, rows, stride=8), :], 3)[2]
+
+
+def lookup(table, third, code):
     rows = table.shape[0] // SPLAT
     column = lax.broadcasted_iota(jnp.int32, (256, 256), 0)
     col = jnp.bitwise_and(code, 255)
     row = lax.shift_right_arithmetic(code, 8)
     hot = jnp.where(column == col, 1.0, 0.0).astype(jnp.bfloat16)
-    found = jnp.dot(table[...], jnp.concatenate([hot, hot, hot], axis=0), preferred_element_type=jnp.float32)
+    found = jnp.dot(table[...], jnp.concatenate([hot, hot], axis=0), preferred_element_type=jnp.float32)
+    finer = jnp.dot(third[...], hot, preferred_element_type=jnp.float32)
     picked = jnp.zeros((8, 256), jnp.float32)
     rows8 = jnp.broadcast_to(row, (8, 256))
     for r in range(rows):
         picked = jnp.where(rows8 == r, found[r * 8 : (r + 1) * 8], picked)
     table_row = lax.broadcasted_iota(jnp.int32, (rows, 256), 0)
-    ninth = jnp.sum(jnp.where(table_row == row, found[8 * rows :], 0.0), axis=0, keepdims=True)
-    return picked, ninth
-
-
-def outgoing_kernel(gauss_ref, code_ref, out_ref, table_a, table_b, table, eight):
+    choose = lambda lines: jnp.sum(jnp.where(table_row == row, lines, 0.0), axis=0, keepdims=True)
+    sub = lax.broadcasted_iota(jnp.int32, (8, 256), 0)
+    for p in range(2):
+        picked = picked + jnp.where(sub == p, choose(finer[p * rows : (p + 1) * rows]), 0.0)
+    return picked, choose(found[8 * rows :])
+
+
+def outgoing_kernel(gauss_ref, pick_ref, out_ref, table_a, table_b, table, third, eight):
     blocks = gauss_ref.shape[1] // LANES
     rows = blocks // 2
     for block in range(blocks):
@@ -140,13 +148,15 @@
         r = block % rows
         ref[r * 8 : r * 8 + 8, :] = jnp.concatenate(splat[:8], axis=0)
         ref[8 * rows + r : 8 * rows + r + 1, :] = splat[8]
-    fill_table(table, (table_a, table_b))
+    fill_table(table, third, (table_a, table_b))
 
     def eight_slots(i, carry):
         where = pl.multiple_of(i * 8, 8)
-        codes = code_ref[pl.ds(where, 8), :]
+        picks = pick_ref[pl.ds(where, 8), :]
+        block = lax.shift_right_logical(picks, 7)
+        codes = jnp.bitwise_and(picks, LANES - 1) + jnp.where(block < rows, block * 256, (block - rows) * 256 + LANES)
         found = [
-            lookup(table, jnp.concatenate([codes[2 * j : 2 * j + 1], codes[2 * j + 1 : 2 * j + 2]], axis=1))
+            lookup(table, third, jnp.concatenate([codes[2 * j : 2 * j + 1], codes[2 * j + 1 : 2 * j + 2]], axis=1))
             for j in range(4)
         ]
         for j, (first, last) in enumerate(found):
@@ -163,31 +173,12 @@
         out_ref[pl.ds(p, LANES, stride=8), :] = jnp.transpose(eight[pl.ds(p, LANES, stride=8), :])
 
 
-def outgoing_splats(gaussians, codes):
-    devices = codes.shape[1]
-    rows = gaussians.shape[1] // (2 * LANES)
-    f32 = jnp.float32
-    return pl.pallas_call(
-        outgoing_kernel,
-        out_shape=jax.ShapeDtypeStruct((devices * 8, LANES), f32),
-        in_specs=[pl.BlockSpec(memory_space=VMEM)] * 2,
-        out_specs=pl.BlockSpec(memory_space=VMEM),
-        scratch_shapes=[
-            VMEM((SPLAT * rows, LANES), f32),
-            VMEM((SPLAT * rows, LANES), f32),
-            VMEM((SPLAT * rows, 768), jnp.bfloat16),
-            VMEM((8 * LANES, LANES), f32),
-        ],
-        compiler_params=pltpu.CompilerParams(vmem_limit_bytes=32 << 20),
-        name="outgoing_splats",
-    )(gaussians, codes)
-
-
-def deal_kernel(out_ref, in_ref, send_sem, done_sem, local_sem):
+def deal_kernel(gauss_ref, pick_ref, in_ref, out_ref, send_sem, done_sem, local_sem, *scratch):
     n_gs, n_img = lax.axis_size("gs"), lax.axis_size("img")
     devices = n_gs * n_img
     me = lax.axis_index("gs") * n_img + lax.axis_index("img")
     place = lambda d: {"gs": lax.div(d, n_img), "img": lax.rem(d, n_img)}
+    block = lambda d: pl.ds(pl.multiple_of(d * 8, 8), 8)
     barrier = pltpu.get_barrier_semaphore()
 
     def greet(d, carry):
@@ -198,8 +189,8 @@
     def send(d, carry):
         to = lax.rem(me + d, devices)
         pltpu.make_async_remote_copy(
-            src_ref=out_ref.at[to],
-            dst_ref=in_ref.at[me],
+            src_ref=out_ref.at[block(to)],
+            dst_ref=in_ref.at[block(me)],
             send_sem=send_sem,
             recv_sem=done_sem,
             device_id=place(to),
@@ -208,30 +199,39 @@
         return carry
 
     lax.fori_loop(1, devices, greet, 0)
-    own = pltpu.make_async_copy(out_ref.at[me], in_ref.at[me], local_sem)
+    outgoing_kernel(gauss_ref, pick_ref, out_ref, *scratch)
+    own = pltpu.make_async_copy(out_ref.at[block(me)], in_ref.at[block(me)], local_sem)
     own.start()
     own.wait()
     pl.semaphore_wait(barrier, devices - 1)
     lax.fori_loop(1, devices, send, 0)
-    others = pl.ds(0, devices - 1)
+    others = pl.ds(0, (devices - 1) * 8)
     pltpu.make_async_copy(out_ref.at[others], out_ref.at[others], send_sem).wait()
     pltpu.make_async_copy(in_ref.at[others], in_ref.at[others], done_sem).wait()
 
 
-def deal(outgoing):
-    devices = lax.axis_size("gs") * lax.axis_size("img")
-    shape = (devices, 8, LANES)
+def deal(gaussians, picks):
+    devices = picks.shape[1]
+    rows = gaussians.shape[1] // (2 * LANES)
     vmem = pl.BlockSpec(memory_space=VMEM)
-    arrived = pl.pallas_call(
+    f32 = jnp.float32
+    return pl.pallas_call(
         deal_kernel,
-        out_shape=jax.ShapeDtypeStruct(shape, jnp.float32),
-        in_specs=[vmem],
+        out_shape=jax.ShapeDtypeStruct((devices * 8, LANES), f32),
+        in_specs=[vmem] * 2,
         out_specs=vmem,
-        scratch_shapes=[pltpu.SemaphoreType.DMA] * 3,
-        compiler_params=pltpu.CompilerParams(collective_id=2, has_side_effects=True, vmem_limit_bytes=16 << 20),
+        scratch_shapes=[VMEM((devices * 8, LANES), f32)]
+        + [pltpu.SemaphoreType.DMA] * 3
+        + [
+            VMEM((SPLAT * rows, LANES), f32),
+            VMEM((SPLAT * rows, LANES), f32),
+            VMEM((SPLAT * rows, 512), jnp.bfloat16),
+            VMEM((2 * rows, 256), jnp.bfloat16),
+            VMEM((8 * LANES, LANES), f32),
+        ],
+        compiler_params=pltpu.CompilerParams(collective_id=2, has_side_effects=True, vmem_limit_bytes=32 << 20),
         name="deal_splats",
-    )(outgoing.reshape(shape))
-    return arrived.reshape(outgoing.shape)
+    )(gaussians, picks)
 
 
 SEG = 32
@@ -254,7 +254,7 @@
 
 
 def blend_kernel(cols_here, first, base, arrived, lists, owner, mono, out_ref,
-                 table_a, table_b, table, packed, codes, params, coefs, power_a, power_b, state, total_ref,
+                 table_a, table_b, table, third, packed, codes, params, coefs, power_a, power_b, state, total_ref,
                  carry_ref, carry_owner):
     tiles = first.shape[0] - 1
     runs = lists.shape[0] // tiles
@@ -267,7 +267,7 @@
             ref[pl.ds(p, ROWS, stride=8), :] = flat[half * ROWS : (half + 1) * ROWS]
             if p == half:
                 ref[8 * ROWS :, :] = flat[CAP : CAP + ROWS]
-    fill_table(table, (table_a, table_b))
+    fill_table(table, third, (table_a, table_b))
 
     packed[...] = jnp.full(packed.shape, -1, jnp.int32)
     for t in range(tiles):
@@ -275,7 +275,11 @@
 
     def turn(g, carry):
         lanes = jnp.transpose(packed[pl.ds(pl.multiple_of(g * LANES, LANES), LANES), :])
-        codes[pl.ds(pl.multiple_of(g * SEG, SEG), SEG), :] = lanes[0:SEG]
+        slot = lanes[0:SEG]
+        source = ((slot.astype(jnp.float32) + 0.5) * (1.0 / CAP)).astype(jnp.int32)
+        k = slot - source * CAP
+        code = source + jnp.where(k < ROWS, k * 256, (k - ROWS) * 256 + LANES)
+        codes[pl.ds(pl.multiple_of(g * SEG, SEG), SEG), :] = jnp.where(slot >= 0, code, -1)
         return carry
 
     lax.fori_loop(0, groups, turn, 0)
@@ -286,7 +290,7 @@
     def look(block, j):
         where = block * BLOCK + 2 * j
         code = jnp.concatenate([codes[pl.ds(where, 1), :], codes[pl.ds(where + 1, 1), :]], axis=1)
-        return ((block % 3) * 72,) + lookup(table, code)
+        return ((block % 3) * 72,) + lookup(table, third, code)
 
     def keep(j, slot, picked, ninth):
         for e in range(2):
@@ -435,7 +439,8 @@
         scratch_shapes=[
             VMEM((9 * ROWS, LANES), f32),
             VMEM((9 * ROWS, LANES), f32),
-            VMEM((9 * ROWS, 768), jnp.bfloat16),
+            VMEM((9 * ROWS, 512), jnp.bfloat16),
+            VMEM((2 * ROWS, 256), jnp.bfloat16),
             VMEM((lists.shape[0] + LANES, LANES), jnp.int32),
             VMEM(((most + 1) * SEG, LANES), jnp.int32),
             VMEM((3 * 72, LANES), f32),
@@ -464,9 +469,7 @@
     most = tiles * runs
     segment = jnp.arange(most + LANES, dtype=jnp.int32)
     owner = jnp.sum((ends[None, :] <= segment[:, None]).astype(jnp.int32), axis=1).reshape(-1, LANES)
-    slot, source = lists % CAP, lists // CAP
-    code = jnp.where(lists >= 0, slot % ROWS * 256 + slot // ROWS * LANES + source, -1)
-    code = jnp.pad(code.reshape(most, SEG), ((0, 0), (0, LANES - SEG)), constant_values=-1)
+    code = jnp.pad(lists.reshape(most, SEG), ((0, 0), (0, LANES - SEG)), constant_values=-1)
     half = TILE // 2
     base = jnp.stack(
         [lax.axis_index("gs") * (cols_here * TILE) + half, lax.axis_index("img") * (rows_here * TILE) + half]
@@ -609,12 +612,10 @@
         first, second, outside = parts
         sums = [weights[TAPS] * first, weights[TAPS] * second]
         for d in range(1, TAPS + 1):
-            ahead = [pltpu.roll(x, LANES - d, 1) for x in (first, second, outside)]
-            back = [pltpu.roll(x, d, 1) for x in (outside, first, second)]
-            inside_ahead, inside_back = lane < LANES - d, lane >= d
-            for half in range(2):
-                pair = jnp.where(inside_ahead, ahead[half], ahead[half + 1])
-                pair = pair + jnp.where(inside_back, back[half + 1], back[half])
+            from_ahead, from_back = lane >= d, lane < LANES - d
+            for half, (before, here, after) in enumerate(((outside, first, second), (first, second, outside))):
+                pair = pltpu.roll(jnp.where(from_ahead, here, after), LANES - d, 1)
+                pair = pair + pltpu.roll(jnp.where(from_back, here, before), d, 1)
                 sums[half] = sums[half] + weights[TAPS + d] * pair
         return sums
 
@@ -660,10 +661,7 @@
 def on_device(gaussians, send_slots, tile_lists, truth):
     rows_here, cols_here, list_len = tile_lists.shape
     devices = send_slots.shape[1] // CAP
-    half = gaussians.shape[1] // 2
-    picks = send_slots.reshape(devices, CAP).T
-    codes = picks % half // LANES * 256 + picks // half * LANES + picks % LANES
-    arrived = deal(outgoing_splats(gaussians, codes))
+    arrived = deal(gaussians, send_slots.reshape(devices, CAP).T)
     first, base, code, owner = arrange(tile_lists)
     rendered = blend_tiles(first, base, arrived, code, owner, cols_here)
     rows, cols = exchange_halos(rendered, truth)

time: 83.9 us -> 73.4 us (0.87)
  the two profiles are of different devices: /device:TPU:0 before, /device:TPU:3 now
where the time goes in v6:
time: 73.4 us; the launch traced here: 73.1 us
  Pallas kernels  65.5 us (89%)
  local copies, waits for them, and re-layouts  4.21 us (6%)
  other arithmetic  2.65 us (4%)
  between operations  0.78 us (1%)
    pallas_call x1, Pallas kernels, blend_tiles(): pl.pallas_call(functools.partial(blend_kernel, cols_here), out_shape=jax....  25.5 us
    pallas_call x1, Pallas kernels, deal(): pl.pallas_call(deal_kernel, out_shape=jax.ShapeDtypeStruct((devices * 8,...  19.6 us
    pallas_call x1, Pallas kernels, exchange_halos(): pl.pallas_call(halo_kernel, out_shape=(jax.ShapeDtypeStruct(rows, f32), j...  13 us
    pallas_call x1, Pallas kernels, pixel_loss(): pl.pallas_call(loss_kernel, out_shape=jax.ShapeDtypeStruct((height, width...  7.26 us
    unnamed x13, local copies, waits for them, and re-layouts  2.67 us

profile of v6, /device:TPU:3, one launch (start us, length us, event | category | flops | bytes accessed | tf_op | source)
XLA Modules:
  0.0 73.1 jit_solution(16803387050533406809)
XLA Ops:
  0.6 0.1 add_convert_fusion.has
  0.7 0.1 pad_add_fusion.1.base
  0.8 1.2 %convert_reduce_fusion.1 = s32[8,16]{1,0:T(8,128)S(1)} fusion(s32[8,16,512]{2,1,0:T(8,128)} %param.7), kind=kLoop, calls=%fused_computation.2 | loop fusion | flops 196480 | bytes 262656 | tf_op jit(solution)/shard_map/reduce_sum | solution.py:465
  2.0 0.1 sub.18
  2.1 0.1 select_reduce_fusion
  2.2 0.4 convert_reduce_fusion
  2.6 0.1 pad_add_fusion.first
  2.7 1.2 %reshape_reshape.3 = s32[2048,32]{1,0:T(8,128)S(1)} reshape(s32[8,16,512]{2,1,0:T(8,128)} %param.7) | data formatting | bytes 524288 | tf_op jit(solution)/shard_map/reshape;reshape | solution.py:472
  3.9 0.0 copy-start.5
  3.9 0.0 copy-start.3
  3.9 0.1 pad.4.lists
  4.0 0.0 copy-start.4
  4.0 0.5 broadcast.54
  4.5 0.2 copy-done.5
  4.7 0.7 %reduce.4 = s32[10240]{0:T(1024)S(1)} reduce(s32[1,10240]{1,0:T(1,128)S(1)} %copy-done.5, s32[]{:T(128)} %broadcast.54), dimensions={0}, to_apply=%param.6.reduce_sub_computation.3 | reduce | bytes 81924 | tf_op args[1]
  5.4 0.1 reshape.36
  5.5 0.1 copy.8
  5.6 0.0 copy-done.3
  5.6 19.6 %deal_splats.1.arrived = f32[1024,128]{1,0:T(8,128)S(1)} custom-call(f32[59,5120]{1,0:T(8,128)S(1)} %copy-done.3, s32[80,128]{1,0:T(8,128)S(1)} %bitcast.8), custom_call_target="tpu_custom_call" | custom-call | tf_op jit(solution)/shard_map/deal_splats/pallas_call | solution.py:218
  25.2 0.0 copy-done.4
  25.2 0.0 copy-start.2
  25.3 25.5 %blend_tiles.1.rendered = f32[3,128,256]{2,1,0:T(8,128)} custom-call(s32[129]{0:T(256)S(1)} %pad_add_fusion.first, s32[2]{0:T(128)S(1)} %pad_add_fusion.1.base, f32[1024,128]{1,0:T(8,128)S(1)} %deal_splats.1.arrived, s32[2048,128]{1,0:T(8,128)S(1)} %pad.4.lists, s32[17,128]{1,0:T(8,128)S(1)} %bitcast.9, bf16[256,32]{1,0:T(8,128)(2,1)S(1)} %copy-done.4), custom_call_target="tpu_custom_call" | custom-call | tf_op jit(solution)/shard_map/blend_tiles/pallas_call | solution.py:434
  50.8 0.0 copy-done.2
  50.8 0.0 copy-start
  50.8 1.0 %copy-done = f32[3,128,256]{2,1,0:T(8,128)S(1)} copy-done((f32[3,128,256]{2,1,0:T(8,128)S(1)}, f32[3,128,256]{2,1,0:T(8,128)}, u32[]{:S(2)}) %copy-start) | copy-done | bytes 393240
  51.8 13.0 %exchange_halos.1 = (f32[2,6,2,8,128]{4,3,2,1,0:T(8,128)S(1)}, f32[6,6,8,128]{3,2,1,0:T(8,128)S(1)}) custom-call(f32[3,128,256]{2,1,0:T(8,128)S(1)} %copy-done, f32[3,128,256]{2,1,0:T(8,128)S(1)} %copy-done.2), custom_call_target="tpu_custom_call" | custom-call | tf_op jit(solution)/shard_map/exchange_halos/pallas_call | solution.py:540
  64.8 0.0 copy-start.1
  64.8 1.0 %copy-done.1 = f32[3,128,256]{2,1,0:T(8,128)S(1)} copy-done((f32[3,128,256]{2,1,0:T(8,128)S(1)}, f32[3,128,256]{2,1,0:T(8,128)}, u32[]{:S(2)}) %copy-start.1) | copy-done | bytes 393240
  65.8 7.3 %pixel_loss.1 = f32[128,256]{1,0:T(8,128)} custom-call(s32[4]{0:T(128)S(1)} %add_convert_fusion.has, f32[3,128,256]{2,1,0:T(8,128)S(1)} %copy-done.1, f32[3,128,256]{2,1,0:T(8,128)S(1)} %copy-done.2, f32[2,6,2,8,128]{4,3,2,1,0:T(8,128)S(1)} %get-tuple-element.4.rows, f32[6,6,8,128]{3,2,1,0:T(8,128)S(1)} %get-tuple-element.5.cols), custom_call_target="tpu_custom_call" | custom-call | tf_op jit(solution)/shard_map/pixel_loss/pallas_call | solution.py:650
  (2 shorter events, 0.0 us)
Async XLA Ops:
  3.9 0.8 %copy-start.5 = (s32[1,10240]{1,0:T(1,128)S(1)}, s32[1,10240]{1,0:T(1,128)}, u32[]{:S(2)}) copy-start(s32[1,10240]{1,0:T(1,128)} %param.6) | copy-start | bytes 122884
  3.9 1.7 %copy-start.3 = (f32[59,5120]{1,0:T(8,128)S(1)}, f32[59,5120]{1,0:T(8,128)}, u32[]{:S(2)}) copy-start(f32[59,5120]{1,0:T(8,128)} %gauss_ref.1) | copy-start | bytes 3624964
  4.0 21.3 %copy-start.4 = (bf16[256,32]{1,0:T(8,128)(2,1)S(1)}, bf16[256,32]{1,0:T(8,128)(2,1)}, u32[]{:S(2)}) copy-start(bf16[256,32]{1,0:T(8,128)(2,1)} %constant.50.mono) | copy-start | bytes 49156
  25.2 25.6 %copy-start.2 = (f32[3,128,256]{2,1,0:T(8,128)S(1)}, f32[3,128,256]{2,1,0:T(8,128)}, u32[]{:S(2)}) copy-start(f32[3,128,256]{2,1,0:T(8,128)} %truth.3) | copy-start | bytes 1179652
  50.8 1.0 %copy-start = (f32[3,128,256]{2,1,0:T(8,128)S(1)}, f32[3,128,256]{2,1,0:T(8,128)}, u32[]{:S(2)}) copy-start(f32[3,128,256]{2,1,0:T(8,128)} %blend_tiles.1.rendered) | copy-start | bytes 1179652
  64.8 1.0 %copy-start.1 = (f32[3,128,256]{2,1,0:T(8,128)S(1)}, f32[3,128,256]{2,1,0:T(8,128)}, u32[]{:S(2)}) copy-start(f32[3,128,256]{2,1,0:T(8,128)} %blend_tiles.1.rendered) | copy-start | bytes 1179652

commit v7 on v6

--- a/solution.py
+++ b/solution.py
@@ -121,10 +121,10 @@
 
 def lookup(table, third, code):
     rows = table.shape[0] // SPLAT
-    column = lax.broadcasted_iota(jnp.int32, (256, 256), 0)
-    col = jnp.bitwise_and(code, 255)
+    column = lax.broadcasted_iota(jnp.int32, (256, 256), 0).astype(jnp.float32).astype(jnp.bfloat16)
+    col = jnp.bitwise_and(code, 255).astype(jnp.float32).astype(jnp.bfloat16)
     row = lax.shift_right_arithmetic(code, 8)
-    hot = jnp.where(column == col, 1.0, 0.0).astype(jnp.bfloat16)
+    hot = jnp.where(column == col, jnp.bfloat16(1), jnp.bfloat16(0))
     found = jnp.dot(table[...], jnp.concatenate([hot, hot], axis=0), preferred_element_type=jnp.float32)
     finer = jnp.dot(third[...], hot, preferred_element_type=jnp.float32)
     picked = jnp.zeros((8, 256), jnp.float32)
@@ -229,7 +229,7 @@
             VMEM((2 * rows, 256), jnp.bfloat16),
             VMEM((8 * LANES, LANES), f32),
         ],
-        compiler_params=pltpu.CompilerParams(collective_id=2, has_side_effects=True, vmem_limit_bytes=32 << 20),
+        compiler_params=pltpu.CompilerParams(collective_id=2, has_side_effects=True, vmem_limit_bytes=16 << 20),
         name="deal_splats",
     )(gaussians, picks)
 
@@ -253,9 +253,9 @@
     return jnp.take_along_axis(value, index, axis=axis, mode="promise_in_bounds")
 
 
-def blend_kernel(cols_here, first, base, arrived, lists, owner, mono, out_ref,
+def blend_kernel(cols_here, first, base, arrived, lists, ends, mono, out_ref,
                  table_a, table_b, table, third, packed, codes, params, coefs, power_a, power_b, state, total_ref,
-                 carry_ref, carry_owner):
+                 carry_ref, carry_owner, owner):
     tiles = first.shape[0] - 1
     runs = lists.shape[0] // tiles
     groups = (first[tiles] + LANES - 1) // LANES
@@ -283,6 +283,15 @@
         return carry
 
     lax.fori_loop(0, groups, turn, 0)
+    ends_down = jnp.transpose(jnp.broadcast_to(ends[...], (LANES, LANES)))
+    along = lax.broadcasted_iota(jnp.int32, (LANES, LANES), 1)
+
+    def own(g, carry):
+        past = jnp.where(ends_down <= along + g * LANES, 1, 0)
+        owner[pl.ds(g, 1), :] = jnp.sum(past, axis=0, keepdims=True)
+        return carry
+
+    lax.fori_loop(0, groups + 1, own, 0)
     total_ref[...] = jnp.zeros_like(total_ref)
     carry_ref[...] = jnp.ones_like(carry_ref)
     carry_owner[...] = jnp.full(carry_owner.shape, -1, jnp.int32)
@@ -425,7 +434,7 @@
                     out_ref[ch, r * TILE + h * 8 : r * TILE + h * 8 + 8, q * LANES : (q + 1) * LANES] = x
 
 
-def blend_tiles(first, base, arrived, lists, owner, cols_here):
+def blend_tiles(first, base, arrived, lists, ends, cols_here):
     tiles = first.shape[0] - 1
     most = lists.shape[0] // LANES
     smem = pl.BlockSpec(memory_space=pltpu.SMEM)
@@ -451,10 +460,11 @@
             VMEM((3, tiles, PIXELS), f32),
             VMEM((PIXELS, LANES), f32),
             VMEM((8, LANES), jnp.int32),
+            VMEM((most + 8, LANES), jnp.int32),
         ],
-        compiler_params=pltpu.CompilerParams(vmem_limit_bytes=48 << 20),
+        compiler_params=pltpu.CompilerParams(vmem_limit_bytes=20 << 20),
         name="blend_tiles",
-    )(first, base, arrived, lists, owner, jnp.asarray(monomials()).astype(jnp.bfloat16))
+    )(first, base, arrived, lists, ends, jnp.asarray(monomials()).astype(jnp.bfloat16))
 
 
 def arrange(tile_lists):
@@ -467,14 +477,12 @@
     ends = jnp.sum(jnp.where(number[None, :] <= number[:, None], live[None, :], 0), axis=1).astype(jnp.int32)
     first = jnp.concatenate([jnp.zeros((1,), jnp.int32), ends])
     most = tiles * runs
-    segment = jnp.arange(most + LANES, dtype=jnp.int32)
-    owner = jnp.sum((ends[None, :] <= segment[:, None]).astype(jnp.int32), axis=1).reshape(-1, LANES)
     code = jnp.pad(lists.reshape(most, SEG), ((0, 0), (0, LANES - SEG)), constant_values=-1)
     half = TILE // 2
     base = jnp.stack(
         [lax.axis_index("gs") * (cols_here * TILE) + half, lax.axis_index("img") * (rows_here * TILE) + half]
     ).astype(jnp.int32)
-    return first, base, code, owner
+    return first, base, code, ends.reshape(1, tiles)
 
 
 EDGE = 8
@@ -550,7 +558,7 @@
             pltpu.SemaphoreType.DMA((2,)),
             pltpu.SemaphoreType.DMA((6,)),
         ],
-        compiler_params=pltpu.CompilerParams(collective_id=1, has_side_effects=True, vmem_limit_bytes=16 << 20),
+        compiler_params=pltpu.CompilerParams(collective_id=1, has_side_effects=True, vmem_limit_bytes=8 << 20),
         name="exchange_halos",
     )(rendered, truth)
 
@@ -561,7 +569,7 @@
     return [float(w) for w in weights / np.sum(weights)]
 
 
-def loss_kernel(has, rendered, truth, rows, cols, out_ref, maps):
+def loss_kernel(has, rendered, truth, rows, cols, out_ref, maps, summed, turned, likeness):
     height = rendered.shape[1]
     tall = height + 2 * EDGE
     start = lambda q, part: (q * 3 + part) * tall
@@ -585,9 +593,9 @@
             upper = keep(flag & above, cols[side + 2, c])
             lower = keep(flag & below, cols[side + 0, c])
             mixed.append(jnp.where(lane < LANES // 2, lower, upper))
-        turned = jnp.transpose(jnp.concatenate([mixed[0], gap, mixed[1]], axis=0))
-        maps[base : base + EDGE, :] = turned[LANES - EDGE :]
-        maps[base + EDGE + height : base + tall, :] = turned[0:EDGE]
+        corners = jnp.transpose(jnp.concatenate([mixed[0], gap, mixed[1]], axis=0))
+        maps[base : base + EDGE, :] = corners[LANES - EDGE :]
+        maps[base + EDGE + height : base + tall, :] = corners[0:EDGE]
 
     def products(n, carry):
         for ch in range(3):
@@ -601,47 +609,52 @@
     lax.fori_loop(0, tall // 8, products, 0)
     weights = window()
 
-    def filtered(q, n):
-        parts = []
-        for part in range(3):
-            row = lambda d: maps[pl.ds(start(q, part) + EDGE + n * 8 + d, 8), :]
-            total = weights[TAPS] * row(0)
-            for d in range(1, TAPS + 1):
-                total = total + weights[TAPS + d] * (row(d) + row(-d))
-            parts.append(total)
-        first, second, outside = parts
-        sums = [weights[TAPS] * first, weights[TAPS] * second]
+    def window_sum(ref, first):
+        row = lambda d: ref[pl.ds(first + d, 8), :]
+        total = weights[TAPS] * row(0)
         for d in range(1, TAPS + 1):
-            from_ahead, from_back = lane >= d, lane < LANES - d
-            for half, (before, here, after) in enumerate(((outside, first, second), (first, second, outside))):
-                pair = pltpu.roll(jnp.where(from_ahead, here, after), LANES - d, 1)
-                pair = pair + pltpu.roll(jnp.where(from_back, here, before), d, 1)
-                sums[half] = sums[half] + weights[TAPS + d] * pair
-        return sums
-
-    def one_block(n, carry):
-        difference = [0.0, 0.0]
-        alike = [0.0, 0.0]
-        where = pl.ds(pl.multiple_of(n * 8, 8), 8)
+            total = total + weights[TAPS + d] * (row(d) + row(-d))
+        return total
+
+    def over_rows(n, carry):
+        for q in range(12):
+            for part in range(3):
+                at = pl.ds(pl.multiple_of((q * 3 + part) * height + n * 8, 8), 8)
+                summed[at, :] = window_sum(maps, start(q, part) + EDGE + n * 8)
+        return carry
+
+    lax.fori_loop(0, height // 8, over_rows, 0)
+    wide = 2 * LANES + 2 * EDGE
+    for q in range(12):
+        blocks = [jnp.transpose(summed[(q * 3 + part) * height : (q * 3 + part + 1) * height, :]) for part in range(3)]
+        base = q * wide
+        turned[base : base + EDGE, :] = blocks[2][LANES - EDGE :]
+        turned[base + EDGE : base + EDGE + LANES, :] = blocks[0]
+        turned[base + EDGE + LANES : base + EDGE + 2 * LANES, :] = blocks[1]
+        turned[base + EDGE + 2 * LANES : base + wide, :] = blocks[2][:EDGE]
+
+    def over_columns(n, carry):
+        alike = 0.0
         for ch in range(3):
-            means_r, means_t, squares, products_rt = [filtered(q + ch, n) for q in (0, 3, 6, 9)]
-            for half in range(2):
-                mean_r, mean_t = means_r[half], means_t[half]
-                both = mean_r * mean_t
-                squared = mean_r * mean_r + mean_t * mean_t
-                above_line = (2.0 * both + stable_one) * (2.0 * (products_rt[half] - both) + stable_two)
-                below_line = (squared + stable_one) * (squares[half] - squared + stable_two)
-                alike[half] = alike[half] + above_line / below_line
-                at = pl.ds(pl.multiple_of(start(ch, half) + EDGE + n * 8, 8), 8)
-                at_t = pl.ds(pl.multiple_of(start(ch + 3, half) + EDGE + n * 8, 8), 8)
-                difference[half] = difference[half] + jnp.abs(maps[at, :] - maps[at_t, :])
-        for half in range(2):
-            out_ref[where, half * LANES : (half + 1) * LANES] = (1.0 - ssim_share) * (
-                difference[half] * (1.0 / 3.0)
-            ) + ssim_share * (1.0 - alike[half] * (1.0 / 3.0))
-        return carry
-
-    lax.fori_loop(0, height // 8, one_block, 0)
+            mean_r, mean_t, square, product = [
+                window_sum(turned, (q + ch) * wide + EDGE + n * 8) for q in (0, 3, 6, 9)
+            ]
+            both = mean_r * mean_t
+            squared = mean_r * mean_r + mean_t * mean_t
+            above_line = (2.0 * both + stable_one) * (2.0 * (product - both) + stable_two)
+            below_line = (squared + stable_one) * (square - squared + stable_two)
+            alike = alike + above_line / below_line
+        likeness[pl.ds(pl.multiple_of(n * 8, 8), 8), :] = alike
+        return carry
+
+    lax.fori_loop(0, 2 * LANES // 8, over_columns, 0)
+    for half in range(2):
+        lanes = slice(half * LANES, (half + 1) * LANES)
+        difference = jnp.abs(rendered[0, :, lanes] - truth[0, :, lanes])
+        for ch in (1, 2):
+            difference = difference + jnp.abs(rendered[ch, :, lanes] - truth[ch, :, lanes])
+        alike = jnp.transpose(likeness[lanes, :])
+        out_ref[:, lanes] = (1.0 - ssim_share) * (difference * (1.0 / 3.0)) + ssim_share * (1.0 - alike * (1.0 / 3.0))
 
 
 def pixel_loss(has, rendered, truth, rows, cols):
@@ -652,8 +665,13 @@
         out_shape=jax.ShapeDtypeStruct((height, width), jnp.float32),
         in_specs=[pl.BlockSpec(memory_space=pltpu.SMEM)] + [vmem] * 4,
         out_specs=vmem,
-        scratch_shapes=[VMEM((12 * 3 * (height + 2 * EDGE), LANES), jnp.float32)],
-        compiler_params=pltpu.CompilerParams(vmem_limit_bytes=32 << 20),
+        scratch_shapes=[
+            VMEM((12 * 3 * (height + 2 * EDGE), LANES), jnp.float32),
+            VMEM((12 * 3 * height, LANES), jnp.float32),
+            VMEM((12 * (width + 2 * EDGE), LANES), jnp.float32),
+            VMEM((width, LANES), jnp.float32),
+        ],
+        compiler_params=pltpu.CompilerParams(vmem_limit_bytes=16 << 20),
         name="pixel_loss",
     )(has, rendered, truth, rows, cols)
 
@@ -662,8 +680,8 @@
     rows_here, cols_here, list_len = tile_lists.shape
     devices = send_slots.shape[1] // CAP
     arrived = deal(gaussians, send_slots.reshape(devices, CAP).T)
-    first, base, code, owner = arrange(tile_lists)
-    rendered = blend_tiles(first, base, arrived, code, owner, cols_here)
+    first, base, code, ends = arrange(tile_lists)
+    rendered = blend_tiles(first, base, arrived, code, ends, cols_here)
     rows, cols = exchange_halos(rendered, truth)
     g, i = lax.axis_index("gs"), lax.axis_index("img")
     has = jnp.stack([g > 0, g < lax.axis_size("gs") - 1, i > 0, i < lax.axis_size("img") - 1]).astype(jnp.int32)

time: 73.4 us -> 71.9 us (0.980)
  the two profiles are of different devices: /device:TPU:3 before, /device:TPU:0 now
where the time goes in v7:
time: 71.9 us; the launch traced here: 71.1 us
  Pallas kernels  63.8 us (89%)
  local copies, waits for them, and re-layouts  4.21 us (6%)
  other arithmetic  2.26 us (3%)
  between operations  0.78 us (1%)
    pallas_call x1, Pallas kernels, blend_tiles(): pl.pallas_call(functools.partial(blend_kernel, cols_here), out_shape=jax....  25 us
    pallas_call x1, Pallas kernels, deal(): pl.pallas_call(deal_kernel, out_shape=jax.ShapeDtypeStruct((devices * 8,...  20.7 us
    pallas_call x1, Pallas kernels, exchange_halos(): pl.pallas_call(halo_kernel, out_shape=(jax.ShapeDtypeStruct(rows, f32), j...  12.7 us
    pallas_call x1, Pallas kernels, pixel_loss(): pl.pallas_call(loss_kernel, out_shape=jax.ShapeDtypeStruct((height, width...  5.48 us
    unnamed x13, local copies, waits for them, and re-layouts  2.67 us

profile of v7, /device:TPU:0, one launch (start us, length us, event | category | flops | bytes accessed | tf_op | source)
XLA Modules:
  0.0 71.1 jit_solution(6309902752179686622)
XLA Ops:
  0.6 0.1 add_convert_fusion.has
  0.7 0.1 pad_add_fusion.1.base
  0.8 1.2 %convert_reduce_fusion = s32[8,16]{1,0:T(8,128)S(1)} fusion(s32[8,16,512]{2,1,0:T(8,128)} %param.7), kind=kLoop, calls=%fused_computation | loop fusion | flops 196480 | bytes 262656 | tf_op jit(solution)/shard_map/reduce_sum | solution.py:475
  2.0 0.1 sub.18
  2.1 0.1 select_reduce_fusion
  2.2 0.1 pad_add_fusion.first
  2.3 1.2 %reshape_reshape.3 = s32[2048,32]{1,0:T(8,128)S(1)} reshape(s32[8,16,512]{2,1,0:T(8,128)} %param.7) | data formatting | bytes 524288 | tf_op jit(solution)/shard_map/reshape;reshape | solution.py:480
  3.5 0.0 copy-start.5
  3.5 0.0 copy-start.3
  3.5 0.1 pad.4.lists
  3.6 0.0 copy-start.4
  3.6 0.5 broadcast.53
  4.1 0.2 copy-done.5
  4.3 0.7 %reduce.4 = s32[10240]{0:T(1024)S(1)} reduce(s32[1,10240]{1,0:T(1,128)S(1)} %copy-done.5, s32[]{:T(128)} %broadcast.53), dimensions={0}, to_apply=%param.6.reduce_sub_computation.3 | reduce | bytes 81924 | tf_op args[1]
  5.0 0.1 reshape.35
  5.1 0.1 copy.8
  5.2 0.0 copy-done.3
  5.2 20.7 %deal_splats.1.arrived = f32[1024,128]{1,0:T(8,128)S(1)} custom-call(f32[59,5120]{1,0:T(8,128)S(1)} %copy-done.3, s32[80,128]{1,0:T(8,128)S(1)} %bitcast.8), custom_call_target="tpu_custom_call" | custom-call | tf_op jit(solution)/shard_map/deal_splats/pallas_call | solution.py:218
  25.9 0.0 copy-done.4
  25.9 0.0 copy-start.2
  25.9 25.0 %blend_tiles.1.rendered = f32[3,128,256]{2,1,0:T(8,128)} custom-call(s32[129]{0:T(256)S(1)} %pad_add_fusion.first, s32[2]{0:T(128)S(1)} %pad_add_fusion.1.base, f32[1024,128]{1,0:T(8,128)S(1)} %deal_splats.1.arrived, s32[2048,128]{1,0:T(8,128)S(1)} %pad.4.lists, s32[1,128]{1,0:T(1,128)S(1)} %bitcast.9, bf16[256,32]{1,0:T(8,128)(2,1)S(1)} %copy-done.4), custom_call_target="tpu_custom_call" | custom-call | tf_op jit(solution)/shard_map/blend_tiles/pallas_call | solution.py:443
  50.9 0.0 copy-done.2
  50.9 0.0 copy-start
  50.9 1.0 %copy-done = f32[3,128,256]{2,1,0:T(8,128)S(1)} copy-done((f32[3,128,256]{2,1,0:T(8,128)S(1)}, f32[3,128,256]{2,1,0:T(8,128)}, u32[]{:S(2)}) %copy-start) | copy-done | bytes 393240
  51.9 12.7 %exchange_halos.1 = (f32[2,6,2,8,128]{4,3,2,1,0:T(8,128)S(1)}, f32[6,6,8,128]{3,2,1,0:T(8,128)S(1)}) custom-call(f32[3,128,256]{2,1,0:T(8,128)S(1)} %copy-done, f32[3,128,256]{2,1,0:T(8,128)S(1)} %copy-done.2), custom_call_target="tpu_custom_call" | custom-call | tf_op jit(solution)/shard_map/exchange_halos/pallas_call | solution.py:548
  64.6 0.0 copy-start.1
  64.6 1.0 %copy-done.1 = f32[3,128,256]{2,1,0:T(8,128)S(1)} copy-done((f32[3,128,256]{2,1,0:T(8,128)S(1)}, f32[3,128,256]{2,1,0:T(8,128)}, u32[]{:S(2)}) %copy-start.1) | copy-done | bytes 393240
  65.6 5.5 %pixel_loss.1 = f32[128,256]{1,0:T(8,128)} custom-call(s32[4]{0:T(128)S(1)} %add_convert_fusion.has, f32[3,128,256]{2,1,0:T(8,128)S(1)} %copy-done.1, f32[3,128,256]{2,1,0:T(8,128)S(1)} %copy-done.2, f32[2,6,2,8,128]{4,3,2,1,0:T(8,128)S(1)} %get-tuple-element.4.rows, f32[6,6,8,128]{3,2,1,0:T(8,128)S(1)} %get-tuple-element.5.cols), custom_call_target="tpu_custom_call" | custom-call | tf_op jit(solution)/shard_map/pixel_loss/pallas_call | solution.py:663
  (2 shorter events, 0.0 us)
Async XLA Ops:
  3.5 0.8 %copy-start.5 = (s32[1,10240]{1,0:T(1,128)S(1)}, s32[1,10240]{1,0:T(1,128)}, u32[]{:S(2)}) copy-start(s32[1,10240]{1,0:T(1,128)} %param.6) | copy-start | bytes 122884
  3.5 1.7 %copy-start.3 = (f32[59,5120]{1,0:T(8,128)S(1)}, f32[59,5120]{1,0:T(8,128)}, u32[]{:S(2)}) copy-start(f32[59,5120]{1,0:T(8,128)} %gauss_ref.1) | copy-start | bytes 3624964
  3.6 22.3 %copy-start.4 = (bf16[256,32]{1,0:T(8,128)(2,1)S(1)}, bf16[256,32]{1,0:T(8,128)(2,1)}, u32[]{:S(2)}) copy-start(bf16[256,32]{1,0:T(8,128)(2,1)} %constant.50.mono) | copy-start | bytes 49156
  25.9 25.0 %copy-start.2 = (f32[3,128,256]{2,1,0:T(8,128)S(1)}, f32[3,128,256]{2,1,0:T(8,128)}, u32[]{:S(2)}) copy-start(f32[3,128,256]{2,1,0:T(8,128)} %truth.3) | copy-start | bytes 1179652
  50.9 1.0 %copy-start = (f32[3,128,256]{2,1,0:T(8,128)S(1)}, f32[3,128,256]{2,1,0:T(8,128)}, u32[]{:S(2)}) copy-start(f32[3,128,256]{2,1,0:T(8,128)} %blend_tiles.1.rendered) | copy-start | bytes 1179652
  64.6 1.0 %copy-start.1 = (f32[3,128,256]{2,1,0:T(8,128)S(1)}, f32[3,128,256]{2,1,0:T(8,128)}, u32[]{:S(2)}) copy-start(f32[3,128,256]{2,1,0:T(8,128)} %blend_tiles.1.rendered) | copy-start | bytes 1179652

commit v8 on v7

--- a/solution.py
+++ b/solution.py
@@ -42,11 +42,9 @@
 stable_two = 0.0009
 
 
-def project_chunk(gauss):
-    row = lambda i: gauss[i : i + 1]
+def project(row):
     mean_x, mean_y, mean_z = (row(0), row(1), row(2))
-    squared = jnp.exp(2.0 * gauss[3:6])
-    sq_0, sq_1, sq_2 = (squared[0:1], squared[1:2], squared[2:3])
+    sq_0, sq_1, sq_2 = [jnp.exp(2.0 * row(i)) for i in (3, 4, 5)]
     inv = 1.0 / jnp.sqrt(row(6) * row(6) + row(7) * row(7) + row(8) * row(8) + row(9) * row(9))
     quat_w, quat_x, quat_y, quat_z = (row(6) * inv, row(7) * inv, row(8) * inv, row(9) * inv)
     first_a = 1.0 - 2.0 * (quat_y * quat_y + quat_z * quat_z)
@@ -65,31 +63,30 @@
     dir_x, dir_y, dir_z = (mean_x / length, mean_y / length, delta_z / length)
     sq_x, sq_y, sq_z = (dir_x * dir_x, dir_y * dir_y, dir_z * dir_z)
     prod_xy, prod_yz, prod_xz = (dir_x * dir_y, dir_y * dir_z, dir_x * dir_z)
-    basis = jnp.concatenate(
-        [
-            coef_zero * jnp.ones_like(dir_x),
-            -coef_one * dir_y,
-            coef_one * dir_z,
-            -coef_one * dir_x,
-            coef_two[0] * prod_xy,
-            coef_two[1] * prod_yz,
-            coef_two[2] * (2.0 * sq_z - sq_x - sq_y),
-            coef_two[3] * prod_xz,
-            coef_two[4] * (sq_x - sq_y),
-            coef_three[0] * dir_y * (3.0 * sq_x - sq_y),
-            coef_three[1] * prod_xy * dir_z,
-            coef_three[2] * dir_y * (4.0 * sq_z - sq_x - sq_y),
-            coef_three[3] * dir_z * (2.0 * sq_z - 3.0 * sq_x - 3.0 * sq_y),
-            coef_three[4] * dir_x * (4.0 * sq_z - sq_x - sq_y),
-            coef_three[5] * dir_z * (sq_x - sq_y),
-            coef_three[6] * dir_x * (sq_x - 3.0 * sq_y),
-        ],
-        axis=0,
-    )
+    basis = [
+        coef_zero * jnp.ones_like(dir_x),
+        -coef_one * dir_y,
+        coef_one * dir_z,
+        -coef_one * dir_x,
+        coef_two[0] * prod_xy,
+        coef_two[1] * prod_yz,
+        coef_two[2] * (2.0 * sq_z - sq_x - sq_y),
+        coef_two[3] * prod_xz,
+        coef_two[4] * (sq_x - sq_y),
+        coef_three[0] * dir_y * (3.0 * sq_x - sq_y),
+        coef_three[1] * prod_xy * dir_z,
+        coef_three[2] * dir_y * (4.0 * sq_z - sq_x - sq_y),
+        coef_three[3] * dir_z * (2.0 * sq_z - 3.0 * sq_x - 3.0 * sq_y),
+        coef_three[4] * dir_x * (4.0 * sq_z - sq_x - sq_y),
+        coef_three[5] * dir_z * (sq_x - sq_y),
+        coef_three[6] * dir_x * (sq_x - 3.0 * sq_y),
+    ]
     colour = []
     for channel in range(3):
-        weights = gauss[11 + 16 * channel : 27 + 16 * channel]
-        colour.append(jnp.maximum(jnp.sum(weights * basis, axis=0, keepdims=True) + 0.5, 0.0))
+        total = 0.5
+        for k, value in enumerate(basis):
+            total = total + row(11 + 16 * channel + k) * value
+        colour.append(jnp.maximum(total, 0.0))
     return [
         mean_x,
         mean_y,
@@ -139,20 +136,30 @@
     return picked, choose(found[8 * rows :])
 
 
-def outgoing_kernel(gauss_ref, pick_ref, out_ref, table_a, table_b, table, third, eight):
+def outgoing_kernel(gauss_ref, pick_ref, out_ref, table_a, table_b, table, third, eight, chunks, turned):
     blocks = gauss_ref.shape[1] // LANES
     rows = blocks // 2
+    height = 64
     for block in range(blocks):
-        splat = project_chunk(gauss_ref[:, block * LANES : (block + 1) * LANES])
-        ref = (table_a, table_b)[block // rows]
-        r = block % rows
-        ref[r * 8 : r * 8 + 8, :] = jnp.concatenate(splat[:8], axis=0)
-        ref[8 * rows + r : 8 * rows + r + 1, :] = splat[8]
+        piece = gauss_ref[:, block * LANES : (block + 1) * LANES]
+        chunks[block * height : block * height + gauss_ref.shape[0], :] = piece
+    for block in range(0, blocks, 8):
+        splat = project(lambda i: chunks[pl.ds(block * height + i, 8, stride=height), :])
+        for half, ref in enumerate((table_a, table_b)):
+            low, high = max(block, half * rows), min(block + 8, (half + 1) * rows)
+            if low < high:
+                r, part = low - half * rows, slice(low - block, high - block)
+                for p in range(8):
+                    ref[pl.ds(r * 8 + p, high - low, stride=8), :] = splat[p][part]
+                ref[8 * rows + r : 8 * rows + r + high - low, :] = splat[8][part]
+    for d in range(LANES):
+        turned[d : d + 1, 0:CAP] = pick_ref[:, d * CAP : (d + 1) * CAP]
+    turned[...] = jnp.transpose(turned[...])
     fill_table(table, third, (table_a, table_b))
 
     def eight_slots(i, carry):
         where = pl.multiple_of(i * 8, 8)
-        picks = pick_ref[pl.ds(where, 8), :]
+        picks = turned[pl.ds(where, 8), :]
         block = lax.shift_right_logical(picks, 7)
         codes = jnp.bitwise_and(picks, LANES - 1) + jnp.where(block < rows, block * 256, (block - rows) * 256 + LANES)
         found = [
@@ -211,7 +218,7 @@
 
 
 def deal(gaussians, picks):
-    devices = picks.shape[1]
+    devices = picks.shape[1] // CAP
     rows = gaussians.shape[1] // (2 * LANES)
     vmem = pl.BlockSpec(memory_space=VMEM)
     f32 = jnp.float32
@@ -228,6 +235,8 @@
             VMEM((SPLAT * rows, 512), jnp.bfloat16),
             VMEM((2 * rows, 256), jnp.bfloat16),
             VMEM((8 * LANES, LANES), f32),
+            VMEM((gaussians.shape[1] // LANES * 64, LANES), f32),
+            VMEM((LANES, LANES), jnp.int32),
         ],
         compiler_params=pltpu.CompilerParams(collective_id=2, has_side_effects=True, vmem_limit_bytes=16 << 20),
         name="deal_splats",
@@ -253,11 +262,12 @@
     return jnp.take_along_axis(value, index, axis=axis, mode="promise_in_bounds")
 
 
-def blend_kernel(cols_here, first, base, arrived, lists, ends, mono, out_ref,
+def blend_kernel(cols_here, first, base, arrived, lists, ends, mono, out_ref, again_ref,
                  table_a, table_b, table, third, packed, codes, params, coefs, power_a, power_b, state, total_ref,
-                 carry_ref, carry_owner, owner):
+                 carry_ref, carry_owner, owner, origin):
     tiles = first.shape[0] - 1
-    runs = lists.shape[0] // tiles
+    runs = lists.shape[2] // SEG
+    share = LANES // SEG
     groups = (first[tiles] + LANES - 1) // LANES
     per_group = SEG // BLOCK
 
@@ -269,13 +279,33 @@
                 ref[8 * ROWS :, :] = flat[CAP : CAP + ROWS]
     fill_table(table, third, (table_a, table_b))
 
+    upper = lax.broadcasted_iota(jnp.int32, (8, LANES), 0) < share
     packed[...] = jnp.full(packed.shape, -1, jnp.int32)
     for t in range(tiles):
-        packed[pl.ds(first[t], runs), :] = lists[t * runs : (t + 1) * runs, :]
+        line = lambda c: jnp.broadcast_to(
+            lists[t // cols_here, t % cols_here : t % cols_here + 1, c * LANES : (c + 1) * LANES], (8, LANES)
+        )
+        for c in range(0, runs // share, 2):
+            packed[pl.ds(first[t] + c * share, 8), :] = jnp.where(upper, line(c), line(c + 1))
+
+    ends_down = jnp.transpose(jnp.broadcast_to(ends[...], (LANES, LANES)))
+    along = lax.broadcasted_iota(jnp.int32, (LANES, LANES), 1)
+
+    def own(g, carry):
+        past = ends_down <= along + g * LANES
+        owner[pl.ds(g, 1), :] = jnp.sum(jnp.where(past, 1, 0), axis=0, keepdims=True)
+        origin[pl.ds(g, 1), :] = jnp.max(jnp.where(past, ends_down, 0), axis=0, keepdims=True)
+        return carry
+
+    lax.fori_loop(0, groups + 1, own, 0)
 
     def turn(g, carry):
         lanes = jnp.transpose(packed[pl.ds(pl.multiple_of(g * LANES, LANES), LANES), :])
+        place = lax.broadcasted_iota(jnp.int32, (1, LANES), 1) + g * LANES - origin[pl.ds(g, 1), :]
+        place = jnp.bitwise_and(place, share - 1)
         slot = lanes[0:SEG]
+        for c in range(1, share):
+            slot = jnp.where(place == c, lanes[c * SEG : (c + 1) * SEG], slot)
         source = ((slot.astype(jnp.float32) + 0.5) * (1.0 / CAP)).astype(jnp.int32)
         k = slot - source * CAP
         code = source + jnp.where(k < ROWS, k * 256, (k - ROWS) * 256 + LANES)
@@ -283,15 +313,6 @@
         return carry
 
     lax.fori_loop(0, groups, turn, 0)
-    ends_down = jnp.transpose(jnp.broadcast_to(ends[...], (LANES, LANES)))
-    along = lax.broadcasted_iota(jnp.int32, (LANES, LANES), 1)
-
-    def own(g, carry):
-        past = jnp.where(ends_down <= along + g * LANES, 1, 0)
-        owner[pl.ds(g, 1), :] = jnp.sum(past, axis=0, keepdims=True)
-        return carry
-
-    lax.fori_loop(0, groups + 1, own, 0)
     total_ref[...] = jnp.zeros_like(total_ref)
     carry_ref[...] = jnp.ones_like(carry_ref)
     carry_owner[...] = jnp.full(carry_owner.shape, -1, jnp.int32)
@@ -431,26 +452,27 @@
                 for h in range(2):
                     x = total_ref[ch, r * cols_here + q * 8 : r * cols_here + q * 8 + 8, h * LANES : (h + 1) * LANES]
                     x = lane_pick(lane_pick(lane_pick(x, skew, 1), down, 0), back, 1)
-                    out_ref[ch, r * TILE + h * 8 : r * TILE + h * 8 + 8, q * LANES : (q + 1) * LANES] = x
+                    for ref in (out_ref, again_ref):
+                        ref[ch, r * TILE + h * 8 : r * TILE + h * 8 + 8, q * LANES : (q + 1) * LANES] = x
 
 
 def blend_tiles(first, base, arrived, lists, ends, cols_here):
     tiles = first.shape[0] - 1
-    most = lists.shape[0] // LANES
+    most = tiles * (lists.shape[2] // SEG) // LANES
     smem = pl.BlockSpec(memory_space=pltpu.SMEM)
     vmem = pl.BlockSpec(memory_space=VMEM)
     f32 = jnp.float32
     return pl.pallas_call(
         functools.partial(blend_kernel, cols_here),
-        out_shape=jax.ShapeDtypeStruct((3, tiles // cols_here * TILE, cols_here * TILE), f32),
+        out_shape=(jax.ShapeDtypeStruct((3, tiles // cols_here * TILE, cols_here * TILE), f32),) * 2,
         in_specs=[smem] * 2 + [vmem] * 4,
-        out_specs=vmem,
+        out_specs=(vmem, vmem),
         scratch_shapes=[
             VMEM((9 * ROWS, LANES), f32),
             VMEM((9 * ROWS, LANES), f32),
             VMEM((9 * ROWS, 512), jnp.bfloat16),
             VMEM((2 * ROWS, 256), jnp.bfloat16),
-            VMEM((lists.shape[0] + LANES, LANES), jnp.int32),
+            VMEM(((most + 1) * LANES, LANES), jnp.int32),
             VMEM(((most + 1) * SEG, LANES), jnp.int32),
             VMEM((3 * 72, LANES), f32),
             VMEM((BLOCK * COEFS, LANES), f32),
@@ -461,6 +483,7 @@
             VMEM((PIXELS, LANES), f32),
             VMEM((8, LANES), jnp.int32),
             VMEM((most + 8, LANES), jnp.int32),
+            VMEM((most + 8, LANES), jnp.int32),
         ],
         compiler_params=pltpu.CompilerParams(vmem_limit_bytes=20 << 20),
         name="blend_tiles",
@@ -471,18 +494,15 @@
     rows_here, cols_here, list_len = tile_lists.shape
     tiles = rows_here * cols_here
     lists = tile_lists.reshape(tiles, list_len)
-    runs = list_len // SEG
     live = (jnp.sum((lists >= 0).astype(jnp.int32), axis=1) + SEG - 1) // SEG
     number = jnp.arange(tiles, dtype=jnp.int32)
     ends = jnp.sum(jnp.where(number[None, :] <= number[:, None], live[None, :], 0), axis=1).astype(jnp.int32)
     first = jnp.concatenate([jnp.zeros((1,), jnp.int32), ends])
-    most = tiles * runs
-    code = jnp.pad(lists.reshape(most, SEG), ((0, 0), (0, LANES - SEG)), constant_values=-1)
     half = TILE // 2
     base = jnp.stack(
         [lax.axis_index("gs") * (cols_here * TILE) + half, lax.axis_index("img") * (rows_here * TILE) + half]
     ).astype(jnp.int32)
-    return first, base, code, ends.reshape(1, tiles)
+    return first, base, ends.reshape(1, tiles)
 
 
 EDGE = 8
@@ -678,14 +698,13 @@
 
 def on_device(gaussians, send_slots, tile_lists, truth):
     rows_here, cols_here, list_len = tile_lists.shape
-    devices = send_slots.shape[1] // CAP
-    arrived = deal(gaussians, send_slots.reshape(devices, CAP).T)
-    first, base, code, ends = arrange(tile_lists)
-    rendered = blend_tiles(first, base, arrived, code, ends, cols_here)
-    rows, cols = exchange_halos(rendered, truth)
+    arrived = deal(gaussians, send_slots)
+    first, base, ends = arrange(tile_lists)
+    rendered, again = blend_tiles(first, base, arrived, tile_lists, ends, cols_here)
+    rows, cols = exchange_halos(again, truth)
     g, i = lax.axis_index("gs"), lax.axis_index("img")
     has = jnp.stack([g > 0, g < lax.axis_size("gs") - 1, i > 0, i < lax.axis_size("img") - 1]).astype(jnp.int32)
-    return (rendered, pixel_loss(has, rendered, truth, rows, cols))
+    return (rendered, pixel_loss(has, again, truth, rows, cols))
 
 
 def solution(mesh):

time: 71.9 us -> 68.1 us (0.947)
  local copies, waits for them, and re-layouts: 4.21 us -> 2.2 us
  other arithmetic: 2.26 us -> 1.52 us
    another operation x1 -> x0, local copies, waits for them, and re-layouts: 1.23 us -> none  [arrange(): lists.reshape(most, SEG)]
    unnamed x1 -> x0, other arithmetic: 0.74 us -> none
    unnamed x13 -> x10, local copies, waits for them, and re-layouts: 2.67 us -> 2.12 us
where the time goes in v8:
time: 68.1 us; the launch traced here: 67.9 us
  Pallas kernels  63.5 us (93%)
  local copies, waits for them, and re-layouts  2.2 us (3%)
  other arithmetic  1.52 us (2%)
  between operations  0.72 us (1%)
    pallas_call x1, Pallas kernels, blend_tiles(): pl.pallas_call(functools.partial(blend_kernel, cols_here), out_shape=(jax...  25.2 us
    pallas_call x1, Pallas kernels, deal(): pl.pallas_call(deal_kernel, out_shape=jax.ShapeDtypeStruct((devices * 8,...  20.1 us
    pallas_call x1, Pallas kernels, exchange_halos(): pl.pallas_call(halo_kernel, out_shape=(jax.ShapeDtypeStruct(rows, f32), j...  12.8 us
    pallas_call x1, Pallas kernels, pixel_loss(): pl.pallas_call(loss_kernel, out_shape=jax.ShapeDtypeStruct((height, width...  5.48 us
    unnamed x10, local copies, waits for them, and re-layouts  2.12 us

profile of v8, /device:TPU:0, one launch (start us, length us, event | category | flops | bytes accessed | tf_op | source)
XLA Modules:
  0.0 67.9 jit_solution(10122778109071553939)
XLA Ops:
  0.6 0.0 copy-start.3
  0.6 0.0 copy-start.2
  0.7 0.1 add_convert_fusion.has
  0.7 0.1 pad_add_fusion.1.base
  0.8 1.2 %convert_reduce_fusion = s32[8,16]{1,0:T(8,128)S(1)} fusion(s32[8,16,512]{2,1,0:T(8,128)} %lists.1), kind=kLoop, calls=%fused_computation | loop fusion | flops 196480 | bytes 262656 | tf_op jit(solution)/shard_map/reduce_sum | solution.py:497
  2.0 0.1 sub.18
  2.1 0.1 select_reduce_fusion
  2.2 0.1 pad_add_fusion.first
  2.3 0.0 copy-start.1
  2.3 1.3 %copy-done.1 = f32[59,5120]{1,0:T(8,128)S(1)} copy-done((f32[59,5120]{1,0:T(8,128)S(1)}, f32[59,5120]{1,0:T(8,128)}, u32[]{:S(2)}) %copy-start.1) | copy-done | bytes 1208344
  3.6 0.0 copy-start.4
  3.6 0.8 %copy-done.4 = s32[1,10240]{1,0:T(1,128)S(1)} copy-done((s32[1,10240]{1,0:T(1,128)S(1)}, s32[1,10240]{1,0:T(1,128)}, u32[]{:S(2)}) %copy-start.4) | copy-done | bytes 40984
  4.4 0.0 copy-start
  4.4 20.1 %deal_splats.1.arrived = f32[1024,128]{1,0:T(8,128)S(1)} custom-call(f32[59,5120]{1,0:T(8,128)S(1)} %copy-done.1, s32[1,10240]{1,0:T(1,128)S(1)} %copy-done.4), custom_call_target="tpu_custom_call" | custom-call | tf_op jit(solution)/shard_map/deal_splats/pallas_call | solution.py:225
  24.5 0.0 copy-done.3
  24.5 0.0 copy-done.2
  24.5 25.2 %blend_tiles.1 = (f32[3,128,256]{2,1,0:T(8,128)}, f32[3,128,256]{2,1,0:T(8,128)S(1)}) custom-call(s32[129]{0:T(256)S(1)} %pad_add_fusion.first, s32[2]{0:T(128)S(1)} %pad_add_fusion.1.base, f32[1024,128]{1,0:T(8,128)S(1)} %deal_splats.1.arrived, s32[8,16,512]{2,1,0:T(8,128)S(1)} %copy-done.2, s32[1,128]{1,0:T(1,128)S(1)} %bitcast.7, ...), custom_call_target="tpu_custom_call" | custom-call | tf_op jit(solution)/shard_map/blend_tiles/pallas_call | solution.py:465
  49.7 0.0 copy-done
  49.7 12.8 %exchange_halos.1 = (f32[2,6,2,8,128]{4,3,2,1,0:T(8,128)S(1)}, f32[6,6,8,128]{3,2,1,0:T(8,128)S(1)}) custom-call(f32[3,128,256]{2,1,0:T(8,128)S(1)} %get-tuple-element.7.rendered, f32[3,128,256]{2,1,0:T(8,128)S(1)} %copy-done), custom_call_target="tpu_custom_call" | custom-call | tf_op jit(solution)/shard_map/exchange_halos/pallas_call | solution.py:568
  62.5 5.5 %pixel_loss.1 = f32[128,256]{1,0:T(8,128)} custom-call(s32[4]{0:T(128)S(1)} %add_convert_fusion.has, f32[3,128,256]{2,1,0:T(8,128)S(1)} %get-tuple-element.7.rendered, f32[3,128,256]{2,1,0:T(8,128)S(1)} %copy-done, f32[2,6,2,8,128]{4,3,2,1,0:T(8,128)S(1)} %get-tuple-element.8.rows, f32[6,6,8,128]{3,2,1,0:T(8,128)S(1)} %get-tuple-element.9.cols), custom_call_target="tpu_custom_call" | custom-call | tf_op jit(solution)/shard_map/pixel_loss/pallas_call | solution.py:683
  (2 shorter events, 0.0 us)
Async XLA Ops:
  0.6 23.8 %copy-start.3 = (bf16[256,32]{1,0:T(8,128)(2,1)S(1)}, bf16[256,32]{1,0:T(8,128)(2,1)}, u32[]{:S(2)}) copy-start(bf16[256,32]{1,0:T(8,128)(2,1)} %constant.47.mono) | copy-start | bytes 49156
  0.6 23.8 %copy-start.2 = (s32[8,16,512]{2,1,0:T(8,128)S(1)}, s32[8,16,512]{2,1,0:T(8,128)}, u32[]{:S(2)}) copy-start(s32[8,16,512]{2,1,0:T(8,128)} %lists.1) | copy-start | bytes 786436
  2.3 1.3 %copy-start.1 = (f32[59,5120]{1,0:T(8,128)S(1)}, f32[59,5120]{1,0:T(8,128)}, u32[]{:S(2)}) copy-start(f32[59,5120]{1,0:T(8,128)} %gauss_ref.1) | copy-start | bytes 3624964
  3.6 0.8 %copy-start.4 = (s32[1,10240]{1,0:T(1,128)S(1)}, s32[1,10240]{1,0:T(1,128)}, u32[]{:S(2)}) copy-start(s32[1,10240]{1,0:T(1,128)} %pick_ref.1) | copy-start | bytes 122884
  4.4 45.3 %copy-start = (f32[3,128,256]{2,1,0:T(8,128)S(1)}, f32[3,128,256]{2,1,0:T(8,128)}, u32[]{:S(2)}) copy-start(f32[3,128,256]{2,1,0:T(8,128)} %truth.3) | copy-start | bytes 1179652

commit v9 on v8

--- a/solution.py
+++ b/solution.py
@@ -180,7 +180,7 @@
         out_ref[pl.ds(p, LANES, stride=8), :] = jnp.transpose(eight[pl.ds(p, LANES, stride=8), :])
 
 
-def deal_kernel(gauss_ref, pick_ref, in_ref, out_ref, send_sem, done_sem, local_sem, *scratch):
+def deal_kernel(gauss_hbm, pick_hbm, in_ref, gauss_ref, pick_ref, out_ref, send_sem, done_sem, local_sem, load_sem, *scratch):
     n_gs, n_img = lax.axis_size("gs"), lax.axis_size("img")
     devices = n_gs * n_img
     me = lax.axis_index("gs") * n_img + lax.axis_index("img")
@@ -205,7 +205,15 @@
         ).start()
         return carry
 
+    loads = [
+        pltpu.make_async_copy(gauss_hbm, gauss_ref, load_sem.at[0]),
+        pltpu.make_async_copy(pick_hbm, pick_ref, load_sem.at[1]),
+    ]
+    for load in loads:
+        load.start()
     lax.fori_loop(1, devices, greet, 0)
+    for load in loads:
+        load.wait()
     outgoing_kernel(gauss_ref, pick_ref, out_ref, *scratch)
     own = pltpu.make_async_copy(out_ref.at[block(me)], in_ref.at[block(me)], local_sem)
     own.start()
@@ -225,10 +233,11 @@
     return pl.pallas_call(
         deal_kernel,
         out_shape=jax.ShapeDtypeStruct((devices * 8, LANES), f32),
-        in_specs=[vmem] * 2,
+        in_specs=[pl.BlockSpec(memory_space=pltpu.HBM)] * 2,
         out_specs=vmem,
-        scratch_shapes=[VMEM((devices * 8, LANES), f32)]
+        scratch_shapes=[VMEM(gaussians.shape, f32), VMEM(picks.shape, jnp.int32), VMEM((devices * 8, LANES), f32)]
         + [pltpu.SemaphoreType.DMA] * 3
+        + [pltpu.SemaphoreType.DMA((2,))]
         + [
             VMEM((SPLAT * rows, LANES), f32),
             VMEM((SPLAT * rows, LANES), f32),
@@ -238,7 +247,7 @@
             VMEM((gaussians.shape[1] // LANES * 64, LANES), f32),
             VMEM((LANES, LANES), jnp.int32),
         ],
-        compiler_params=pltpu.CompilerParams(collective_id=2, has_side_effects=True, vmem_limit_bytes=16 << 20),
+        compiler_params=pltpu.CompilerParams(collective_id=2, has_side_effects=True, vmem_limit_bytes=211 << 18),
         name="deal_splats",
     )(gaussians, picks)
 

time: 68.1 us -> 68.2 us (level)
  Pallas kernels: 63.5 us -> 64.9 us
  local copies, waits for them, and re-layouts: 2.2 us -> 0.89 us
    pallas_call x1, Pallas kernels: 25.2 us -> 29.5 us  [blend_tiles(): pl.pallas_call(functools.partial(blend_kernel, cols_here), out_shape=(jax...]
    pallas_call x1, Pallas kernels: 12.8 us -> 9.61 us  [exchange_halos(): pl.pallas_call(halo_kernel, out_shape=(jax.ShapeDtypeStruct(rows, f32), j...]
    unnamed x10 -> x8, local copies, waits for them, and re-layouts: 2.12 us -> 0.81 us
where the time goes in v9:
time: 68.2 us; the launch traced here: 68 us
  Pallas kernels  64.9 us (95%)
  other arithmetic  1.52 us (2%)
  local copies, waits for them, and re-layouts  0.89 us (1%)
  between operations  0.71 us (1%)
    pallas_call x1, Pallas kernels, blend_tiles(): pl.pallas_call(functools.partial(blend_kernel, cols_here), out_shape=(jax...  29.5 us
    pallas_call x1, Pallas kernels, deal(): pl.pallas_call(deal_kernel, out_shape=jax.ShapeDtypeStruct((devices * 8,...  20.3 us
    pallas_call x1, Pallas kernels, exchange_halos(): pl.pallas_call(halo_kernel, out_shape=(jax.ShapeDtypeStruct(rows, f32), j...  9.61 us
    pallas_call x1, Pallas kernels, pixel_loss(): pl.pallas_call(loss_kernel, out_shape=jax.ShapeDtypeStruct((height, width...  5.48 us

profile of v9, /device:TPU:0, one launch (start us, length us, event | category | flops | bytes accessed | tf_op | source)
XLA Modules:
  0.0 68.0 jit_solution(12754906132490340882)
XLA Ops:
  0.6 0.0 copy-start.2
  0.6 0.0 copy-start.1
  0.7 0.1 add_convert_fusion.has
  0.7 0.1 pad_add_fusion.1.base
  0.8 1.2 %convert_reduce_fusion = s32[8,16]{1,0:T(8,128)S(1)} fusion(s32[8,16,512]{2,1,0:T(8,128)} %lists.1), kind=kLoop, calls=%fused_computation | loop fusion | flops 196480 | bytes 262656 | tf_op jit(solution)/shard_map/reduce_sum | solution.py:506
  2.0 0.1 sub.18
  2.1 0.1 select_reduce_fusion
  2.2 0.1 pad_add_fusion.first
  2.3 0.0 copy-start.3
  2.3 0.8 %copy-done.3 = s32[1,10240]{1,0:T(1,128)S(1)} copy-done((s32[1,10240]{1,0:T(1,128)S(1)}, s32[1,10240]{1,0:T(1,128)}, u32[]{:S(2)}) %copy-start.3) | copy-done | bytes 40984
  3.1 0.0 copy-start
  3.1 20.3 %deal_splats.1.arrived = f32[1024,128]{1,0:T(8,128)S(1)} custom-call(f32[59,5120]{1,0:T(8,128)} %gauss_hbm.1, s32[1,10240]{1,0:T(1,128)S(1)} %copy-done.3), custom_call_target="tpu_custom_call" | custom-call | tf_op jit(solution)/shard_map/deal_splats/pallas_call | solution.py:233
  23.4 0.0 copy-done.2
  23.4 0.0 copy-done.1
  23.4 29.5 %blend_tiles.1 = (f32[3,128,256]{2,1,0:T(8,128)}, f32[3,128,256]{2,1,0:T(8,128)S(1)}) custom-call(s32[129]{0:T(256)S(1)} %pad_add_fusion.first, s32[2]{0:T(128)S(1)} %pad_add_fusion.1.base, f32[1024,128]{1,0:T(8,128)S(1)} %deal_splats.1.arrived, s32[8,16,512]{2,1,0:T(8,128)S(1)} %copy-done.1, s32[1,128]{1,0:T(1,128)S(1)} %bitcast.7, ...), custom_call_target="tpu_custom_call" | custom-call | tf_op jit(solution)/shard_map/blend_tiles/pallas_call | solution.py:474
  52.9 0.0 copy-done
  52.9 9.6 %exchange_halos.1 = (f32[2,6,2,8,128]{4,3,2,1,0:T(8,128)S(1)}, f32[6,6,8,128]{3,2,1,0:T(8,128)S(1)}) custom-call(f32[3,128,256]{2,1,0:T(8,128)S(1)} %get-tuple-element.7.rendered, f32[3,128,256]{2,1,0:T(8,128)S(1)} %copy-done), custom_call_target="tpu_custom_call" | custom-call | tf_op jit(solution)/shard_map/exchange_halos/pallas_call | solution.py:577
  62.5 5.5 %pixel_loss.1 = f32[128,256]{1,0:T(8,128)} custom-call(s32[4]{0:T(128)S(1)} %add_convert_fusion.has, f32[3,128,256]{2,1,0:T(8,128)S(1)} %get-tuple-element.7.rendered, f32[3,128,256]{2,1,0:T(8,128)S(1)} %copy-done, f32[2,6,2,8,128]{4,3,2,1,0:T(8,128)S(1)} %get-tuple-element.8.rows, f32[6,6,8,128]{3,2,1,0:T(8,128)S(1)} %get-tuple-element.9.cols), custom_call_target="tpu_custom_call" | custom-call | tf_op jit(solution)/shard_map/pixel_loss/pallas_call | solution.py:692
  (2 shorter events, 0.0 us)
Async XLA Ops:
  0.6 22.7 %copy-start.2 = (bf16[256,32]{1,0:T(8,128)(2,1)S(1)}, bf16[256,32]{1,0:T(8,128)(2,1)}, u32[]{:S(2)}) copy-start(bf16[256,32]{1,0:T(8,128)(2,1)} %constant.47.mono) | copy-start | bytes 49156
  0.6 22.7 %copy-start.1 = (s32[8,16,512]{2,1,0:T(8,128)S(1)}, s32[8,16,512]{2,1,0:T(8,128)}, u32[]{:S(2)}) copy-start(s32[8,16,512]{2,1,0:T(8,128)} %lists.1) | copy-start | bytes 786436
  2.3 0.8 %copy-start.3 = (s32[1,10240]{1,0:T(1,128)S(1)}, s32[1,10240]{1,0:T(1,128)}, u32[]{:S(2)}) copy-start(s32[1,10240]{1,0:T(1,128)} %pick_hbm.1) | copy-start | bytes 122884
  3.1 49.8 %copy-start = (f32[3,128,256]{2,1,0:T(8,128)S(1)}, f32[3,128,256]{2,1,0:T(8,128)}, u32[]{:S(2)}) copy-start(f32[3,128,256]{2,1,0:T(8,128)} %truth.3) | copy-start | bytes 1179652

commit v10 on v9

--- a/solution.py
+++ b/solution.py
@@ -635,7 +635,7 @@
                 maps[at(9), :] = r * t
         return carry
 
-    lax.fori_loop(0, tall // 8, products, 0)
+    lax.fori_loop(0, tall // 8, products, 0, unroll=3)
     weights = window()
 
     def window_sum(ref, first):
@@ -652,7 +652,7 @@
                 summed[at, :] = window_sum(maps, start(q, part) + EDGE + n * 8)
         return carry
 
-    lax.fori_loop(0, height // 8, over_rows, 0)
+    lax.fori_loop(0, height // 8, over_rows, 0, unroll=2)
     wide = 2 * LANES + 2 * EDGE
     for q in range(12):
         blocks = [jnp.transpose(summed[(q * 3 + part) * height : (q * 3 + part + 1) * height, :]) for part in range(3)]
@@ -676,7 +676,7 @@
         likeness[pl.ds(pl.multiple_of(n * 8, 8), 8), :] = alike
         return carry
 
-    lax.fori_loop(0, 2 * LANES // 8, over_columns, 0)
+    lax.fori_loop(0, 2 * LANES // 8, over_columns, 0, unroll=4)
     for half in range(2):
         lanes = slice(half * LANES, (half + 1) * LANES)
         difference = jnp.abs(rendered[0, :, lanes] - truth[0, :, lanes])

time: 68.2 us -> 65.8 us (0.965)
  Pallas kernels: 64.9 us -> 62.8 us
    pallas_call x1, Pallas kernels: 29.5 us -> 25.2 us  [blend_tiles(): pl.pallas_call(functools.partial(blend_kernel, cols_here), out_shape=(jax...]
    pallas_call x1, Pallas kernels: 9.61 us -> 12.3 us  [exchange_halos(): pl.pallas_call(halo_kernel, out_shape=(jax.ShapeDtypeStruct(rows, f32), j...]
where the time goes in v10:
time: 65.8 us; the launch traced here: 65.9 us
  Pallas kernels  62.8 us (95%)
  other arithmetic  1.52 us (2%)
  local copies, waits for them, and re-layouts  0.89 us (1%)
  between operations  0.71 us (1%)
    pallas_call x1, Pallas kernels, blend_tiles(): pl.pallas_call(functools.partial(blend_kernel, cols_here), out_shape=(jax...  25.2 us
    pallas_call x1, Pallas kernels, deal(): pl.pallas_call(deal_kernel, out_shape=jax.ShapeDtypeStruct((devices * 8,...  20.3 us
    pallas_call x1, Pallas kernels, exchange_halos(): pl.pallas_call(halo_kernel, out_shape=(jax.ShapeDtypeStruct(rows, f32), j...  12.3 us
    pallas_call x1, Pallas kernels, pixel_loss(): pl.pallas_call(loss_kernel, out_shape=jax.ShapeDtypeStruct((height, width...  5.03 us

profile of v10, /device:TPU:0, one launch (start us, length us, event | category | flops | bytes accessed | tf_op | source)
XLA Modules:
  0.0 65.9 jit_solution(8550516229589178697)
XLA Ops:
  0.6 0.0 copy-start.2
  0.6 0.0 copy-start.1
  0.7 0.1 add_convert_fusion.has
  0.7 0.1 pad_add_fusion.1.base
  0.8 1.2 %convert_reduce_fusion = s32[8,16]{1,0:T(8,128)S(1)} fusion(s32[8,16,512]{2,1,0:T(8,128)} %lists.1), kind=kLoop, calls=%fused_computation | loop fusion | flops 196480 | bytes 262656 | tf_op jit(solution)/shard_map/reduce_sum | solution.py:506
  2.0 0.1 sub.18
  2.1 0.1 select_reduce_fusion
  2.2 0.1 pad_add_fusion.first
  2.3 0.0 copy-start.3
  2.3 0.8 %copy-done.3 = s32[1,10240]{1,0:T(1,128)S(1)} copy-done((s32[1,10240]{1,0:T(1,128)S(1)}, s32[1,10240]{1,0:T(1,128)}, u32[]{:S(2)}) %copy-start.3) | copy-done | bytes 40984
  3.1 0.0 copy-start
  3.1 20.3 %deal_splats.1.arrived = f32[1024,128]{1,0:T(8,128)S(1)} custom-call(f32[59,5120]{1,0:T(8,128)} %gauss_hbm.1, s32[1,10240]{1,0:T(1,128)S(1)} %copy-done.3), custom_call_target="tpu_custom_call" | custom-call | tf_op jit(solution)/shard_map/deal_splats/pallas_call | solution.py:233
  23.4 0.0 copy-done.2
  23.4 0.0 copy-done.1
  23.4 25.2 %blend_tiles.1 = (f32[3,128,256]{2,1,0:T(8,128)}, f32[3,128,256]{2,1,0:T(8,128)S(1)}) custom-call(s32[129]{0:T(256)S(1)} %pad_add_fusion.first, s32[2]{0:T(128)S(1)} %pad_add_fusion.1.base, f32[1024,128]{1,0:T(8,128)S(1)} %deal_splats.1.arrived, s32[8,16,512]{2,1,0:T(8,128)S(1)} %copy-done.1, s32[1,128]{1,0:T(1,128)S(1)} %bitcast.7, ...), custom_call_target="tpu_custom_call" | custom-call | tf_op jit(solution)/shard_map/blend_tiles/pallas_call | solution.py:474
  48.6 0.0 copy-done
  48.6 12.3 %exchange_halos.1 = (f32[2,6,2,8,128]{4,3,2,1,0:T(8,128)S(1)}, f32[6,6,8,128]{3,2,1,0:T(8,128)S(1)}) custom-call(f32[3,128,256]{2,1,0:T(8,128)S(1)} %get-tuple-element.7.rendered, f32[3,128,256]{2,1,0:T(8,128)S(1)} %copy-done), custom_call_target="tpu_custom_call" | custom-call | tf_op jit(solution)/shard_map/exchange_halos/pallas_call | solution.py:577
  60.8 5.0 %pixel_loss.1 = f32[128,256]{1,0:T(8,128)} custom-call(s32[4]{0:T(128)S(1)} %add_convert_fusion.has, f32[3,128,256]{2,1,0:T(8,128)S(1)} %get-tuple-element.7.rendered, f32[3,128,256]{2,1,0:T(8,128)S(1)} %copy-done, f32[2,6,2,8,128]{4,3,2,1,0:T(8,128)S(1)} %get-tuple-element.8.rows, f32[6,6,8,128]{3,2,1,0:T(8,128)S(1)} %get-tuple-element.9.cols), custom_call_target="tpu_custom_call" | custom-call | tf_op jit(solution)/shard_map/pixel_loss/pallas_call | solution.py:692
  (2 shorter events, 0.0 us)
Async XLA Ops:
  0.6 22.7 %copy-start.2 = (bf16[256,32]{1,0:T(8,128)(2,1)S(1)}, bf16[256,32]{1,0:T(8,128)(2,1)}, u32[]{:S(2)}) copy-start(bf16[256,32]{1,0:T(8,128)(2,1)} %constant.47.mono) | copy-start | bytes 49156
  0.6 22.7 %copy-start.1 = (s32[8,16,512]{2,1,0:T(8,128)S(1)}, s32[8,16,512]{2,1,0:T(8,128)}, u32[]{:S(2)}) copy-start(s32[8,16,512]{2,1,0:T(8,128)} %lists.1) | copy-start | bytes 786436
  2.3 0.8 %copy-start.3 = (s32[1,10240]{1,0:T(1,128)S(1)}, s32[1,10240]{1,0:T(1,128)}, u32[]{:S(2)}) copy-start(s32[1,10240]{1,0:T(1,128)} %pick_hbm.1) | copy-start | bytes 122884
  3.1 45.5 %copy-start = (f32[3,128,256]{2,1,0:T(8,128)S(1)}, f32[3,128,256]{2,1,0:T(8,128)}, u32[]{:S(2)}) copy-start(f32[3,128,256]{2,1,0:T(8,128)} %truth.3) | copy-start | bytes 1179652
